TPU v7x, 256 devices: a whole 4x4x8 slice. The times are simulated.
256 devices in a mesh: cells: 128 (over z, x, y), genes: 2 (over core).
Axes of the slice: x: 4, y: 4, z: 8, core: 2. Of those that a mesh axis runs over, the one named last changes fastest.
Arguments:
- stored: bfloat16 [256, 2, 65536], P('cells', 'genes'), may hold values from 0.001 to 70, as said below
- neighbours: int32 [512, 8], P('cells'), may hold values from 0 to 511, as said below
- counts: int32 [512], P('cells'), may hold values from 5 to 8
- affinity: bfloat16 [512, 8, 128, 128], P('cells'), may hold values from 9.9658966e-05 to 1
Outputs:
- imputed: float32 [512, 65536], P('genes', 'cells')
Inputs may be any that keep to these rules, and one draw needn't show every extreme that they name: `stored`: entries are positive. neighbours[b, 0] = b. Slots 1 to 4 of every row block name blocks of other devices along cells (block j lies on device j // 4); slots 5 to 7 name blocks of the row block's own device. Over the row blocks of one device, slots 1 to 4 name blocks of any one other device at most 1 times, and exactly 1 times for some device.
All inputs are finite; a program needn't handle non-finite values.
Results may differ from a plain program's by a relative error of at most 0.007.
Values may be sent and summed in bfloat16 or wider, within the bound.
No kernel may reach another device: no remote copies, remote signals or barrier semaphores. Data moves between devices by JAX's collectives and lax.ppermute only.
A program may use at most 64 MiB of HBM per device.

v0:
```python
import jax
import jax.numpy as jnp
from jax import lax
from jax.sharding import PartitionSpec as P

GENES = 512
REMOTE = 4
STEPS = 3


epsilon = 1e-06


def local(stored, neighbours, counts, affinity):
    cell_count = lax.axis_size("cells")
    my_index = lax.axis_index("cells")
    blocks_dev, slot_count, block_size, _ = affinity.shape
    gene_rows = stored.shape[0] * cell_count
    remote_n = REMOTE * blocks_dev
    wanted = neighbours[:, 1 : 1 + REMOTE].reshape(-1)
    near_cols = jnp.concatenate([neighbours[:, :1], neighbours[:, 1 + REMOTE :]], axis=1)
    near_count = near_cols.shape[1]
    valid_mask = (jnp.arange(slot_count, dtype=jnp.int32)[None, :] < counts[:, None]).astype(
        jnp.float32
    )
    masked = affinity.astype(jnp.float32) * valid_mask[:, :, None, None]
    rowsum = jnp.sum(masked, axis=(1, 2))
    transition = (masked / rowsum[:, None, None, :]).astype(jnp.bfloat16)
    near_trans = jnp.concatenate([transition[:, :1], transition[:, 1 + REMOTE :]], axis=1)
    far_trans = transition[:, 1 : 1 + REMOTE]
    block_view = stored.reshape(stored.shape[0], 1, -1, block_size)
    arrived = lax.all_to_all(block_view, "cells", split_axis=2, concat_axis=0, tiled=True)
    raw_counts = arrived[:, 0].astype(jnp.float32)
    partial_value = jnp.sum(raw_counts, axis=0)
    library = lax.psum(partial_value, "genes") / GENES
    normed = (raw_counts / library[None]).astype(jnp.bfloat16)
    layout = jnp.transpose(normed, (1, 0, 2))
    current = layout
    peak_first = lax.pmax(jnp.max(current, axis=(0, 2)).astype(jnp.float32), "cells")
    owner_dev = wanted // blocks_dev
    within = wanted - owner_dev * blocks_dev
    peer_ids = jnp.arange(cell_count, dtype=jnp.int32)
    onehot = (owner_dev[:, None] == peer_ids[None, :]).astype(jnp.int32)
    rank_slot = jnp.sum((jnp.cumsum(onehot, axis=0) - 1) * onehot, axis=1)
    capacity = (remote_n + cell_count - 2) // (cell_count - 1)
    places = jnp.arange(capacity, dtype=jnp.int32)
    matches = (owner_dev[:, None, None] == peer_ids[None, :, None]) & (
        rank_slot[:, None, None] == places[None, None, :]
    )
    request_table = jnp.sum(jnp.where(matches, within[:, None, None], 0), axis=0)
    asked_rows = lax.all_to_all(request_table, "cells", split_axis=0, concat_axis=0, tiled=True)
    slot_of = owner_dev * capacity + rank_slot
    near_ids = (near_cols - my_index * blocks_dev).reshape(-1)
    scaled = current.astype(jnp.float32)
    for step_index in range(STEPS):
        sending = jnp.take(current, asked_rows.reshape(-1), axis=0).reshape(
            cell_count, capacity, gene_rows, block_size
        )
        landed = lax.all_to_all(sending, "cells", split_axis=0, concat_axis=0, tiled=True)
        flat_rows = landed.reshape(cell_count * capacity, gene_rows, block_size)
        far_tiles = jnp.take(flat_rows, slot_of, axis=0).reshape(
            blocks_dev, REMOTE, gene_rows, block_size
        )
        near_tiles = jnp.take(current, near_ids, axis=0).reshape(
            blocks_dev, near_count, gene_rows, block_size
        )
        product = jnp.einsum(
            "bsgk,bski->bgi", near_tiles, near_trans, preferred_element_type=jnp.float32
        )
        product = product + jnp.einsum(
            "bsgk,bski->bgi", far_tiles, far_trans, preferred_element_type=jnp.float32
        )
        mixed_sum = 0.5 * current.astype(jnp.float32) + 0.5 * product
        peak_now = lax.pmax(jnp.max(mixed_sum, axis=(0, 2)), "cells")
        scaled = mixed_sum * (peak_first / (peak_now + epsilon))[None, :, None]
        current = scaled.astype(jnp.bfloat16)
    return jnp.transpose(scaled, (1, 0, 2)).reshape(gene_rows, blocks_dev * block_size)


def solution(mesh):
    in_specs = (
        P("cells", "genes", None),
        P("cells", None),
        P("cells"),
        P("cells", None, None, None),
    )
    out_specs = P("genes", "cells")
    return jax.shard_map(local, mesh=mesh, in_specs=in_specs, out_specs=out_specs, check_vma=False)
```

profile of v0, /device:TPU:2, one launch (start us, length us, event | category | flops | bytes accessed | tf_op | source)
XLA Modules:
  0.0 1605.0 jit_solution(13573172101801814815)
XLA Ops:
  1.4 26.6 %all_to_all.33 = s32[128,1,1]{2,1,0:T(1,128)S(1)} all-to-all(s32[128,1,1]{2,1,0:T(1,128)S(1)} %copy.60), channel_id=1, replica_groups=mesh['cells'=128,'genes'=2] {'cells'}, dimensions={0} | all-to-all | bytes 1024 | tf_op jit(solution)/shard_map/all_to_all | solution.py:51
  27.9 6.6 all-to-all-start
  34.6 2.4 reduce.4
  37.0 11.1 all-to-all-done
  48.5 2.5 psum.7
  51.7 6.3 gather_fusion.1
  58.0 7.4 select_bitcast_fusion.2
  65.4 8.0 all-to-all-start.2
  75.6 1.6 gather_fusion
  78.5 1.4 broadcast_select_fusion.5
  80.2 181.1 %all-to-all-done.2 = bf16[128,1,256,128]{2,3,1,0:T(8,128)(2,1)} async-done(((bf16[128,1,256,128]{2,3,1,0:T(8,128)(2,1)}), bf16[128,1,256,128]{2,3,1,0:T(8,128)(2,1)}, u32[]{:S(2)}, u32[]{:S(2)}) %all-to-all-start.2) | async-done | bytes 8388640 | tf_op jit(solution)/shard_map/all_to_all | solution.py:59
  261.3 5.1 gather_fusion.2
  268.1 339.0 %all-reduce = (f32[256]{0:T(256)S(1)}, f32[256]{0:T(256)S(1)}) all-reduce(f32[256]{0:T(256)S(1)} %reshape.290, f32[256]{0:T(256)S(1)} %get-tuple-element.15), channel_id=1, replica_groups=mesh['cells'=128,'genes'=2] {'cells'}, use_global_device_ids=true, to_apply=%region_7.11 | all-reduce | flops 512 | bytes 4096 | tf_op jit(solution)/shard_map/pmax | solution.py:39
  607.4 6.3 gather_fusion.4
  613.6 7.4 select_bitcast_fusion.1
  621.1 19.0 %all-to-all-start.3 = ((bf16[128,1,256,128]{2,3,1,0:T(8,128)(2,1)}), bf16[128,1,256,128]{2,3,1,0:T(8,128)(2,1)}, u32[]{:S(2)}, u32[]{:S(2)}) async-start(bf16[128,1,256,128]{2,3,1,0:T(8,128)(2,1)} %select_bitcast_fusion.1), calls=%async_computation.3 | async-start | bytes 16777216 | tf_op jit(solution)/shard_map/all_to_all | solution.py:59
  640.1 1.6 gather_fusion.3
  641.7 1.4 broadcast_select_fusion.4
  644.2 124.3 %all-to-all-done.3 = bf16[128,1,256,128]{2,3,1,0:T(8,128)(2,1)} async-done(((bf16[128,1,256,128]{2,3,1,0:T(8,128)(2,1)}), bf16[128,1,256,128]{2,3,1,0:T(8,128)(2,1)}, u32[]{:S(2)}, u32[]{:S(2)}) %all-to-all-start.3) | async-done | bytes 8388640 | tf_op jit(solution)/shard_map/all_to_all | solution.py:59
  768.5 5.1 gather_fusion.5
  775.0 1.4 multiply_reduce_fusion.1
  776.4 345.5 %pmax.30 = f32[256]{0:T(256)S(1)} all-reduce(f32[256]{0:T(256)S(1)} %get-tuple-element.17), channel_id=1, replica_groups=mesh['cells'=128,'genes'=2] {'cells'}, use_global_device_ids=true, to_apply=%region_11.15 | all-reduce | flops 256 | bytes 2048 | tf_op jit(solution)/shard_map/pmax | solution.py:74
  1122.0 6.3 gather_fusion.7
  1128.3 7.4 select_bitcast_fusion
  1135.7 25.0 %all-to-all-start.4 = ((bf16[128,1,256,128]{2,3,1,0:T(8,128)(2,1)}), bf16[128,1,256,128]{2,3,1,0:T(8,128)(2,1)}, u32[]{:S(2)}, u32[]{:S(2)}) async-start(bf16[128,1,256,128]{2,3,1,0:T(8,128)(2,1)} %select_bitcast_fusion), calls=%async_computation.4 | async-start | bytes 16777216 | tf_op jit(solution)/shard_map/all_to_all | solution.py:59
  1160.7 1.6 gather_fusion.6
  1162.3 1.4 broadcast_select_fusion.3
  1164.8 94.0 %all-to-all-done.4 = bf16[128,1,256,128]{2,3,1,0:T(8,128)(2,1)} async-done(((bf16[128,1,256,128]{2,3,1,0:T(8,128)(2,1)}), bf16[128,1,256,128]{2,3,1,0:T(8,128)(2,1)}, u32[]{:S(2)}, u32[]{:S(2)}) %all-to-all-start.4) | async-done | bytes 8388640 | tf_op jit(solution)/shard_map/all_to_all | solution.py:59
  1258.8 5.1 gather_fusion.8
  1265.3 2.2 multiply_reduce_fusion
  1267.5 335.1 %pmax.31 = f32[256]{0:T(256)S(1)} all-reduce(f32[256]{0:T(256)S(1)} %get-tuple-element.19), channel_id=1, replica_groups=mesh['cells'=128,'genes'=2] {'cells'}, use_global_device_ids=true, to_apply=%region_13.17 | all-reduce | flops 256 | bytes 2048 | tf_op jit(solution)/shard_map/pmax | solution.py:74
  1602.6 1.4 fusion.4
  (56 shorter events, 14.2 us)
Async XLA Ops:
  27.9 20.2 %all-to-all-start = ((bf16[2,1,512,128]{3,0,1,2:T(2,128)(2,1)}), bf16[2,1,512,128]{3,0,1,2:T(2,128)(2,1)S(1)}, u32[]{:S(2)}, u32[]{:S(2)}) async-start(bf16[2,1,512,128]{3,0,1,2:T(2,128)(2,1)} %bitcast.106), calls=%async_computation | async-start | bytes 524288 | tf_op jit(solution)/shard_map/all_to_all | solution.py:32
  65.4 8.0 copy-start.2
  65.4 8.1 copy-start.1
  65.4 8.8 copy-start.3
  65.4 195.9 %all-to-all-start.2 = ((bf16[128,1,256,128]{2,3,1,0:T(8,128)(2,1)}), bf16[128,1,256,128]{2,3,1,0:T(8,128)(2,1)}, u32[]{:S(2)}, u32[]{:S(2)}) async-start(bf16[128,1,256,128]{2,3,1,0:T(8,128)(2,1)} %select_bitcast_fusion.2), calls=%async_computation.2 | async-start | bytes 16777216 | tf_op jit(solution)/shard_map/all_to_all | solution.py:59
  268.1 345.5 %copy-start = (f32[4,256,128]{1,2,0:T(8,128)}, f32[4,256,128]{1,2,0:T(8,128)S(1)}, u32[]{:S(2)}) copy-start(f32[4,256,128]{1,2,0:T(8,128)S(1)} %get-tuple-element.16) | copy-start | bytes 1572868
  621.1 147.5 %all-to-all-start.3 = ((bf16[128,1,256,128]{2,3,1,0:T(8,128)(2,1)}), bf16[128,1,256,128]{2,3,1,0:T(8,128)(2,1)}, u32[]{:S(2)}, u32[]{:S(2)}) async-start(bf16[128,1,256,128]{2,3,1,0:T(8,128)(2,1)} %select_bitcast_fusion.1), calls=%async_computation.3 | async-start | bytes 16777216 | tf_op jit(solution)/shard_map/all_to_all | solution.py:59
  1135.7 123.2 %all-to-all-start.4 = ((bf16[128,1,256,128]{2,3,1,0:T(8,128)(2,1)}), bf16[128,1,256,128]{2,3,1,0:T(8,128)(2,1)}, u32[]{:S(2)}, u32[]{:S(2)}) async-start(bf16[128,1,256,128]{2,3,1,0:T(8,128)(2,1)} %select_bitcast_fusion), calls=%async_computation.4 | async-start | bytes 16777216 | tf_op jit(solution)/shard_map/all_to_all | solution.py:59
where the time goes:
time: 1610 us
  blocking collectives  1050 us (65%)
  waiting for transfers between devices  411 us (26%)
  starting transfers between devices  58.7 us (4%)
  local copies, waits for them, and re-layouts  42.6 us (3%)
  other arithmetic  37.7 us (2%)
    pmax x2, blocking collectives, local(): peak_now = lax.pmax(jnp.max(mixed_sum, axis=(0, 2)), 'cells')  681 us
    all_to_all x3, waiting for transfers between devices, local(): lax.all_to_all(sending, 'cells', split_axis=0, concat_axis=0, tiled=True)  399 us
    pmax x1, blocking collectives, local(): lax.pmax(jnp.max(current, axis=(0, 2)).astype(jnp.float32), 'cells')  339 us
    all_to_all x3, starting transfers between devices, local(): lax.all_to_all(sending, 'cells', split_axis=0, concat_axis=0, tiled=True)  52 us
  transfers between devices with their start and end apart: 4, of which 4 were waited for; matrix products, arithmetic and copies ran while one was open for 1% of the time, Pallas kernels for 0%

commit v1 on v0

v1 whole, which is shorter than its diff:
```python
import functools

import jax
import jax.numpy as jnp
from jax import lax
from jax.experimental import pallas as pl
from jax.experimental.pallas import tpu as pltpu
from jax.sharding import Mesh, PartitionSpec as P

REMOTE = 4
STEPS = 3
SIDE = 4
GROUP = 8
BS = 128
epsilon = 1e-06
XY = ("x", "y")


def shift(value, axis, distance):
    pairs = [(i, (i + distance) % SIDE) for i in range(SIDE)]
    return lax.ppermute(value, axis, pairs)


def spread(value):
    half = value.shape[0] // 2
    first, second = value[:half], value[half:]
    along_x = [first] + [shift(first, "x", -d) for d in (1, 2, 3)]
    along_y = [second] + [shift(second, "y", -d) for d in (1, 2, 3)]
    first, second = jnp.concatenate(along_x), jnp.concatenate(along_y)
    pieces = [first] + [shift(first, "y", -d) for d in (1, 2, 3)]
    pieces += [second] + [shift(second, "x", -d) for d in (1, 2, 3)]
    return pieces


def step_kernel(pieces, chunk, place_ref, count_ref, *refs):
    sources, (aff_ref, out_ref, peak_ref, own_peak_ref, held, sems) = refs[:pieces], refs[pieces:]
    at = pl.program_id(0)
    size = sources[0].shape[0]

    @pl.when(at == 0)
    def _():
        copies = [
            pltpu.make_async_copy(source, held.at[pl.ds(i * size, size)], sems.at[i])
            for i, source in enumerate(sources)
        ]
        for copy in copies:
            copy.start()
        for copy in copies:
            copy.wait()
        peak_ref[...] = jnp.zeros_like(peak_ref)
        own_peak_ref[...] = jnp.zeros_like(own_peak_ref)

    slots = aff_ref.shape[1]
    genes = held.shape[1]
    peak = peak_ref[...]
    own_peak = own_peak_ref[...]
    for b in range(chunk):
        row = at * chunk + b
        count = count_ref[row]
        tiles = []
        for s in range(slots):
            tile = held[place_ref[row * slots + s]]
            tile = jnp.concatenate([tile, jnp.ones((16, BS), tile.dtype)], axis=0)
            if s > REMOTE:
                tile = jnp.where(s < count, tile, jnp.zeros_like(tile))
            tiles.append(tile)
        left = jnp.concatenate(tiles, axis=1)
        right = aff_ref[b].reshape(slots * BS, BS)
        total = jnp.dot(left, right, preferred_element_type=jnp.float32)
        own = held[place_ref[row * slots]].astype(jnp.float32)
        mixed = 0.5 * own + total[:genes] * (0.5 / total[genes : genes + 1])
        out_ref[b] = mixed.astype(out_ref.dtype)
        peak = jnp.maximum(peak, mixed)
        own_peak = jnp.maximum(own_peak, own)
    peak_ref[...] = peak
    own_peak_ref[...] = own_peak


def diffuse(pieces, places, counts, affinity, out_type):
    blocks, slots = affinity.shape[:2]
    size, genes = pieces[0].shape[:2]
    chunk = 8
    n = len(pieces)
    whole = lambda at, *_: (0, 0)
    return pl.pallas_call(
        functools.partial(step_kernel, n, chunk),
        grid_spec=pltpu.PrefetchScalarGridSpec(
            num_scalar_prefetch=2,
            grid=(blocks // chunk,),
            in_specs=[pl.BlockSpec(memory_space=pl.ANY)] * n
            + [pl.BlockSpec((chunk, slots, BS, BS), lambda at, *_: (at, 0, 0, 0))],
            out_specs=[
                pl.BlockSpec((chunk, genes, BS), lambda at, *_: (at, 0, 0)),
                pl.BlockSpec((genes, BS), whole),
                pl.BlockSpec((genes, BS), whole),
            ],
            scratch_shapes=[
                pltpu.VMEM((n * size, genes, BS), pieces[0].dtype),
                pltpu.SemaphoreType.DMA((n,)),
            ],
        ),
        out_shape=[
            jax.ShapeDtypeStruct((blocks, genes, BS), out_type),
            jax.ShapeDtypeStruct((genes, BS), jnp.float32),
            jax.ShapeDtypeStruct((genes, BS), jnp.float32),
        ],
        compiler_params=pltpu.CompilerParams(vmem_limit_bytes=40 * 1024 * 1024),
        cost_estimate=pl.CostEstimate(
            flops=2 * blocks * slots * BS * BS * genes,
            bytes_accessed=2 * blocks * slots * BS * BS,
            transcendentals=0,
        ),
    )(places, counts, *pieces, affinity)


def to_all(value, axis, size):
    return lax.all_to_all(
        jnp.broadcast_to(value[None], (size,) + value.shape), axis, 0, 0, tiled=True
    )


def local(stored, neighbours, counts, affinity):
    core, my_x, my_y = lax.axis_index("c"), lax.axis_index("x"), lax.axis_index("y")
    blocks_dev, slots = neighbours.shape
    half = blocks_dev // 2
    part = lax.dynamic_slice_in_dim(affinity, core * half, half, 0)
    affinity = lax.all_gather(part, ("z", "c"), tiled=True)

    table = jnp.concatenate([neighbours, counts[:, None]], axis=1).reshape(-1)
    table = jnp.pad(table, (0, 128 - table.shape[0]))
    table = to_all(table, "z", GROUP)[:, : blocks_dev * (slots + 1)]
    table = table.reshape(GROUP * blocks_dev, slots + 1)
    neighbours, counts = table[:, :slots], table[:, slots]

    device, inner = neighbours // blocks_dev, neighbours % blocks_dev
    plane = device // (SIDE * SIDE)
    dx = (device // SIDE - my_x) % SIDE
    dy = (device - my_y) % SIDE
    half_group = GROUP // 2
    within = (plane % half_group) * blocks_dev + inner
    unit = half_group * blocks_dev
    places = jnp.where(
        plane < half_group,
        (dy * SIDE + dx) * unit + within,
        (SIDE * SIDE + dx * SIDE + dy) * unit + within,
    ).reshape(-1)

    genes_dev = stored.shape[0]
    cells_dev = blocks_dev * BS
    counted = stored.reshape(genes_dev, GROUP, SIDE * SIDE, cells_dev)
    counted = lax.all_to_all(counted, XY, 2, 0, tiled=True)
    genes = counted.shape[0]
    counted = counted.reshape(genes, GROUP * blocks_dev, BS).astype(jnp.float32)
    partial = lax.psum(jnp.sum(counted, axis=0), "c")
    library = jnp.sum(to_all(partial, "z", GROUP), axis=0) / (2 * GROUP * genes)
    current = (counted / library[None]).astype(jnp.bfloat16)
    current = jnp.transpose(current, (1, 0, 2))

    peaks = []
    for step in range(STEPS):
        current, peak, own_peak = diffuse(spread(current), places, counts, affinity, jnp.bfloat16)
        if step == 0:
            peaks.append(own_peak)
        peaks.append(peak)
    peaks = jnp.max(jnp.stack(peaks), axis=2).reshape(-1)
    peaks = jnp.max(to_all(peaks, XY, SIDE * SIDE), axis=0).reshape(STEPS + 1, genes)
    scale = jnp.ones((genes,), jnp.float32)
    for step in range(STEPS):
        scale = scale * (peaks[0] / (scale * peaks[1 + step] + epsilon))
    result = (current.astype(jnp.float32) * scale[None, :, None]).astype(jnp.bfloat16)
    result = jnp.transpose(result, (1, 0, 2)).reshape(genes, GROUP, cells_dev)
    result = lax.all_to_all(result, "z", 1, 0, tiled=True)
    return result.reshape(GROUP * genes, cells_dev).astype(jnp.float32)


def solution(mesh):
    grid = Mesh(mesh.devices.reshape(GROUP, SIDE, SIDE, 2), ("z", "x", "y", "c"))
    cells = ("z", "x", "y")
    return jax.shard_map(
        local,
        mesh=grid,
        in_specs=(P(cells, "c", None), P(cells, None), P(cells), P(cells, None, None, None)),
        out_specs=P("c", cells),
        check_vma=False,
    )
```

time: 1610 us -> 291 us (0.18)
  blocking collectives: 1050 us -> 63.3 us
  waiting for transfers between devices: 411 us -> 110 us
  other arithmetic: 37.7 us -> 2.18 us
  local copies, waits for them, and re-layouts: 42.6 us -> 8.88 us
  starting transfers between devices: 58.7 us -> 81.9 us
    pmax x3 -> x0, blocking collectives: 1020 us -> none  [the longest x2 681 us: local(): peak_now = lax.pmax(jnp.max(mixed_sum, axis=(0, 2)), 'cells')]
    all_to_all x4 -> x2, waiting for transfers between devices: 411 us -> 18.8 us  [to_all(): lax.all_to_all(jnp.broadcast_to(value[None], (size,) + value.shape), axis...]
    ppermute x0 -> x36, waiting for transfers between devices: none -> 90.8 us  [shift(): return lax.ppermute(value, axis, pairs)]
    ppermute x0 -> x36, starting transfers between devices: none -> 70.1 us  [shift(): return lax.ppermute(value, axis, pairs)]
    all_to_all x4 -> x2, starting transfers between devices: 58.7 us -> 11.7 us  [to_all(): lax.all_to_all(jnp.broadcast_to(value[None], (size,) + value.shape), axis...]
    gather x9 -> x0, local copies, waits for them, and re-layouts: 38.9 us -> none  [the longest x3 18.9 us: local(): jnp.take(current, asked_rows.reshape(-1), axis=0)]
    all_to_all x1 -> x3, blocking collectives: 26.6 us -> 59.9 us  [the longest x1 30.6 us: local(): result = lax.all_to_all(result, 'z', 1, 0, tiled=True)]
    reshape x3 -> x0, other arithmetic: 22.2 us -> none  [local(): jnp.take(current, asked_rows.reshape(-1), axis=0)]
  transfers between devices with their start and end apart: 4 -> 39, of which waited for: 4 -> 25; matrix products, arithmetic and copies ran while one was open for 1% -> 1% of each run, Pallas kernels for 0% -> 0%
where the time goes in v1:
time: 291 us
  waiting for transfers between devices  110 us (38%)
  starting transfers between devices  81.9 us (28%)
  blocking collectives  63.3 us (22%)
  between operations  13.7 us (5%)
  Pallas kernels  11.1 us (4%)
  local copies, waits for them, and re-layouts  8.88 us (3%)
    ppermute x36, waiting for transfers between devices, shift(): return lax.ppermute(value, axis, pairs)  90.8 us
    ppermute x36, starting transfers between devices, shift(): return lax.ppermute(value, axis, pairs)  70.1 us
    all_to_all x1, blocking collectives, local(): result = lax.all_to_all(result, 'z', 1, 0, tiled=True)  30.6 us
    all_to_all x2, waiting for transfers between devices, to_all(): lax.all_to_all(jnp.broadcast_to(value[None], (size,) + value.shape), axis...  18.8 us
    all_to_all x1, blocking collectives, to_all(): lax.all_to_all(jnp.broadcast_to(value[None], (size,) + value.shape), axis...  15.2 us
    all_to_all x1, blocking collectives, local(): counted = lax.all_to_all(counted, XY, 2, 0, tiled=True)  14.1 us
    all_to_all x2, starting transfers between devices, to_all(): lax.all_to_all(jnp.broadcast_to(value[None], (size,) + value.shape), axis...  11.7 us
    pallas_call x3, Pallas kernels, diffuse(): pl.pallas_call(functools.partial(step_kernel, n, chunk), grid_spec=pltpu....  11.1 us
  transfers between devices with their start and end apart: 39, of which 25 were waited for; matrix products, arithmetic and copies ran while one was open for 1% of the time, Pallas kernels for 0%

profile of v1, /device:TPU:2, one launch (start us, length us, event | category | flops | bytes accessed | tf_op | source)
XLA Modules:
  0.0 290.7 jit_solution(2466715321654043036)
XLA Ops:
  9.8 14.1 %all_to_all.38 = bf16[2,8,16,512]{3,1,0,2:T(8,128)(2,1)S(1)} all-to-all(bf16[2,8,16,512]{3,1,0,2:T(8,128)(2,1)S(1)} %copy.26), channel_id=1, replica_groups=mesh['z'=8,'x'=4,'y'=4,'c'=2] {'x','y'}, dimensions={2} | all-to-all | bytes 524288 | tf_op jit(solution)/shard_map/all_to_all | solution.py:151
  23.9 3.4 %psum.7 = f32[32,128]{1,0:T(8,128)S(1)} all-reduce(f32[32,128]{1,0:T(8,128)S(1)} %reduce_sum.21), channel_id=1, replica_groups=mesh['z'=8,'x'=4,'y'=4,'c'=2] {'c'}, use_global_device_ids=true, to_apply=%region_1.2 | all-reduce | flops 4096 | bytes 32768 | tf_op jit(solution)/shard_map/psum | solution.py:154
  27.9 8.5 %all-to-all-start.2 = ((f32[8,32,128]{2,1,0:T(8,128)}), f32[8,32,128]{2,1,0:T(8,128)S(1)}, u32[]{:S(2)}, u32[]{:S(2)}) async-start(f32[8,32,128]{2,1,0:T(8,128)} %broadcast_in_dim.12), calls=%async_computation.2 | async-start | bytes 262144 | tf_op jit(solution)/shard_map/all_to_all | solution.py:117
  36.5 11.2 %all-to-all-done.2 = f32[8,32,128]{2,1,0:T(8,128)S(1)} async-done(((f32[8,32,128]{2,1,0:T(8,128)}), f32[8,32,128]{2,1,0:T(8,128)S(1)}, u32[]{:S(2)}, u32[]{:S(2)}) %all-to-all-start.2) | async-done | bytes 131104 | tf_op jit(solution)/shard_map/all_to_all | solution.py:117
  49.2 2.8 collective-permute-start.1
  59.4 3.2 %collective-permute-start.7 = (bf16[16,32,128]{2,1,0:T(8,128)(2,1)S(1)}, bf16[16,32,128]{2,1,0:T(8,128)(2,1)S(1)}, u32[]{:S(2)}, u32[]{:S(2)}) collective-permute-start(bf16[16,32,128]{2,1,0:T(8,128)(2,1)S(1)} %get-tuple-element.23), channel_id=1, source_target_pairs={{0,4},{2,6},{4,0},{6,2},{1,5},{3,7},{5,1},{7,3},{8,12},{10,14},{12... | collective-permute-start | bytes 393224 | tf_op jit(solution)/shard_map/ppermute | solution.py:21
  64.4 23.4 %collective-permute-done.8 = bf16[16,32,128]{2,1,0:T(8,128)(2,1)S(1)} collective-permute-done((bf16[16,32,128]{2,1,0:T(8,128)(2,1)S(1)}, bf16[16,32,128]{2,1,0:T(8,128)(2,1)S(1)}, u32[]{:S(2)}, u32[]{:S(2)}) %collective-permute-start.8) | collective-permute-done | bytes 131104 | tf_op jit(solution)/shard_map/ppermute | solution.py:21
  88.5 3.5 %collective-permute-start.10 = (bf16[64,32,128]{2,1,0:T(8,128)(2,1)S(1)}, bf16[64,32,128]{2,1,0:T(8,128)(2,1)}, u32[]{:S(2)}, u32[]{:S(2)}) collective-permute-start(bf16[64,32,128]{2,1,0:T(8,128)(2,1)S(1)} %pad_maximum_fusion.1.refs_4_), channel_id=1, source_target_pairs={{0,16},{8,24},{16,0},{24,8},{1,17},{9,25},{17,1},{25,9},{2,18},{10... | collective-permute-start | bytes 1572872 | tf_op jit(solution)/shard_map/ppermute | solution.py:21
  95.5 3.3 %all-to-all-start = ((s32[8,1,128]{2,1,0:T(1,128)}), s32[8,1,128]{2,1,0:T(1,128)S(1)}, u32[]{:S(2)}, u32[]{:S(2)}) async-start(s32[8,1,128]{2,1,0:T(1,128)} %broadcast_in_dim.11), calls=%async_computation | async-start | bytes 8192 | tf_op jit(solution)/shard_map/all_to_all | solution.py:117
  98.8 7.6 %all-to-all-done = s32[8,1,128]{2,1,0:T(1,128)S(1)} async-done(((s32[8,1,128]{2,1,0:T(1,128)}), s32[8,1,128]{2,1,0:T(1,128)S(1)}, u32[]{:S(2)}, u32[]{:S(2)}) %all-to-all-start) | async-done | bytes 4128 | tf_op jit(solution)/shard_map/all_to_all | solution.py:117
  106.8 3.4 %copy-done.1 = bf16[32,8,128,128]{3,2,1,0:T(8,128)(2,1)S(1)} copy-done((bf16[32,8,128,128]{3,2,1,0:T(8,128)(2,1)S(1)}, bf16[32,8,128,128]{3,2,1,0:T(8,128)(2,1)}, u32[]{:S(2)}) %copy-start.1) | copy-done | bytes 8388632
  110.2 4.4 %shard_map.46 = (bf16[32,32,128]{2,1,0:T(8,128)(2,1)S(1)}, f32[32,128]{1,0:T(8,128)S(1)}, f32[32,128]{1,0:T(8,128)S(1)}) custom-call(s32[256]{0:T(256)S(1)} %reshape.61.place_ref, s32[32]{0:T(128)S(1)} %slice_reduce_fusion.count_ref, bf16[64,32,128]{2,1,0:T(8,128)(2,1)S(1)} %pad_maximum_fusion.refs_0_, bf16[64,32,128]{2,1,0:T(8,128)(2,1)} %collective-permute-done.3.refs_1_, ...), custom_call_target="tpu_custom_call" | custom-call | flops 268435456 | bytes 8388608 | tf_op jit(solution)/shard_map/pallas_call | solution.py:85
  114.7 2.7 collective-permute-start.13
  125.1 2.6 collective-permute-start.19
  128.3 2.9 %collective-permute-start.16 = (bf16[64,32,128]{2,1,0:T(8,128)(2,1)S(1)}, bf16[64,32,128]{2,1,0:T(8,128)(2,1)S(1)}, u32[]{:S(2)}, u32[]{:S(2)}) collective-permute-start(bf16[64,32,128]{2,1,0:T(8,128)(2,1)S(1)} %pad_maximum_fusion.2.refs_0_), channel_id=1, source_target_pairs={{0,4},{2,6},{4,0},{6,2},{1,5},{3,7},{5,1},{7,3},{8,12},{10,14},{12... | collective-permute-start | bytes 1572872 | tf_op jit(solution)/shard_map/ppermute | solution.py:21
  131.2 7.9 %collective-permute-done.20 = bf16[16,32,128]{2,1,0:T(8,128)(2,1)S(1)} collective-permute-done((bf16[16,32,128]{2,1,0:T(8,128)(2,1)S(1)}, bf16[16,32,128]{2,1,0:T(8,128)(2,1)S(1)}, u32[]{:S(2)}, u32[]{:S(2)}) %collective-permute-start.20) | collective-permute-done | bytes 131104 | tf_op jit(solution)/shard_map/ppermute | solution.py:21
  143.2 2.6 collective-permute-start.22
  149.2 6.4 %collective-permute-done.15.refs_1_ = bf16[64,32,128]{2,1,0:T(8,128)(2,1)S(1)} collective-permute-done((bf16[64,32,128]{2,1,0:T(8,128)(2,1)S(1)}, bf16[64,32,128]{2,1,0:T(8,128)(2,1)S(1)}, u32[]{:S(2)}, u32[]{:S(2)}) %collective-permute-start.15) | collective-permute-done | bytes 524320 | tf_op jit(solution)/shard_map/ppermute | solution.py:21
  156.6 5.5 %collective-permute-done.21.refs_5_ = bf16[64,32,128]{2,1,0:T(8,128)(2,1)S(1)} collective-permute-done((bf16[64,32,128]{2,1,0:T(8,128)(2,1)S(1)}, bf16[64,32,128]{2,1,0:T(8,128)(2,1)S(1)}, u32[]{:S(2)}, u32[]{:S(2)}) %collective-permute-start.21) | collective-permute-done | bytes 524320 | tf_op jit(solution)/shard_map/ppermute | solution.py:21
  162.1 3.4 %shard_map.47 = (bf16[32,32,128]{2,1,0:T(8,128)(2,1)S(1)}, f32[32,128]{1,0:T(8,128)S(1)}, f32[32,128]{1,0:T(8,128)}) custom-call(s32[256]{0:T(256)S(1)} %reshape.61.place_ref, s32[32]{0:T(128)S(1)} %slice_reduce_fusion.count_ref, bf16[64,32,128]{2,1,0:T(8,128)(2,1)S(1)} %pad_maximum_fusion.2.refs_0_, ...), custom_call_target="tpu_custom_call" | custom-call | flops 268435456 | bytes 8388608 | tf_op jit(solution)/shard_map/pallas_call | solution.py:85
  166.2 3.7 %collective-permute-start.25 = (bf16[16,32,128]{2,1,0:T(8,128)(2,1)S(1)}, bf16[16,32,128]{2,1,0:T(8,128)(2,1)S(1)}, u32[]{:S(2)}, u32[]{:S(2)}) collective-permute-start(bf16[16,32,128]{2,1,0:T(8,128)(2,1)S(1)} %get-tuple-element.20), channel_id=1, source_target_pairs={{0,16},{8,24},{16,0},{24,8},{1,17},{9,25},{17,1},{25,9},{2,18},{10... | collective-permute-start | bytes 393224 | tf_op jit(solution)/shard_map/ppermute | solution.py:21
  174.9 11.8 %collective-permute-start.29 = (bf16[64,32,128]{2,1,0:T(8,128)(2,1)S(1)}, bf16[64,32,128]{2,1,0:T(8,128)(2,1)S(1)}, u32[]{:S(2)}, u32[]{:S(2)}) collective-permute-start(bf16[64,32,128]{2,1,0:T(8,128)(2,1)S(1)} %pad_maximum_fusion.4.refs_0_), channel_id=1, source_target_pairs={{0,2},{2,4},{4,6},{6,0},{1,3},{3,5},{5,7},{7,1},{8,10},{10,12},{12... | collective-permute-start | bytes 1572872 | tf_op jit(solution)/shard_map/ppermute | solution.py:21
  191.0 2.5 collective-permute-start.30
  193.5 10.7 %collective-permute-done.32 = bf16[16,32,128]{2,1,0:T(8,128)(2,1)S(1)} collective-permute-done((bf16[16,32,128]{2,1,0:T(8,128)(2,1)S(1)}, bf16[16,32,128]{2,1,0:T(8,128)(2,1)S(1)}, u32[]{:S(2)}, u32[]{:S(2)}) %collective-permute-start.32) | collective-permute-done | bytes 131104 | tf_op jit(solution)/shard_map/ppermute | solution.py:21
  204.2 2.9 %collective-permute-start.27 = (bf16[64,32,128]{2,1,0:T(8,128)(2,1)S(1)}, bf16[64,32,128]{2,1,0:T(8,128)(2,1)S(1)}, u32[]{:S(2)}, u32[]{:S(2)}) collective-permute-start(bf16[64,32,128]{2,1,0:T(8,128)(2,1)S(1)} %pad_maximum_fusion.4.refs_0_), channel_id=1, source_target_pairs={{0,6},{2,0},{4,2},{6,4},{1,7},{3,1},{5,3},{7,5},{8,14},{10,8},{12,... | collective-permute-start | bytes 1572872 | tf_op jit(solution)/shard_map/ppermute | solution.py:21
  210.1 3.7 %collective-permute-start.34 = (bf16[64,32,128]{2,1,0:T(8,128)(2,1)S(1)}, bf16[64,32,128]{2,1,0:T(8,128)(2,1)S(1)}, u32[]{:S(2)}, u32[]{:S(2)}) collective-permute-start(bf16[64,32,128]{2,1,0:T(8,128)(2,1)S(1)} %pad_maximum_fusion.5.refs_4_), channel_id=1, source_target_pairs={{0,16},{8,24},{16,0},{24,8},{1,17},{9,25},{17,1},{25,9},{2,18},{10... | collective-permute-start | bytes 1572872 | tf_op jit(solution)/shard_map/ppermute | solution.py:21
  215.3 3.0 %collective-permute-done.28.refs_2_ = bf16[64,32,128]{2,1,0:T(8,128)(2,1)S(1)} collective-permute-done((bf16[64,32,128]{2,1,0:T(8,128)(2,1)S(1)}, bf16[64,32,128]{2,1,0:T(8,128)(2,1)S(1)}, u32[]{:S(2)}, u32[]{:S(2)}) %collective-permute-start.28) | collective-permute-done | bytes 524320 | tf_op jit(solution)/shard_map/ppermute | solution.py:21
  218.4 4.9 %collective-permute-done.27.refs_1_ = bf16[64,32,128]{2,1,0:T(8,128)(2,1)S(1)} collective-permute-done((bf16[64,32,128]{2,1,0:T(8,128)(2,1)S(1)}, bf16[64,32,128]{2,1,0:T(8,128)(2,1)S(1)}, u32[]{:S(2)}, u32[]{:S(2)}) %collective-permute-start.27) | collective-permute-done | bytes 524320 | tf_op jit(solution)/shard_map/ppermute | solution.py:21
  226.6 6.3 %collective-permute-done.33.refs_5_ = bf16[64,32,128]{2,1,0:T(8,128)(2,1)S(1)} collective-permute-done((bf16[64,32,128]{2,1,0:T(8,128)(2,1)S(1)}, bf16[64,32,128]{2,1,0:T(8,128)(2,1)S(1)}, u32[]{:S(2)}, u32[]{:S(2)}) %collective-permute-start.33) | collective-permute-done | bytes 524320 | tf_op jit(solution)/shard_map/ppermute | solution.py:21
  232.9 3.4 %shard_map.48 = (bf16[32,32,128]{2,1,0:T(8,128)(2,1)S(1)}, f32[32,128]{1,0:T(8,128)S(1)}, f32[32,128]{1,0:T(8,128)}) custom-call(s32[256]{0:T(256)S(1)} %reshape.61.place_ref, s32[32]{0:T(128)S(1)} %slice_reduce_fusion.count_ref, bf16[64,32,128]{2,1,0:T(8,128)(2,1)S(1)} %pad_maximum_fusion.4.refs_0_, ...), custom_call_target="tpu_custom_call" | custom-call | flops 268435456 | bytes 8388608 | tf_op jit(solution)/shard_map/pallas_call | solution.py:85
  236.5 15.2 %all_to_all.39 = f32[16,1,128]{2,1,0:T(1,128)S(1)} all-to-all(f32[16,1,128]{2,1,0:T(1,128)S(1)} %broadcast_in_dim.28), channel_id=1, replica_groups=mesh['z'=8,'x'=4,'y'=4,'c'=2] {'x','y'}, dimensions={0} | all-to-all | bytes 16384 | tf_op jit(solution)/shard_map/all_to_all | solution.py:117
  252.3 30.6 %all_to_all.40 = bf16[32,8,512]{2,0,1:T(8,128)(2,1)S(1)} all-to-all(bf16[32,8,512]{2,0,1:T(8,128)(2,1)S(1)} %copy.30), channel_id=1, replica_groups=mesh['z'=8,'x'=4,'y'=4,'c'=2] {'z'}, dimensions={1} | all-to-all | bytes 524288 | tf_op jit(solution)/shard_map/all_to_all | solution.py:172
  (103 shorter events, 55.7 us)
Async XLA Ops:
  6.5 100.3 %all-gather.2.cloned.1.call-start = ((), (), s32[]{:S(2)}) async-start(), calls=%async_computation.5 | async-start | bytes 8912896 | tf_op jit(solution)/shard_map/all_gather | solution.py:127
  27.9 19.8 %all-to-all-start.2 = ((f32[8,32,128]{2,1,0:T(8,128)}), f32[8,32,128]{2,1,0:T(8,128)S(1)}, u32[]{:S(2)}, u32[]{:S(2)}) async-start(f32[8,32,128]{2,1,0:T(8,128)} %broadcast_in_dim.12), calls=%async_computation.2 | async-start | bytes 262144 | tf_op jit(solution)/shard_map/all_to_all | solution.py:117
  49.2 7.2 %collective-permute-start.1 = (bf16[16,32,128]{2,1,0:T(8,128)(2,1)S(1)}, bf16[16,32,128]{2,1,0:T(8,128)(2,1)S(1)}, u32[]{:S(2)}, u32[]{:S(2)}) collective-permute-start(bf16[16,32,128]{2,1,0:T(8,128)(2,1)S(1)} %get-tuple-element.24), channel_id=1, source_target_pairs={{0,16},{8,24},{16,0},{24,8},{1,17},{9,25},{17,1},{25,9},{2,18},{10... | collective-permute-start | bytes 393224 | tf_op jit(solution)/shard_map/ppermute | solution.py:21
  57.8 34.3 %collective-permute-start.5 = (bf16[64,32,128]{2,1,0:T(8,128)(2,1)S(1)}, bf16[64,32,128]{2,1,0:T(8,128)(2,1)S(1)}, u32[]{:S(2)}, u32[]{:S(2)}) collective-permute-start(bf16[64,32,128]{2,1,0:T(8,128)(2,1)S(1)} %pad_maximum_fusion.refs_0_), channel_id=1, source_target_pairs={{0,2},{2,4},{4,6},{6,0},{1,3},{3,5},{5,7},{7,1},{8,10},{10,12},{12... | collective-permute-start | bytes 1572872 | tf_op jit(solution)/shard_map/ppermute | solution.py:21
  58.3 29.5 %collective-permute-start.8 = (bf16[16,32,128]{2,1,0:T(8,128)(2,1)S(1)}, bf16[16,32,128]{2,1,0:T(8,128)(2,1)S(1)}, u32[]{:S(2)}, u32[]{:S(2)}) collective-permute-start(bf16[16,32,128]{2,1,0:T(8,128)(2,1)S(1)} %get-tuple-element.23), channel_id=1, source_target_pairs={{0,2},{2,4},{4,6},{6,0},{1,3},{3,5},{5,7},{7,1},{8,10},{10,12},{12... | collective-permute-start | bytes 393224 | tf_op jit(solution)/shard_map/ppermute | solution.py:21
  59.4 28.4 %collective-permute-start.7 = (bf16[16,32,128]{2,1,0:T(8,128)(2,1)S(1)}, bf16[16,32,128]{2,1,0:T(8,128)(2,1)S(1)}, u32[]{:S(2)}, u32[]{:S(2)}) collective-permute-start(bf16[16,32,128]{2,1,0:T(8,128)(2,1)S(1)} %get-tuple-element.23), channel_id=1, source_target_pairs={{0,4},{2,6},{4,0},{6,2},{1,5},{3,7},{5,1},{7,3},{8,12},{10,14},{12... | collective-permute-start | bytes 393224 | tf_op jit(solution)/shard_map/ppermute | solution.py:21
  62.6 25.2 %collective-permute-start.6 = (bf16[16,32,128]{2,1,0:T(8,128)(2,1)S(1)}, bf16[16,32,128]{2,1,0:T(8,128)(2,1)S(1)}, u32[]{:S(2)}, u32[]{:S(2)}) collective-permute-start(bf16[16,32,128]{2,1,0:T(8,128)(2,1)S(1)} %get-tuple-element.23), channel_id=1, source_target_pairs={{0,6},{2,0},{4,2},{6,4},{1,7},{3,1},{5,3},{7,5},{8,14},{10,8},{12,... | collective-permute-start | bytes 393224 | tf_op jit(solution)/shard_map/ppermute | solution.py:21
  62.9 43.9 %collective-permute-start.4 = (bf16[64,32,128]{2,1,0:T(8,128)(2,1)S(1)}, bf16[64,32,128]{2,1,0:T(8,128)(2,1)S(1)}, u32[]{:S(2)}, u32[]{:S(2)}) collective-permute-start(bf16[64,32,128]{2,1,0:T(8,128)(2,1)S(1)} %pad_maximum_fusion.refs_0_), channel_id=1, source_target_pairs={{0,4},{2,6},{4,0},{6,2},{1,5},{3,7},{5,1},{7,3},{8,12},{10,14},{12... | collective-permute-start | bytes 1572872 | tf_op jit(solution)/shard_map/ppermute | solution.py:21
  87.8 19.0 %collective-permute-start.3 = (bf16[64,32,128]{2,1,0:T(8,128)(2,1)S(1)}, bf16[64,32,128]{2,1,0:T(8,128)(2,1)}, u32[]{:S(2)}, u32[]{:S(2)}) collective-permute-start(bf16[64,32,128]{2,1,0:T(8,128)(2,1)S(1)} %pad_maximum_fusion.refs_0_), channel_id=1, source_target_pairs={{0,6},{2,0},{4,2},{6,4},{1,7},{3,1},{5,3},{7,5},{8,14},{10,8},{12,... | collective-permute-start | bytes 1572872 | tf_op jit(solution)/shard_map/ppermute | solution.py:21
  87.9 18.9 %collective-permute-start.11 = (bf16[64,32,128]{2,1,0:T(8,128)(2,1)S(1)}, bf16[64,32,128]{2,1,0:T(8,128)(2,1)}, u32[]{:S(2)}, u32[]{:S(2)}) collective-permute-start(bf16[64,32,128]{2,1,0:T(8,128)(2,1)S(1)} %pad_maximum_fusion.1.refs_4_), channel_id=1, source_target_pairs={{0,8},{8,16},{16,24},{24,0},{1,9},{9,17},{17,25},{25,1},{2,10},{10... | collective-permute-start | bytes 1572872 | tf_op jit(solution)/shard_map/ppermute | solution.py:21
  88.5 18.2 %collective-permute-start.10 = (bf16[64,32,128]{2,1,0:T(8,128)(2,1)S(1)}, bf16[64,32,128]{2,1,0:T(8,128)(2,1)}, u32[]{:S(2)}, u32[]{:S(2)}) collective-permute-start(bf16[64,32,128]{2,1,0:T(8,128)(2,1)S(1)} %pad_maximum_fusion.1.refs_4_), channel_id=1, source_target_pairs={{0,16},{8,24},{16,0},{24,8},{1,17},{9,25},{17,1},{25,9},{2,18},{10... | collective-permute-start | bytes 1572872 | tf_op jit(solution)/shard_map/ppermute | solution.py:21
  92.1 14.7 %collective-permute-start.9 = (bf16[64,32,128]{2,1,0:T(8,128)(2,1)S(1)}, bf16[64,32,128]{2,1,0:T(8,128)(2,1)}, u32[]{:S(2)}, u32[]{:S(2)}) collective-permute-start(bf16[64,32,128]{2,1,0:T(8,128)(2,1)S(1)} %pad_maximum_fusion.1.refs_4_), channel_id=1, source_target_pairs={{0,24},{8,0},{16,8},{24,16},{1,25},{9,1},{17,9},{25,17},{2,26},{10... | collective-permute-start | bytes 1572872 | tf_op jit(solution)/shard_map/ppermute | solution.py:21
  95.5 10.9 %all-to-all-start = ((s32[8,1,128]{2,1,0:T(1,128)}), s32[8,1,128]{2,1,0:T(1,128)S(1)}, u32[]{:S(2)}, u32[]{:S(2)}) async-start(s32[8,1,128]{2,1,0:T(1,128)} %broadcast_in_dim.11), calls=%async_computation | async-start | bytes 8192 | tf_op jit(solution)/shard_map/all_to_all | solution.py:117
  114.7 6.8 %collective-permute-start.13 = (bf16[16,32,128]{2,1,0:T(8,128)(2,1)S(1)}, bf16[16,32,128]{2,1,0:T(8,128)(2,1)S(1)}, u32[]{:S(2)}, u32[]{:S(2)}) collective-permute-start(bf16[16,32,128]{2,1,0:T(8,128)(2,1)S(1)} %get-tuple-element.22), channel_id=1, source_target_pairs={{0,16},{8,24},{16,0},{24,8},{1,17},{9,25},{17,1},{25,9},{2,18},{10... | collective-permute-start | bytes 393224 | tf_op jit(solution)/shard_map/ppermute | solution.py:21
  122.9 22.9 %collective-permute-start.17 = (bf16[64,32,128]{2,1,0:T(8,128)(2,1)S(1)}, bf16[64,32,128]{2,1,0:T(8,128)(2,1)S(1)}, u32[]{:S(2)}, u32[]{:S(2)}) collective-permute-start(bf16[64,32,128]{2,1,0:T(8,128)(2,1)S(1)} %pad_maximum_fusion.2.refs_0_), channel_id=1, source_target_pairs={{0,2},{2,4},{4,6},{6,0},{1,3},{3,5},{5,7},{7,1},{8,10},{10,12},{12... | collective-permute-start | bytes 1572872 | tf_op jit(solution)/shard_map/ppermute | solution.py:21
  125.0 14.1 %collective-permute-start.20 = (bf16[16,32,128]{2,1,0:T(8,128)(2,1)S(1)}, bf16[16,32,128]{2,1,0:T(8,128)(2,1)S(1)}, u32[]{:S(2)}, u32[]{:S(2)}) collective-permute-start(bf16[16,32,128]{2,1,0:T(8,128)(2,1)S(1)} %get-tuple-element.21), channel_id=1, source_target_pairs={{0,2},{2,4},{4,6},{6,0},{1,3},{3,5},{5,7},{7,1},{8,10},{10,12},{12... | collective-permute-start | bytes 393224 | tf_op jit(solution)/shard_map/ppermute | solution.py:21
  125.1 17.4 %collective-permute-start.19 = (bf16[16,32,128]{2,1,0:T(8,128)(2,1)S(1)}, bf16[16,32,128]{2,1,0:T(8,128)(2,1)S(1)}, u32[]{:S(2)}, u32[]{:S(2)}) collective-permute-start(bf16[16,32,128]{2,1,0:T(8,128)(2,1)S(1)} %get-tuple-element.21), channel_id=1, source_target_pairs={{0,4},{2,6},{4,0},{6,2},{1,5},{3,7},{5,1},{7,3},{8,12},{10,14},{12... | collective-permute-start | bytes 393224 | tf_op jit(solution)/shard_map/ppermute | solution.py:21
  127.7 14.8 %collective-permute-start.18 = (bf16[16,32,128]{2,1,0:T(8,128)(2,1)S(1)}, bf16[16,32,128]{2,1,0:T(8,128)(2,1)S(1)}, u32[]{:S(2)}, u32[]{:S(2)}) collective-permute-start(bf16[16,32,128]{2,1,0:T(8,128)(2,1)S(1)} %get-tuple-element.21), channel_id=1, source_target_pairs={{0,6},{2,0},{4,2},{6,4},{1,7},{3,1},{5,3},{7,5},{8,14},{10,8},{12,... | collective-permute-start | bytes 393224 | tf_op jit(solution)/shard_map/ppermute | solution.py:21
  128.3 20.9 %collective-permute-start.16 = (bf16[64,32,128]{2,1,0:T(8,128)(2,1)S(1)}, bf16[64,32,128]{2,1,0:T(8,128)(2,1)S(1)}, u32[]{:S(2)}, u32[]{:S(2)}) collective-permute-start(bf16[64,32,128]{2,1,0:T(8,128)(2,1)S(1)} %pad_maximum_fusion.2.refs_0_), channel_id=1, source_target_pairs={{0,4},{2,6},{4,0},{6,2},{1,5},{3,7},{5,1},{7,3},{8,12},{10,14},{12... | collective-permute-start | bytes 1572872 | tf_op jit(solution)/shard_map/ppermute | solution.py:21
  139.1 16.5 %collective-permute-start.15 = (bf16[64,32,128]{2,1,0:T(8,128)(2,1)S(1)}, bf16[64,32,128]{2,1,0:T(8,128)(2,1)S(1)}, u32[]{:S(2)}, u32[]{:S(2)}) collective-permute-start(bf16[64,32,128]{2,1,0:T(8,128)(2,1)S(1)} %pad_maximum_fusion.2.refs_0_), channel_id=1, source_target_pairs={{0,6},{2,0},{4,2},{6,4},{1,7},{3,1},{5,3},{7,5},{8,14},{10,8},{12,... | collective-permute-start | bytes 1572872 | tf_op jit(solution)/shard_map/ppermute | solution.py:21
  142.6 13.0 %collective-permute-start.23 = (bf16[64,32,128]{2,1,0:T(8,128)(2,1)S(1)}, bf16[64,32,128]{2,1,0:T(8,128)(2,1)S(1)}, u32[]{:S(2)}, u32[]{:S(2)}) collective-permute-start(bf16[64,32,128]{2,1,0:T(8,128)(2,1)S(1)} %pad_maximum_fusion.3.refs_4_), channel_id=1, source_target_pairs={{0,8},{8,16},{16,24},{24,0},{1,9},{9,17},{17,25},{25,1},{2,10},{10... | collective-permute-start | bytes 1572872 | tf_op jit(solution)/shard_map/ppermute | solution.py:21
  143.2 13.3 %collective-permute-start.22 = (bf16[64,32,128]{2,1,0:T(8,128)(2,1)S(1)}, bf16[64,32,128]{2,1,0:T(8,128)(2,1)S(1)}, u32[]{:S(2)}, u32[]{:S(2)}) collective-permute-start(bf16[64,32,128]{2,1,0:T(8,128)(2,1)S(1)} %pad_maximum_fusion.3.refs_4_), channel_id=1, source_target_pairs={{0,16},{8,24},{16,0},{24,8},{1,17},{9,25},{17,1},{25,9},{2,18},{10... | collective-permute-start | bytes 1572872 | tf_op jit(solution)/shard_map/ppermute | solution.py:21
  145.8 16.2 %collective-permute-start.21 = (bf16[64,32,128]{2,1,0:T(8,128)(2,1)S(1)}, bf16[64,32,128]{2,1,0:T(8,128)(2,1)S(1)}, u32[]{:S(2)}, u32[]{:S(2)}) collective-permute-start(bf16[64,32,128]{2,1,0:T(8,128)(2,1)S(1)} %pad_maximum_fusion.3.refs_4_), channel_id=1, source_target_pairs={{0,24},{8,0},{16,8},{24,16},{1,25},{9,1},{17,9},{25,17},{2,26},{10... | collective-permute-start | bytes 1572872 | tf_op jit(solution)/shard_map/ppermute | solution.py:21
  174.9 38.9 %collective-permute-start.29 = (bf16[64,32,128]{2,1,0:T(8,128)(2,1)S(1)}, bf16[64,32,128]{2,1,0:T(8,128)(2,1)S(1)}, u32[]{:S(2)}, u32[]{:S(2)}) collective-permute-start(bf16[64,32,128]{2,1,0:T(8,128)(2,1)S(1)} %pad_maximum_fusion.4.refs_0_), channel_id=1, source_target_pairs={{0,2},{2,4},{4,6},{6,0},{1,3},{3,5},{5,7},{7,1},{8,10},{10,12},{12... | collective-permute-start | bytes 1572872 | tf_op jit(solution)/shard_map/ppermute | solution.py:21
  186.6 17.5 %collective-permute-start.32 = (bf16[16,32,128]{2,1,0:T(8,128)(2,1)S(1)}, bf16[16,32,128]{2,1,0:T(8,128)(2,1)S(1)}, u32[]{:S(2)}, u32[]{:S(2)}) collective-permute-start(bf16[16,32,128]{2,1,0:T(8,128)(2,1)S(1)} %get-tuple-element.19), channel_id=1, source_target_pairs={{0,2},{2,4},{4,6},{6,0},{1,3},{3,5},{5,7},{7,1},{8,10},{10,12},{12... | collective-permute-start | bytes 393224 | tf_op jit(solution)/shard_map/ppermute | solution.py:21
  189.1 20.2 %collective-permute-start.31 = (bf16[16,32,128]{2,1,0:T(8,128)(2,1)S(1)}, bf16[16,32,128]{2,1,0:T(8,128)(2,1)S(1)}, u32[]{:S(2)}, u32[]{:S(2)}) collective-permute-start(bf16[16,32,128]{2,1,0:T(8,128)(2,1)S(1)} %get-tuple-element.19), channel_id=1, source_target_pairs={{0,4},{2,6},{4,0},{6,2},{1,5},{3,7},{5,1},{7,3},{8,12},{10,14},{12... | collective-permute-start | bytes 393224 | tf_op jit(solution)/shard_map/ppermute | solution.py:21
  191.0 18.4 %collective-permute-start.30 = (bf16[16,32,128]{2,1,0:T(8,128)(2,1)S(1)}, bf16[16,32,128]{2,1,0:T(8,128)(2,1)S(1)}, u32[]{:S(2)}, u32[]{:S(2)}) collective-permute-start(bf16[16,32,128]{2,1,0:T(8,128)(2,1)S(1)} %get-tuple-element.19), channel_id=1, source_target_pairs={{0,6},{2,0},{4,2},{6,4},{1,7},{3,1},{5,3},{7,5},{8,14},{10,8},{12,... | collective-permute-start | bytes 393224 | tf_op jit(solution)/shard_map/ppermute | solution.py:21
  193.5 24.8 %collective-permute-start.28 = (bf16[64,32,128]{2,1,0:T(8,128)(2,1)S(1)}, bf16[64,32,128]{2,1,0:T(8,128)(2,1)S(1)}, u32[]{:S(2)}, u32[]{:S(2)}) collective-permute-start(bf16[64,32,128]{2,1,0:T(8,128)(2,1)S(1)} %pad_maximum_fusion.4.refs_0_), channel_id=1, source_target_pairs={{0,4},{2,6},{4,0},{6,2},{1,5},{3,7},{5,1},{7,3},{8,12},{10,14},{12... | collective-permute-start | bytes 1572872 | tf_op jit(solution)/shard_map/ppermute | solution.py:21
  204.2 19.1 %collective-permute-start.27 = (bf16[64,32,128]{2,1,0:T(8,128)(2,1)S(1)}, bf16[64,32,128]{2,1,0:T(8,128)(2,1)S(1)}, u32[]{:S(2)}, u32[]{:S(2)}) collective-permute-start(bf16[64,32,128]{2,1,0:T(8,128)(2,1)S(1)} %pad_maximum_fusion.4.refs_0_), channel_id=1, source_target_pairs={{0,6},{2,0},{4,2},{6,4},{1,7},{3,1},{5,3},{7,5},{8,14},{10,8},{12,... | collective-permute-start | bytes 1572872 | tf_op jit(solution)/shard_map/ppermute | solution.py:21
  209.4 15.1 %collective-permute-start.35 = (bf16[64,32,128]{2,1,0:T(8,128)(2,1)S(1)}, bf16[64,32,128]{2,1,0:T(8,128)(2,1)S(1)}, u32[]{:S(2)}, u32[]{:S(2)}) collective-permute-start(bf16[64,32,128]{2,1,0:T(8,128)(2,1)S(1)} %pad_maximum_fusion.5.refs_4_), channel_id=1, source_target_pairs={{0,8},{8,16},{16,24},{24,0},{1,9},{9,17},{17,25},{25,1},{2,10},{10... | collective-permute-start | bytes 1572872 | tf_op jit(solution)/shard_map/ppermute | solution.py:21
  210.1 16.6 %collective-permute-start.34 = (bf16[64,32,128]{2,1,0:T(8,128)(2,1)S(1)}, bf16[64,32,128]{2,1,0:T(8,128)(2,1)S(1)}, u32[]{:S(2)}, u32[]{:S(2)}) collective-permute-start(bf16[64,32,128]{2,1,0:T(8,128)(2,1)S(1)} %pad_maximum_fusion.5.refs_4_), channel_id=1, source_target_pairs={{0,16},{8,24},{16,0},{24,8},{1,17},{9,25},{17,1},{25,9},{2,18},{10... | collective-permute-start | bytes 1572872 | tf_op jit(solution)/shard_map/ppermute | solution.py:21
  213.8 19.1 %collective-permute-start.33 = (bf16[64,32,128]{2,1,0:T(8,128)(2,1)S(1)}, bf16[64,32,128]{2,1,0:T(8,128)(2,1)S(1)}, u32[]{:S(2)}, u32[]{:S(2)}) collective-permute-start(bf16[64,32,128]{2,1,0:T(8,128)(2,1)S(1)} %pad_maximum_fusion.5.refs_4_), channel_id=1, source_target_pairs={{0,24},{8,0},{16,8},{24,16},{1,25},{9,1},{17,9},{25,17},{2,26},{10... | collective-permute-start | bytes 1572872 | tf_op jit(solution)/shard_map/ppermute | solution.py:21
  (12 other events, 273.0 us)
Sparse Core Ops, SparseCore 0:
  9.2 61.6 all-gather.1

commit v2 on v1

v2 whole, which is shorter than its diff:
```python
import functools

import jax
import jax.numpy as jnp
from jax import lax
from jax.experimental import pallas as pl
from jax.experimental.pallas import tpu as pltpu
from jax.sharding import Mesh, PartitionSpec as P

REMOTE = 4
STEPS = 3
SIDE = 4
GROUP = 8
BS = 128
STREAMS = 2
UNROLL = 4
epsilon = 1e-06
XY = ("x", "y")


def shift(value, distance, stage):
    pairs = []
    for x in range(SIDE):
        for y in range(SIDE):
            for core in range(2):
                if core == stage:
                    source = ((x + distance) % SIDE) * SIDE + y
                else:
                    source = x * SIDE + (y + distance) % SIDE
                pairs.append((source * 2 + core, (x * SIDE + y) * 2 + core))
    return lax.ppermute(value, ("x", "y", "c"), pairs)


def pack_kernel(*refs):
    for i, source in enumerate(refs[:-1]):
        size = source.shape[0]
        refs[-1][pl.ds(i * size, size)] = source[...]


def pack(parts):
    size, genes, width = parts[0].shape
    return pl.pallas_call(
        pack_kernel,
        out_shape=jax.ShapeDtypeStruct((len(parts) * size, genes, width), parts[0].dtype),
        compiler_params=pltpu.CompilerParams(vmem_limit_bytes=16 * 1024 * 1024),
    )(*parts)


def spread(value, ring):
    value = pack([value] + [shift(value, d, 0) for d in (1, 2, 3)])
    if not ring:
        return [value] + [shift(value, d, 1) for d in (1, 2, 3)]
    half = value.shape[0] // 2
    after, before = shift(value, 1, 1), shift(value, 3, 1)
    low, high = shift(after[:half], 1, 1), shift(before[half:], 3, 1)
    return [value, after, low, high, before]


def step_kernel(pieces, raw, ends, place_ref, count_ref, table_ref, *refs):
    sources, refs = refs[:pieces], refs[pieces:]
    if raw:
        inverse_ref, refs = refs[0], refs[1:]
    aff_ref, out_refs, refs = refs[0], refs[1 : 1 + ends], refs[1 + ends :]
    peak_ref, own_peak_ref, held, kept, sems = refs
    blocks, slots = aff_ref.shape[:2]
    genes = held.shape[1]
    parts = 4
    size = blocks // parts

    def part(i):
        rows = pl.ds(i * size, size)
        return pltpu.make_async_copy(aff_ref.at[rows], kept.at[rows], sems.at[pieces + i])

    copies, start = [], 0
    for i, source in enumerate(sources):
        rows = source.shape[0]
        copies.append(pltpu.make_async_copy(source, held.at[pl.ds(start, rows)], sems.at[i]))
        start += rows
    part(0).start()
    for copy in copies:
        copy.start()
    for i in range(1, parts):
        part(i).start()
    for copy in copies:
        copy.wait()

    def fetch(item):
        tile = held[place_ref[item]]
        if raw:
            tile = tile.astype(jnp.float32) * inverse_ref[pl.ds(table_ref[item], 1), :]
            tile = tile.astype(jnp.bfloat16)
        return tile

    def one(row, peak, own_peak):
        count = count_ref[row]
        tiles = []
        for s in range(slots):
            tile = fetch(row * slots + s)
            if s == 0:
                own = tile.astype(jnp.float32)
            tile = jnp.concatenate([tile, jnp.ones((16, BS), tile.dtype)], axis=0)
            if s > REMOTE:
                tile = jnp.where(s < count, tile, jnp.zeros_like(tile))
            tiles.append(tile)
        left = jnp.concatenate(tiles, axis=1)
        right = kept[row].reshape(slots * BS, BS)
        total = jnp.dot(left, right, preferred_element_type=jnp.float32)
        mixed = 0.5 * own + total[:genes] * (0.5 / total[genes : genes + 1])
        for out_ref in out_refs:
            share = out_ref.shape[1]
            out_ref[row] = mixed[:share].astype(out_ref.dtype)
            mixed = jnp.concatenate([mixed[share:], mixed[:share]]) if ends > 1 else mixed
        return jnp.maximum(peak, mixed), jnp.maximum(own_peak, own)

    def several(i, carry):
        for j in range(UNROLL):
            carry = one(i * UNROLL + j, *carry)
        return carry

    carry = (jnp.zeros((genes, BS), jnp.float32),) * 2
    for i in range(parts):
        part(i).wait()
        each = size // UNROLL
        carry = lax.fori_loop(i * each, (i + 1) * each, several, carry)
    peak_ref[...], own_peak_ref[...] = carry


def diffuse(pieces, places, counts, tables, inverse, affinity, ends):
    blocks = affinity.shape[0]
    genes = pieces[0].shape[1]
    total = sum(piece.shape[0] for piece in pieces)
    n = len(pieces)
    raw = inverse is not None
    smem = pl.BlockSpec(memory_space=pltpu.SMEM)
    vmem = pl.BlockSpec(memory_space=pltpu.VMEM)
    return pl.pallas_call(
        functools.partial(step_kernel, n, raw, ends),
        in_specs=[smem] * 3
        + [pl.BlockSpec(memory_space=pl.ANY)] * n
        + [vmem] * raw
        + [pl.BlockSpec(memory_space=pl.ANY)],
        out_specs=[vmem] * (ends + 2),
        scratch_shapes=[
            pltpu.VMEM((total, genes, BS), pieces[0].dtype),
            pltpu.VMEM(affinity.shape, affinity.dtype),
            pltpu.SemaphoreType.DMA((n + 4,)),
        ],
        out_shape=[jax.ShapeDtypeStruct((blocks, genes // ends, BS), jnp.bfloat16)] * ends
        + [jax.ShapeDtypeStruct((genes, BS), jnp.float32)] * 2,
        compiler_params=pltpu.CompilerParams(vmem_limit_bytes=32 * 1024 * 1024),
        cost_estimate=pl.CostEstimate(
            flops=2 * affinity.size * genes,
            bytes_accessed=2 * affinity.size,
            transcendentals=0,
        ),
    )(places, counts, tables, *pieces, *([inverse] if raw else []), affinity)


def to_all(value, axis, size):
    return lax.all_to_all(
        jnp.broadcast_to(value[None], (size,) + value.shape), axis, 0, 0, tiled=True
    )


def local(stored, neighbours, counts, affinity):
    core, my_x, my_y = lax.axis_index("c"), lax.axis_index("x"), lax.axis_index("y")
    blocks_dev, slots = neighbours.shape
    part = lax.dynamic_slice_in_dim(affinity, core * (blocks_dev // 2), blocks_dev // 2, 0)
    affinity = lax.all_gather(part, ("z", "c"), tiled=True)

    genes_dev = stored.shape[0]
    cells_dev = blocks_dev * BS
    blocks = GROUP * blocks_dev
    counted = stored.reshape(genes_dev, GROUP, SIDE * SIDE, cells_dev)
    counted = lax.all_to_all(counted, XY, 2, 0, tiled=True)
    genes = counted.shape[0]
    counted = jnp.transpose(counted.reshape(genes, blocks, BS), (1, 0, 2))

    table = jnp.concatenate([neighbours, counts[:, None]], axis=1).reshape(1, -1)
    used = table.shape[1]
    table = jnp.pad(table.astype(jnp.float32), ((0, 7), (0, BS - used)))
    sums = lax.psum(jnp.sum(counted.astype(jnp.float32), axis=1), "c")
    sums = to_all(jnp.concatenate([sums, table]), "z", GROUP)
    inverse = (2 * GROUP * genes) / jnp.sum(sums[:, :blocks], axis=0)
    inverse = to_all(inverse, XY, SIDE * SIDE).reshape(-1, BS)
    table = sums[:, blocks, :used].astype(jnp.int32).reshape(blocks, slots + 1)
    neighbours, counts = table[:, :slots], table[:, slots]

    device, inner = neighbours // blocks_dev, neighbours % blocks_dev
    within = device // (SIDE * SIDE) * blocks_dev + inner
    dx = (device // SIDE - my_x) % SIDE
    dy = (device - my_y) % SIDE
    first, second = jnp.where(core == 0, dx, dy), jnp.where(core == 0, dy, dx)
    places = ((second * SIDE + first) * blocks + within).reshape(-1)
    tables = ((device % (SIDE * SIDE)) * blocks + within).reshape(-1)

    *streams, peak, own_peak = diffuse(
        spread(counted, False), places, counts, tables, inverse, affinity, STREAMS
    )
    peaks = [own_peak, peak]
    for step in range(1, STEPS):
        pieces = [spread(stream, True) for stream in streams]
        ends = [diffuse(piece, places, counts, tables, None, affinity, 1) for piece in pieces]
        streams = [end[0] for end in ends]
        peaks.append(jnp.concatenate([end[1] for end in ends]))
    current = jnp.concatenate(streams, axis=1)
    peaks = jnp.max(jnp.stack(peaks), axis=2).reshape(-1)
    peaks = jnp.max(to_all(peaks, XY, SIDE * SIDE), axis=0).reshape(STEPS + 1, genes)
    scale = jnp.ones((genes,), jnp.float32)
    for step in range(STEPS):
        scale = scale * (peaks[0] / (scale * peaks[1 + step] + epsilon))
    result = (current.astype(jnp.float32) * scale[None, :, None]).astype(jnp.bfloat16)
    result = lax.all_to_all(result, "z", 0, 0, tiled=True)
    result = result.reshape(GROUP, blocks_dev, genes, BS).astype(jnp.float32)
    return jnp.transpose(result, (0, 2, 1, 3)).reshape(GROUP * genes, cells_dev)


def solution(mesh):
    grid = Mesh(mesh.devices.reshape(GROUP, SIDE, SIDE, 2), ("z", "x", "y", "c"))
    cells = ("z", "x", "y")
    return jax.shard_map(
        local,
        mesh=grid,
        in_specs=(P(cells, "c", None), P(cells, None), P(cells), P(cells, None, None, None)),
        out_specs=P("c", cells),
        check_vma=False,
    )
```

time: 291 us -> 198 us (0.68)
  waiting for transfers between devices: 110 us -> 38.5 us
  blocking collectives: 63.3 us -> 35 us
  Pallas kernels: 11.1 us -> 22.3 us
  starting transfers between devices: 81.9 us -> 75 us
    ppermute x36 -> x34, waiting for transfers between devices: 90.8 us -> 13.7 us  [shift(): return lax.ppermute(value, ('x', 'y', 'c'), pairs)]
    all_to_all x2 -> x1, blocking collectives: 44.7 us -> 17.9 us  [local(): result = lax.all_to_all(result, 'z', 0, 0, tiled=True)]
    ppermute x36 -> x34, starting transfers between devices: 70.1 us -> 53.2 us  [shift(): return lax.ppermute(value, ('x', 'y', 'c'), pairs)]
    pallas_call x3 -> x10, Pallas kernels: 11.1 us -> 22.3 us  [the longest x5 22.1 us: diffuse(): pl.pallas_call(functools.partial(step_kernel, n, raw, ends), in_specs=[sm...]
    all_to_all x0 -> x1, starting transfers between devices: none -> 7.48 us  [local(): counted = lax.all_to_all(counted, XY, 2, 0, tiled=True)]
    all_to_all x0 -> x1, waiting for transfers between devices: none -> 5.22 us  [local(): counted = lax.all_to_all(counted, XY, 2, 0, tiled=True)]
    unnamed x11 -> x8, local copies, waits for them, and re-layouts: 5.58 us -> 6.41 us
  transfers between devices with their start and end apart: 39 -> 38, of which waited for: 25 -> 11; matrix products, arithmetic and copies ran while one was open for 1% -> 3% of each run, Pallas kernels for 0% -> 7%
where the time goes in v2:
time: 198 us
  starting transfers between devices  75 us (38%)
  waiting for transfers between devices  38.5 us (19%)
  blocking collectives  35 us (18%)
  Pallas kernels  22.3 us (11%)
  between operations  13.7 us (7%)
  local copies, waits for them, and re-layouts  11.7 us (6%)
    ppermute x34, starting transfers between devices, shift(): return lax.ppermute(value, ('x', 'y', 'c'), pairs)  53.2 us
    pallas_call x5, Pallas kernels, diffuse(): pl.pallas_call(functools.partial(step_kernel, n, raw, ends), in_specs=[sm...  22.1 us
    all_to_all x2, waiting for transfers between devices, to_all(): lax.all_to_all(jnp.broadcast_to(value[None], (size,) + value.shape), axis...  19.5 us
    all_to_all x1, blocking collectives, local(): result = lax.all_to_all(result, 'z', 0, 0, tiled=True)  17.9 us
    all_to_all x2, starting transfers between devices, to_all(): lax.all_to_all(jnp.broadcast_to(value[None], (size,) + value.shape), axis...  14.3 us
    all_to_all x1, blocking collectives, to_all(): lax.all_to_all(jnp.broadcast_to(value[None], (size,) + value.shape), axis...  13.7 us
    ppermute x34, waiting for transfers between devices, shift(): return lax.ppermute(value, ('x', 'y', 'c'), pairs)  13.7 us
    all_to_all x1, starting transfers between devices, local(): counted = lax.all_to_all(counted, XY, 2, 0, tiled=True)  7.48 us
  transfers between devices with their start and end apart: 38, of which 11 were waited for; matrix products, arithmetic and copies ran while one was open for 3% of the time, Pallas kernels for 7%

profile of v2, /device:TPU:2, one launch (start us, length us, event | category | flops | bytes accessed | tf_op | source)
XLA Modules:
  0.0 197.6 jit_solution(7933963094660547007)
XLA Ops:
  10.5 7.5 %all-to-all-start = ((bf16[2,8,16,512]{3,1,0,2:T(8,128)(2,1)}), bf16[2,8,16,512]{3,1,0,2:T(8,128)(2,1)S(1)}, u32[]{:S(2)}, u32[]{:S(2)}) async-start(bf16[2,8,16,512]{3,1,0,2:T(8,128)(2,1)} %copy.23), calls=%async_computation | async-start | bytes 524288 | tf_op jit(solution)/shard_map/all_to_all | solution.py:175
  19.5 5.2 %all-to-all-done = bf16[2,8,16,512]{3,1,0,2:T(8,128)(2,1)S(1)} async-done(((bf16[2,8,16,512]{3,1,0,2:T(8,128)(2,1)}), bf16[2,8,16,512]{3,1,0,2:T(8,128)(2,1)S(1)}, u32[]{:S(2)}, u32[]{:S(2)}) %all-to-all-start) | async-done | bytes 262176 | tf_op jit(solution)/shard_map/all_to_all | solution.py:175
  26.2 2.8 %collective-permute-start.1 = (bf16[32,32,128]{2,1,0:T(8,128)(2,1)S(1)}, bf16[32,32,128]{2,1,0:T(8,128)(2,1)S(1)}, u32[]{:S(2)}, u32[]{:S(2)}) collective-permute-start(bf16[32,32,128]{2,1,0:T(8,128)(2,1)S(1)} %bitcast.37), channel_id=1, source_target_pairs={{16,0},{5,1},{18,2},{7,3},{20,4},{1,5},{22,6},{3,7},{24,8},{13,9},... | collective-permute-start | bytes 786440 | tf_op jit(solution)/shard_map/ppermute | solution.py:31
  29.5 3.4 %psum.7 = f32[32,128]{1,0:T(8,128)S(1)} all-reduce(f32[32,128]{1,0:T(8,128)S(1)} %convert_reduce_fusion), channel_id=1, replica_groups=mesh['z'=8,'x'=4,'y'=4,'c'=2] {'c'}, use_global_device_ids=true, to_apply=%region_1.2 | all-reduce | flops 4096 | bytes 32768 | tf_op jit(solution)/shard_map/psum | solution.py:182
  33.6 8.5 %all-to-all-start.1 = ((f32[8,40,128]{2,1,0:T(8,128)}), f32[8,40,128]{2,1,0:T(8,128)S(1)}, u32[]{:S(2)}, u32[]{:S(2)}) async-start(f32[8,40,128]{2,1,0:T(8,128)} %broadcast_in_dim.11), calls=%async_computation.1 | async-start | bytes 327680 | tf_op jit(solution)/shard_map/all_to_all | solution.py:160
  42.8 1.8 collective-permute-start.4
  46.3 8.1 %all-to-all-done.1 = f32[8,40,128]{2,1,0:T(8,128)S(1)} async-done(((f32[8,40,128]{2,1,0:T(8,128)}), f32[8,40,128]{2,1,0:T(8,128)S(1)}, u32[]{:S(2)}, u32[]{:S(2)}) %all-to-all-start.1) | async-done | bytes 163872 | tf_op jit(solution)/shard_map/all_to_all | solution.py:160
  55.3 5.9 %all-to-all-start.2 = ((f32[16,32,128]{2,1,0:T(8,128)}), f32[16,32,128]{2,1,0:T(8,128)S(1)}, u32[]{:S(2)}, u32[]{:S(2)}) async-start(f32[16,32,128]{2,1,0:T(8,128)} %broadcast_in_dim.12), calls=%async_computation.2 | async-start | bytes 524288 | tf_op jit(solution)/shard_map/all_to_all | solution.py:160
  61.6 11.4 %all-to-all-done.2 = f32[16,32,128]{2,1,0:T(8,128)S(1)} async-done(((f32[16,32,128]{2,1,0:T(8,128)}), f32[16,32,128]{2,1,0:T(8,128)S(1)}, u32[]{:S(2)}, u32[]{:S(2)}) %all-to-all-start.2) | async-done | bytes 262176 | tf_op jit(solution)/shard_map/all_to_all | solution.py:160
  73.1 3.4 %copy-done.1 = bf16[32,8,128,128]{3,2,1,0:T(8,128)(2,1)S(1)} copy-done((bf16[32,8,128,128]{3,2,1,0:T(8,128)(2,1)S(1)}, bf16[32,8,128,128]{3,2,1,0:T(8,128)(2,1)}, u32[]{:S(2)}) %copy-start.1) | copy-done | bytes 8388632
  76.5 5.2 %shard_map.47 = (bf16[32,16,128]{2,1,0:T(8,128)(2,1)S(1)}, bf16[32,16,128]{2,1,0:T(8,128)(2,1)S(1)}, f32[32,128]{1,0:T(8,128)S(1)}, f32[32,128]{1,0:T(8,128)S(1)}) custom-call(s32[256]{0:T(256)S(1)} %reshape.66.place_ref, s32[32]{0:T(128)S(1)} %slice_reduce_fusion.1.count_ref, s32[256]{0:T(256)S(1)} %reshape.67.table_ref, ...), custom_call_target="tpu_custom_call" | custom-call | flops 268435456 | bytes 8388608 | tf_op jit(solution)/shard_map/pallas_call | solution.py:136
  83.3 1.9 collective-permute-start.21
  87.2 2.8 %collective-permute-start.7 = (bf16[32,16,128]{2,1,0:T(8,128)(2,1)S(1)}, bf16[32,16,128]{2,1,0:T(8,128)(2,1)S(1)}, u32[]{:S(2)}, u32[]{:S(2)}) collective-permute-start(bf16[32,16,128]{2,1,0:T(8,128)(2,1)S(1)} %get-tuple-element.17.refs_0_), channel_id=1, source_target_pairs={{16,0},{5,1},{18,2},{7,3},{20,4},{1,5},{22,6},{3,7},{24,8},{13,9},... | collective-permute-start | bytes 393224 | tf_op jit(solution)/shard_map/ppermute | solution.py:31
  92.5 2.2 %collective-permute-start.23 = (bf16[128,16,128]{2,1,0:T(8,128)(2,1)S(1)}, bf16[128,16,128]{2,1,0:T(8,128)(2,1)S(1)}, u32[]{:S(2)}, u32[]{:S(2)}) collective-permute-start(bf16[128,16,128]{2,1,0:T(8,128)(2,1)S(1)} %shard_map.52.refs_0_), channel_id=1, source_target_pairs={{2,0},{9,1},{4,2},{11,3},{6,4},{13,5},{0,6},{15,7},{10,8},{17,9},{... | collective-permute-start | bytes 1572872 | tf_op jit(solution)/shard_map/ppermute | solution.py:31
  94.7 1.9 collective-permute-done.6.refs_1_
  97.8 2.2 %collective-permute-start.9 = (bf16[128,16,128]{2,1,0:T(8,128)(2,1)S(1)}, bf16[128,16,128]{2,1,0:T(8,128)(2,1)S(1)}, u32[]{:S(2)}, u32[]{:S(2)}) collective-permute-start(bf16[128,16,128]{2,1,0:T(8,128)(2,1)S(1)} %shard_map.48.refs_0_), channel_id=1, source_target_pairs={{2,0},{9,1},{4,2},{11,3},{6,4},{13,5},{0,6},{15,7},{10,8},{17,9},{... | collective-permute-start | bytes 1572872 | tf_op jit(solution)/shard_map/ppermute | solution.py:31
  100.0 1.9 collective-permute-done.25.refs_4_
  102.0 3.3 %collective-permute-start.24 = (bf16[64,16,128]{2,1,0:T(8,128)(2,1)S(1)}, bf16[64,16,128]{2,1,0:T(8,128)(2,1)S(1)}, u32[]{:S(2)}, u32[]{:S(2)}) collective-permute-start(bf16[64,16,128]{2,1,0:T(8,128)(2,1)S(1)} %slice.78), channel_id=1, source_target_pairs={{2,0},{9,1},{4,2},{11,3},{6,4},{13,5},{0,6},{15,7},{10,8},{17,9},{... | collective-permute-start | bytes 786440 | tf_op jit(solution)/shard_map/ppermute | solution.py:31
  105.3 2.2 %collective-permute-done.11.refs_4_ = bf16[128,16,128]{2,1,0:T(8,128)(2,1)S(1)} collective-permute-done((bf16[128,16,128]{2,1,0:T(8,128)(2,1)S(1)}, bf16[128,16,128]{2,1,0:T(8,128)(2,1)S(1)}, u32[]{:S(2)}, u32[]{:S(2)}) %collective-permute-start.11) | collective-permute-done | bytes 524320 | tf_op jit(solution)/shard_map/ppermute | solution.py:31
  107.6 3.3 %collective-permute-start.10 = (bf16[64,16,128]{2,1,0:T(8,128)(2,1)S(1)}, bf16[64,16,128]{2,1,0:T(8,128)(2,1)S(1)}, u32[]{:S(2)}, u32[]{:S(2)}) collective-permute-start(bf16[64,16,128]{2,1,0:T(8,128)(2,1)S(1)} %slice.74), channel_id=1, source_target_pairs={{2,0},{9,1},{4,2},{11,3},{6,4},{13,5},{0,6},{15,7},{10,8},{17,9},{... | collective-permute-start | bytes 786440 | tf_op jit(solution)/shard_map/ppermute | solution.py:31
  110.9 4.2 %shard_map.53 = (bf16[32,16,128]{2,1,0:T(8,128)(2,1)S(1)}, f32[16,128]{1,0:T(8,128)S(1)}, f32[16,128]{1,0:T(8,128)}) custom-call(s32[256]{0:T(256)S(1)} %reshape.66.place_ref, s32[32]{0:T(128)S(1)} %slice_reduce_fusion.1.count_ref, s32[256]{0:T(256)S(1)} %reshape.67.table_ref, bf16[128,16,128]{2,1,0:T(8,128)(2,1)S(1)} %shard_map.52.refs_0_, ...), custom_call_target="tpu_custom_call" | custom-call | flops 134217728 | bytes 8388608 | tf_op jit(solution)/shard_map/pallas_call | solution.py:136
  116.2 3.2 %collective-permute-start.28 = (bf16[32,16,128]{2,1,0:T(8,128)(2,1)S(1)}, bf16[32,16,128]{2,1,0:T(8,128)(2,1)S(1)}, u32[]{:S(2)}, u32[]{:S(2)}) collective-permute-start(bf16[32,16,128]{2,1,0:T(8,128)(2,1)S(1)} %get-tuple-element.21.refs_0_), channel_id=1, source_target_pairs={{16,0},{5,1},{18,2},{7,3},{20,4},{1,5},{22,6},{3,7},{24,8},{13,9},... | collective-permute-start | bytes 393224 | tf_op jit(solution)/shard_map/ppermute | solution.py:31
  120.4 4.2 %shard_map.49 = (bf16[32,16,128]{2,1,0:T(8,128)(2,1)S(1)}, f32[16,128]{1,0:T(8,128)S(1)}, f32[16,128]{1,0:T(8,128)}) custom-call(s32[256]{0:T(256)S(1)} %reshape.66.place_ref, s32[32]{0:T(128)S(1)} %slice_reduce_fusion.1.count_ref, s32[256]{0:T(256)S(1)} %reshape.67.table_ref, bf16[128,16,128]{2,1,0:T(8,128)(2,1)S(1)} %shard_map.48.refs_0_, ...), custom_call_target="tpu_custom_call" | custom-call | flops 134217728 | bytes 8388608 | tf_op jit(solution)/shard_map/pallas_call | solution.py:136
  128.9 2.6 %collective-permute-start.30 = (bf16[128,16,128]{2,1,0:T(8,128)(2,1)S(1)}, bf16[128,16,128]{2,1,0:T(8,128)(2,1)S(1)}, u32[]{:S(2)}, u32[]{:S(2)}) collective-permute-start(bf16[128,16,128]{2,1,0:T(8,128)(2,1)S(1)} %shard_map.54.refs_0_), channel_id=1, source_target_pairs={{2,0},{9,1},{4,2},{11,3},{6,4},{13,5},{0,6},{15,7},{10,8},{17,9},{... | collective-permute-start | bytes 1572872 | tf_op jit(solution)/shard_map/ppermute | solution.py:31
  135.6 2.7 %collective-permute-start.16 = (bf16[128,16,128]{2,1,0:T(8,128)(2,1)S(1)}, bf16[128,16,128]{2,1,0:T(8,128)(2,1)S(1)}, u32[]{:S(2)}, u32[]{:S(2)}) collective-permute-start(bf16[128,16,128]{2,1,0:T(8,128)(2,1)S(1)} %shard_map.50.refs_0_), channel_id=1, source_target_pairs={{2,0},{9,1},{4,2},{11,3},{6,4},{13,5},{0,6},{15,7},{10,8},{17,9},{... | collective-permute-start | bytes 1572872 | tf_op jit(solution)/shard_map/ppermute | solution.py:31
  138.8 3.3 %collective-permute-start.31 = (bf16[64,16,128]{2,1,0:T(8,128)(2,1)S(1)}, bf16[64,16,128]{2,1,0:T(8,128)(2,1)S(1)}, u32[]{:S(2)}, u32[]{:S(2)}) collective-permute-start(bf16[64,16,128]{2,1,0:T(8,128)(2,1)S(1)} %slice.80), channel_id=1, source_target_pairs={{2,0},{9,1},{4,2},{11,3},{6,4},{13,5},{0,6},{15,7},{10,8},{17,9},{... | collective-permute-start | bytes 786440 | tf_op jit(solution)/shard_map/ppermute | solution.py:31
  142.1 3.4 %collective-permute-done.18.refs_4_ = bf16[128,16,128]{2,1,0:T(8,128)(2,1)S(1)} collective-permute-done((bf16[128,16,128]{2,1,0:T(8,128)(2,1)S(1)}, bf16[128,16,128]{2,1,0:T(8,128)(2,1)S(1)}, u32[]{:S(2)}, u32[]{:S(2)}) %collective-permute-start.18) | collective-permute-done | bytes 524320 | tf_op jit(solution)/shard_map/ppermute | solution.py:31
  145.7 3.3 %collective-permute-start.17 = (bf16[64,16,128]{2,1,0:T(8,128)(2,1)S(1)}, bf16[64,16,128]{2,1,0:T(8,128)(2,1)S(1)}, u32[]{:S(2)}, u32[]{:S(2)}) collective-permute-start(bf16[64,16,128]{2,1,0:T(8,128)(2,1)S(1)} %slice.76), channel_id=1, source_target_pairs={{2,0},{9,1},{4,2},{11,3},{6,4},{13,5},{0,6},{15,7},{10,8},{17,9},{... | collective-permute-start | bytes 786440 | tf_op jit(solution)/shard_map/ppermute | solution.py:31
  149.0 4.2 %shard_map.55 = (bf16[32,16,128]{2,1,0:T(8,128)(2,1)S(1)}, f32[16,128]{1,0:T(8,128)S(1)}, f32[16,128]{1,0:T(8,128)}) custom-call(s32[256]{0:T(256)S(1)} %reshape.66.place_ref, s32[32]{0:T(128)S(1)} %slice_reduce_fusion.1.count_ref, s32[256]{0:T(256)S(1)} %reshape.67.table_ref, bf16[128,16,128]{2,1,0:T(8,128)(2,1)S(1)} %shard_map.54.refs_0_, ...), custom_call_target="tpu_custom_call" | custom-call | flops 134217728 | bytes 8388608 | tf_op jit(solution)/shard_map/pallas_call | solution.py:136
  153.2 4.2 %shard_map.51 = (bf16[32,16,128]{2,1,0:T(8,128)(2,1)S(1)}, f32[16,128]{1,0:T(8,128)S(1)}, f32[16,128]{1,0:T(8,128)}) custom-call(s32[256]{0:T(256)S(1)} %reshape.66.place_ref, s32[32]{0:T(128)S(1)} %slice_reduce_fusion.1.count_ref, s32[256]{0:T(256)S(1)} %reshape.67.table_ref, bf16[128,16,128]{2,1,0:T(8,128)(2,1)S(1)} %shard_map.50.refs_0_, ...), custom_call_target="tpu_custom_call" | custom-call | flops 134217728 | bytes 8388608 | tf_op jit(solution)/shard_map/pallas_call | solution.py:136
  157.7 13.7 %all_to_all.36 = f32[16,1,128]{2,1,0:T(1,128)S(1)} all-to-all(f32[16,1,128]{2,1,0:T(1,128)S(1)} %broadcast_in_dim.27), channel_id=1, replica_groups=mesh['z'=8,'x'=4,'y'=4,'c'=2] {'x','y'}, dimensions={0} | all-to-all | bytes 16384 | tf_op jit(solution)/shard_map/all_to_all | solution.py:160
  171.6 17.9 %all_to_all.37 = bf16[32,32,128]{2,1,0:T(8,128)(2,1)S(1)} all-to-all(bf16[32,32,128]{2,1,0:T(8,128)(2,1)S(1)} %multiply_convert_fusion), channel_id=1, replica_groups=mesh['z'=8,'x'=4,'y'=4,'c'=2] {'z'}, dimensions={0} | all-to-all | bytes 524288 | tf_op jit(solution)/shard_map/all_to_all | solution.py:213
  (104 shorter events, 31.9 us)
Async XLA Ops:
  6.5 66.5 %all-gather.2.cloned.1.call-start = ((), (), s32[]{:S(2)}) async-start(), calls=%async_computation.5 | async-start | bytes 8912896 | tf_op jit(solution)/shard_map/all_gather | solution.py:169
  10.5 14.3 %all-to-all-start = ((bf16[2,8,16,512]{3,1,0,2:T(8,128)(2,1)}), bf16[2,8,16,512]{3,1,0,2:T(8,128)(2,1)S(1)}, u32[]{:S(2)}, u32[]{:S(2)}) async-start(bf16[2,8,16,512]{3,1,0,2:T(8,128)(2,1)} %copy.23), calls=%async_computation | async-start | bytes 524288 | tf_op jit(solution)/shard_map/all_to_all | solution.py:175
  25.0 17.0 %collective-permute-start.2 = (bf16[32,32,128]{2,1,0:T(8,128)(2,1)S(1)}, bf16[32,32,128]{2,1,0:T(8,128)(2,1)S(1)}, u32[]{:S(2)}, u32[]{:S(2)}) collective-permute-start(bf16[32,32,128]{2,1,0:T(8,128)(2,1)S(1)} %bitcast.36), channel_id=1, source_target_pairs={{24,0},{7,1},{26,2},{1,3},{28,4},{3,5},{30,6},{5,7},{0,8},{15,9},{... | collective-permute-start | bytes 786440 | tf_op jit(solution)/shard_map/ppermute | solution.py:31
  26.2 15.9 %collective-permute-start.1 = (bf16[32,32,128]{2,1,0:T(8,128)(2,1)S(1)}, bf16[32,32,128]{2,1,0:T(8,128)(2,1)S(1)}, u32[]{:S(2)}, u32[]{:S(2)}) collective-permute-start(bf16[32,32,128]{2,1,0:T(8,128)(2,1)S(1)} %bitcast.37), channel_id=1, source_target_pairs={{16,0},{5,1},{18,2},{7,3},{20,4},{1,5},{22,6},{3,7},{24,8},{13,9},... | collective-permute-start | bytes 786440 | tf_op jit(solution)/shard_map/ppermute | solution.py:31
  29.0 13.1 %collective-permute-start = (bf16[32,32,128]{2,1,0:T(8,128)(2,1)S(1)}, bf16[32,32,128]{2,1,0:T(8,128)(2,1)S(1)}, u32[]{:S(2)}, u32[]{:S(2)}) collective-permute-start(bf16[32,32,128]{2,1,0:T(8,128)(2,1)S(1)} %bitcast.38), channel_id=1, source_target_pairs={{8,0},{3,1},{10,2},{5,3},{12,4},{7,5},{14,6},{1,7},{16,8},{11,9},{... | collective-permute-start | bytes 786440 | tf_op jit(solution)/shard_map/ppermute | solution.py:31
  33.6 20.8 %all-to-all-start.1 = ((f32[8,40,128]{2,1,0:T(8,128)}), f32[8,40,128]{2,1,0:T(8,128)S(1)}, u32[]{:S(2)}, u32[]{:S(2)}) async-start(f32[8,40,128]{2,1,0:T(8,128)} %broadcast_in_dim.11), calls=%async_computation.1 | async-start | bytes 327680 | tf_op jit(solution)/shard_map/all_to_all | solution.py:160
  42.2 30.9 %collective-permute-start.5 = (bf16[128,32,128]{2,1,0:T(8,128)(2,1)S(1)}, bf16[128,32,128]{2,1,0:T(8,128)(2,1)S(1)}, u32[]{:S(2)}, u32[]{:S(2)}) collective-permute-start(bf16[128,32,128]{2,1,0:T(8,128)(2,1)S(1)} %shard_map.46.refs_0_), channel_id=1, source_target_pairs={{6,0},{25,1},{0,2},{27,3},{2,4},{29,5},{4,6},{31,7},{14,8},{1,9},{... | collective-permute-start | bytes 3145736 | tf_op jit(solution)/shard_map/ppermute | solution.py:31
  42.8 30.2 %collective-permute-start.4 = (bf16[128,32,128]{2,1,0:T(8,128)(2,1)S(1)}, bf16[128,32,128]{2,1,0:T(8,128)(2,1)}, u32[]{:S(2)}, u32[]{:S(2)}) collective-permute-start(bf16[128,32,128]{2,1,0:T(8,128)(2,1)S(1)} %shard_map.46.refs_0_), channel_id=1, source_target_pairs={{4,0},{17,1},{6,2},{19,3},{0,4},{21,5},{2,6},{23,7},{12,8},{25,9},... | collective-permute-start | bytes 3145736 | tf_op jit(solution)/shard_map/ppermute | solution.py:31
  44.6 28.4 %collective-permute-start.3 = (bf16[128,32,128]{2,1,0:T(8,128)(2,1)S(1)}, bf16[128,32,128]{2,1,0:T(8,128)(2,1)}, u32[]{:S(2)}, u32[]{:S(2)}) collective-permute-start(bf16[128,32,128]{2,1,0:T(8,128)(2,1)S(1)} %shard_map.46.refs_0_), channel_id=1, source_target_pairs={{2,0},{9,1},{4,2},{11,3},{6,4},{13,5},{0,6},{15,7},{10,8},{17,9},{... | collective-permute-start | bytes 3145736 | tf_op jit(solution)/shard_map/ppermute | solution.py:31
  55.3 17.7 %all-to-all-start.2 = ((f32[16,32,128]{2,1,0:T(8,128)}), f32[16,32,128]{2,1,0:T(8,128)S(1)}, u32[]{:S(2)}, u32[]{:S(2)}) async-start(f32[16,32,128]{2,1,0:T(8,128)} %broadcast_in_dim.12), calls=%async_computation.2 | async-start | bytes 524288 | tf_op jit(solution)/shard_map/all_to_all | solution.py:160
  81.6 8.5 %collective-permute-start.22 = (bf16[32,16,128]{2,1,0:T(8,128)(2,1)S(1)}, bf16[32,16,128]{2,1,0:T(8,128)(2,1)S(1)}, u32[]{:S(2)}, u32[]{:S(2)}) collective-permute-start(bf16[32,16,128]{2,1,0:T(8,128)(2,1)S(1)} %get-tuple-element.20.refs_0_), channel_id=1, source_target_pairs={{24,0},{7,1},{26,2},{1,3},{28,4},{3,5},{30,6},{5,7},{0,8},{15,9},{... | collective-permute-start | bytes 393224 | tf_op jit(solution)/shard_map/ppermute | solution.py:31
  85.5 9.2 %collective-permute-start.8 = (bf16[32,16,128]{2,1,0:T(8,128)(2,1)S(1)}, bf16[32,16,128]{2,1,0:T(8,128)(2,1)S(1)}, u32[]{:S(2)}, u32[]{:S(2)}) collective-permute-start(bf16[32,16,128]{2,1,0:T(8,128)(2,1)S(1)} %get-tuple-element.17.refs_0_), channel_id=1, source_target_pairs={{24,0},{7,1},{26,2},{1,3},{28,4},{3,5},{30,6},{5,7},{0,8},{15,9},{... | collective-permute-start | bytes 393224 | tf_op jit(solution)/shard_map/ppermute | solution.py:31
  91.2 10.6 %collective-permute-start.25 = (bf16[128,16,128]{2,1,0:T(8,128)(2,1)S(1)}, bf16[128,16,128]{2,1,0:T(8,128)(2,1)S(1)}, u32[]{:S(2)}, u32[]{:S(2)}) collective-permute-start(bf16[128,16,128]{2,1,0:T(8,128)(2,1)S(1)} %shard_map.52.refs_0_), channel_id=1, source_target_pairs={{6,0},{25,1},{0,2},{27,3},{2,4},{29,5},{4,6},{31,7},{14,8},{1,9},{... | collective-permute-start | bytes 1572872 | tf_op jit(solution)/shard_map/ppermute | solution.py:31
  92.5 9.5 %collective-permute-start.23 = (bf16[128,16,128]{2,1,0:T(8,128)(2,1)S(1)}, bf16[128,16,128]{2,1,0:T(8,128)(2,1)S(1)}, u32[]{:S(2)}, u32[]{:S(2)}) collective-permute-start(bf16[128,16,128]{2,1,0:T(8,128)(2,1)S(1)} %shard_map.52.refs_0_), channel_id=1, source_target_pairs={{2,0},{9,1},{4,2},{11,3},{6,4},{13,5},{0,6},{15,7},{10,8},{17,9},{... | collective-permute-start | bytes 1572872 | tf_op jit(solution)/shard_map/ppermute | solution.py:31
  96.7 10.8 %collective-permute-start.11 = (bf16[128,16,128]{2,1,0:T(8,128)(2,1)S(1)}, bf16[128,16,128]{2,1,0:T(8,128)(2,1)S(1)}, u32[]{:S(2)}, u32[]{:S(2)}) collective-permute-start(bf16[128,16,128]{2,1,0:T(8,128)(2,1)S(1)} %shard_map.48.refs_0_), channel_id=1, source_target_pairs={{6,0},{25,1},{0,2},{27,3},{2,4},{29,5},{4,6},{31,7},{14,8},{1,9},{... | collective-permute-start | bytes 1572872 | tf_op jit(solution)/shard_map/ppermute | solution.py:31
  97.8 9.9 %collective-permute-start.9 = (bf16[128,16,128]{2,1,0:T(8,128)(2,1)S(1)}, bf16[128,16,128]{2,1,0:T(8,128)(2,1)S(1)}, u32[]{:S(2)}, u32[]{:S(2)}) collective-permute-start(bf16[128,16,128]{2,1,0:T(8,128)(2,1)S(1)} %shard_map.48.refs_0_), channel_id=1, source_target_pairs={{2,0},{9,1},{4,2},{11,3},{6,4},{13,5},{0,6},{15,7},{10,8},{17,9},{... | collective-permute-start | bytes 1572872 | tf_op jit(solution)/shard_map/ppermute | solution.py:31
  101.9 9.0 %collective-permute-start.26 = (bf16[64,16,128]{2,1,0:T(8,128)(2,1)S(1)}, bf16[64,16,128]{2,1,0:T(8,128)(2,1)S(1)}, u32[]{:S(2)}, u32[]{:S(2)}) collective-permute-start(bf16[64,16,128]{2,1,0:T(8,128)(2,1)S(1)} %slice.79), channel_id=1, source_target_pairs={{6,0},{25,1},{0,2},{27,3},{2,4},{29,5},{4,6},{31,7},{14,8},{1,9},{... | collective-permute-start | bytes 786440 | tf_op jit(solution)/shard_map/ppermute | solution.py:31
  102.0 8.9 %collective-permute-start.24 = (bf16[64,16,128]{2,1,0:T(8,128)(2,1)S(1)}, bf16[64,16,128]{2,1,0:T(8,128)(2,1)S(1)}, u32[]{:S(2)}, u32[]{:S(2)}) collective-permute-start(bf16[64,16,128]{2,1,0:T(8,128)(2,1)S(1)} %slice.78), channel_id=1, source_target_pairs={{2,0},{9,1},{4,2},{11,3},{6,4},{13,5},{0,6},{15,7},{10,8},{17,9},{... | collective-permute-start | bytes 786440 | tf_op jit(solution)/shard_map/ppermute | solution.py:31
  107.5 12.8 %collective-permute-start.12 = (bf16[64,16,128]{2,1,0:T(8,128)(2,1)S(1)}, bf16[64,16,128]{2,1,0:T(8,128)(2,1)S(1)}, u32[]{:S(2)}, u32[]{:S(2)}) collective-permute-start(bf16[64,16,128]{2,1,0:T(8,128)(2,1)S(1)} %slice.75), channel_id=1, source_target_pairs={{6,0},{25,1},{0,2},{27,3},{2,4},{29,5},{4,6},{31,7},{14,8},{1,9},{... | collective-permute-start | bytes 786440 | tf_op jit(solution)/shard_map/ppermute | solution.py:31
  107.6 12.7 %collective-permute-start.10 = (bf16[64,16,128]{2,1,0:T(8,128)(2,1)S(1)}, bf16[64,16,128]{2,1,0:T(8,128)(2,1)S(1)}, u32[]{:S(2)}, u32[]{:S(2)}) collective-permute-start(bf16[64,16,128]{2,1,0:T(8,128)(2,1)S(1)} %slice.74), channel_id=1, source_target_pairs={{2,0},{9,1},{4,2},{11,3},{6,4},{13,5},{0,6},{15,7},{10,8},{17,9},{... | collective-permute-start | bytes 786440 | tf_op jit(solution)/shard_map/ppermute | solution.py:31
  115.2 12.1 %collective-permute-start.29 = (bf16[32,16,128]{2,1,0:T(8,128)(2,1)S(1)}, bf16[32,16,128]{2,1,0:T(8,128)(2,1)S(1)}, u32[]{:S(2)}, u32[]{:S(2)}) collective-permute-start(bf16[32,16,128]{2,1,0:T(8,128)(2,1)S(1)} %get-tuple-element.21.refs_0_), channel_id=1, source_target_pairs={{24,0},{7,1},{26,2},{1,3},{28,4},{3,5},{30,6},{5,7},{0,8},{15,9},{... | collective-permute-start | bytes 393224 | tf_op jit(solution)/shard_map/ppermute | solution.py:31
  116.2 11.7 %collective-permute-start.28 = (bf16[32,16,128]{2,1,0:T(8,128)(2,1)S(1)}, bf16[32,16,128]{2,1,0:T(8,128)(2,1)S(1)}, u32[]{:S(2)}, u32[]{:S(2)}) collective-permute-start(bf16[32,16,128]{2,1,0:T(8,128)(2,1)S(1)} %get-tuple-element.21.refs_0_), channel_id=1, source_target_pairs={{16,0},{5,1},{18,2},{7,3},{20,4},{1,5},{22,6},{3,7},{24,8},{13,9},... | collective-permute-start | bytes 393224 | tf_op jit(solution)/shard_map/ppermute | solution.py:31
  119.4 8.5 %collective-permute-start.27 = (bf16[32,16,128]{2,1,0:T(8,128)(2,1)S(1)}, bf16[32,16,128]{2,1,0:T(8,128)(2,1)S(1)}, u32[]{:S(2)}, u32[]{:S(2)}) collective-permute-start(bf16[32,16,128]{2,1,0:T(8,128)(2,1)S(1)} %get-tuple-element.21.refs_0_), channel_id=1, source_target_pairs={{8,0},{3,1},{10,2},{5,3},{12,4},{7,5},{14,6},{1,7},{16,8},{11,9},{... | collective-permute-start | bytes 393224 | tf_op jit(solution)/shard_map/ppermute | solution.py:31
  127.3 7.7 %collective-permute-start.13 = (bf16[32,16,128]{2,1,0:T(8,128)(2,1)S(1)}, bf16[32,16,128]{2,1,0:T(8,128)(2,1)S(1)}, u32[]{:S(2)}, u32[]{:S(2)}) collective-permute-start(bf16[32,16,128]{2,1,0:T(8,128)(2,1)S(1)} %get-tuple-element.18.refs_0_), channel_id=1, source_target_pairs={{8,0},{3,1},{10,2},{5,3},{12,4},{7,5},{14,6},{1,7},{16,8},{11,9},{... | collective-permute-start | bytes 393224 | tf_op jit(solution)/shard_map/ppermute | solution.py:31
  128.0 10.7 %collective-permute-start.32 = (bf16[128,16,128]{2,1,0:T(8,128)(2,1)S(1)}, bf16[128,16,128]{2,1,0:T(8,128)(2,1)S(1)}, u32[]{:S(2)}, u32[]{:S(2)}) collective-permute-start(bf16[128,16,128]{2,1,0:T(8,128)(2,1)S(1)} %shard_map.54.refs_0_), channel_id=1, source_target_pairs={{6,0},{25,1},{0,2},{27,3},{2,4},{29,5},{4,6},{31,7},{14,8},{1,9},{... | collective-permute-start | bytes 1572872 | tf_op jit(solution)/shard_map/ppermute | solution.py:31
  128.9 9.9 %collective-permute-start.30 = (bf16[128,16,128]{2,1,0:T(8,128)(2,1)S(1)}, bf16[128,16,128]{2,1,0:T(8,128)(2,1)S(1)}, u32[]{:S(2)}, u32[]{:S(2)}) collective-permute-start(bf16[128,16,128]{2,1,0:T(8,128)(2,1)S(1)} %shard_map.54.refs_0_), channel_id=1, source_target_pairs={{2,0},{9,1},{4,2},{11,3},{6,4},{13,5},{0,6},{15,7},{10,8},{17,9},{... | collective-permute-start | bytes 1572872 | tf_op jit(solution)/shard_map/ppermute | solution.py:31
  135.1 10.5 %collective-permute-start.18 = (bf16[128,16,128]{2,1,0:T(8,128)(2,1)S(1)}, bf16[128,16,128]{2,1,0:T(8,128)(2,1)S(1)}, u32[]{:S(2)}, u32[]{:S(2)}) collective-permute-start(bf16[128,16,128]{2,1,0:T(8,128)(2,1)S(1)} %shard_map.50.refs_0_), channel_id=1, source_target_pairs={{6,0},{25,1},{0,2},{27,3},{2,4},{29,5},{4,6},{31,7},{14,8},{1,9},{... | collective-permute-start | bytes 1572872 | tf_op jit(solution)/shard_map/ppermute | solution.py:31
  135.6 10.0 %collective-permute-start.16 = (bf16[128,16,128]{2,1,0:T(8,128)(2,1)S(1)}, bf16[128,16,128]{2,1,0:T(8,128)(2,1)S(1)}, u32[]{:S(2)}, u32[]{:S(2)}) collective-permute-start(bf16[128,16,128]{2,1,0:T(8,128)(2,1)S(1)} %shard_map.50.refs_0_), channel_id=1, source_target_pairs={{2,0},{9,1},{4,2},{11,3},{6,4},{13,5},{0,6},{15,7},{10,8},{17,9},{... | collective-permute-start | bytes 1572872 | tf_op jit(solution)/shard_map/ppermute | solution.py:31
  138.7 10.3 %collective-permute-start.33 = (bf16[64,16,128]{2,1,0:T(8,128)(2,1)S(1)}, bf16[64,16,128]{2,1,0:T(8,128)(2,1)S(1)}, u32[]{:S(2)}, u32[]{:S(2)}) collective-permute-start(bf16[64,16,128]{2,1,0:T(8,128)(2,1)S(1)} %slice.81), channel_id=1, source_target_pairs={{6,0},{25,1},{0,2},{27,3},{2,4},{29,5},{4,6},{31,7},{14,8},{1,9},{... | collective-permute-start | bytes 786440 | tf_op jit(solution)/shard_map/ppermute | solution.py:31
  138.8 10.2 %collective-permute-start.31 = (bf16[64,16,128]{2,1,0:T(8,128)(2,1)S(1)}, bf16[64,16,128]{2,1,0:T(8,128)(2,1)S(1)}, u32[]{:S(2)}, u32[]{:S(2)}) collective-permute-start(bf16[64,16,128]{2,1,0:T(8,128)(2,1)S(1)} %slice.80), channel_id=1, source_target_pairs={{2,0},{9,1},{4,2},{11,3},{6,4},{13,5},{0,6},{15,7},{10,8},{17,9},{... | collective-permute-start | bytes 786440 | tf_op jit(solution)/shard_map/ppermute | solution.py:31
  145.5 7.7 %collective-permute-start.19 = (bf16[64,16,128]{2,1,0:T(8,128)(2,1)S(1)}, bf16[64,16,128]{2,1,0:T(8,128)(2,1)S(1)}, u32[]{:S(2)}, u32[]{:S(2)}) collective-permute-start(bf16[64,16,128]{2,1,0:T(8,128)(2,1)S(1)} %slice.77), channel_id=1, source_target_pairs={{6,0},{25,1},{0,2},{27,3},{2,4},{29,5},{4,6},{31,7},{14,8},{1,9},{... | collective-permute-start | bytes 786440 | tf_op jit(solution)/shard_map/ppermute | solution.py:31
  145.7 7.6 %collective-permute-start.17 = (bf16[64,16,128]{2,1,0:T(8,128)(2,1)S(1)}, bf16[64,16,128]{2,1,0:T(8,128)(2,1)S(1)}, u32[]{:S(2)}, u32[]{:S(2)}) collective-permute-start(bf16[64,16,128]{2,1,0:T(8,128)(2,1)S(1)} %slice.76), channel_id=1, source_target_pairs={{2,0},{9,1},{4,2},{11,3},{6,4},{13,5},{0,6},{15,7},{10,8},{17,9},{... | collective-permute-start | bytes 786440 | tf_op jit(solution)/shard_map/ppermute | solution.py:31
  (9 other events, 81.0 us)
Sparse Core Ops, SparseCore 0:
  9.2 62.3 all-gather.1

commit v3 on v2

--- a/solution.py
+++ b/solution.py
@@ -31,23 +31,29 @@
     return lax.ppermute(value, ("x", "y", "c"), pairs)
 
 
-def pack_kernel(*refs):
-    for i, source in enumerate(refs[:-1]):
+def pack_kernel(parts, *refs):
+    for i, source in enumerate(refs[:parts]):
         size = source.shape[0]
-        refs[-1][pl.ds(i * size, size)] = source[...]
-
-
-def pack(parts):
+        for j, out_ref in enumerate(refs[parts:]):
+            share = out_ref.shape[1]
+            out_ref[pl.ds(i * size, size)] = source[:, j * share : (j + 1) * share]
+
+
+def pack(parts, ends):
     size, genes, width = parts[0].shape
+    shape = jax.ShapeDtypeStruct((len(parts) * size, genes // ends, width), parts[0].dtype)
     return pl.pallas_call(
-        pack_kernel,
-        out_shape=jax.ShapeDtypeStruct((len(parts) * size, genes, width), parts[0].dtype),
+        functools.partial(pack_kernel, len(parts)),
+        out_shape=[shape] * ends,
         compiler_params=pltpu.CompilerParams(vmem_limit_bytes=16 * 1024 * 1024),
     )(*parts)
 
 
-def spread(value, ring):
-    value = pack([value] + [shift(value, d, 0) for d in (1, 2, 3)])
+def line(value, ends):
+    return pack([value] + [shift(value, d, 0) for d in (1, 2, 3)], ends)
+
+
+def plane(value, ring):
     if not ring:
         return [value] + [shift(value, d, 1) for d in (1, 2, 3)]
     half = value.shape[0] // 2
@@ -61,26 +67,19 @@
     if raw:
         inverse_ref, refs = refs[0], refs[1:]
     aff_ref, out_refs, refs = refs[0], refs[1 : 1 + ends], refs[1 + ends :]
-    peak_ref, own_peak_ref, held, kept, sems = refs
+    peak_ref, refs = refs[0], refs[1:]
+    if raw:
+        own_peak_ref, refs = refs[0], refs[1:]
+    held, sems = refs
     blocks, slots = aff_ref.shape[:2]
     genes = held.shape[1]
-    parts = 4
-    size = blocks // parts
-
-    def part(i):
-        rows = pl.ds(i * size, size)
-        return pltpu.make_async_copy(aff_ref.at[rows], kept.at[rows], sems.at[pieces + i])
-
     copies, start = [], 0
     for i, source in enumerate(sources):
         rows = source.shape[0]
         copies.append(pltpu.make_async_copy(source, held.at[pl.ds(start, rows)], sems.at[i]))
         start += rows
-    part(0).start()
     for copy in copies:
         copy.start()
-    for i in range(1, parts):
-        part(i).start()
     for copy in copies:
         copy.wait()
 
@@ -91,7 +90,7 @@
             tile = tile.astype(jnp.bfloat16)
         return tile
 
-    def one(row, peak, own_peak):
+    def one(row, peaks):
         count = count_ref[row]
         tiles = []
         for s in range(slots):
@@ -103,26 +102,26 @@
                 tile = jnp.where(s < count, tile, jnp.zeros_like(tile))
             tiles.append(tile)
         left = jnp.concatenate(tiles, axis=1)
-        right = kept[row].reshape(slots * BS, BS)
+        right = aff_ref[row].reshape(slots * BS, BS)
         total = jnp.dot(left, right, preferred_element_type=jnp.float32)
         mixed = 0.5 * own + total[:genes] * (0.5 / total[genes : genes + 1])
         for out_ref in out_refs:
             share = out_ref.shape[1]
             out_ref[row] = mixed[:share].astype(out_ref.dtype)
             mixed = jnp.concatenate([mixed[share:], mixed[:share]]) if ends > 1 else mixed
-        return jnp.maximum(peak, mixed), jnp.maximum(own_peak, own)
+        found = (mixed, own) if raw else (mixed,)
+        return tuple(jnp.maximum(a, b) for a, b in zip(peaks, found))
 
     def several(i, carry):
         for j in range(UNROLL):
-            carry = one(i * UNROLL + j, *carry)
+            carry = one(i * UNROLL + j, carry)
         return carry
 
-    carry = (jnp.zeros((genes, BS), jnp.float32),) * 2
-    for i in range(parts):
-        part(i).wait()
-        each = size // UNROLL
-        carry = lax.fori_loop(i * each, (i + 1) * each, several, carry)
-    peak_ref[...], own_peak_ref[...] = carry
+    carry = (jnp.zeros((genes, BS), jnp.float32),) * (1 + raw)
+    carry = lax.fori_loop(0, blocks // UNROLL, several, carry)
+    peak_ref[...] = carry[0]
+    if raw:
+        own_peak_ref[...] = carry[1]
 
 
 def diffuse(pieces, places, counts, tables, inverse, affinity, ends):
@@ -138,15 +137,14 @@
         in_specs=[smem] * 3
         + [pl.BlockSpec(memory_space=pl.ANY)] * n
         + [vmem] * raw
-        + [pl.BlockSpec(memory_space=pl.ANY)],
-        out_specs=[vmem] * (ends + 2),
+        + [vmem],
+        out_specs=[vmem] * (ends + 1 + raw),
         scratch_shapes=[
             pltpu.VMEM((total, genes, BS), pieces[0].dtype),
-            pltpu.VMEM(affinity.shape, affinity.dtype),
-            pltpu.SemaphoreType.DMA((n + 4,)),
+            pltpu.SemaphoreType.DMA((n,)),
         ],
         out_shape=[jax.ShapeDtypeStruct((blocks, genes // ends, BS), jnp.bfloat16)] * ends
-        + [jax.ShapeDtypeStruct((genes, BS), jnp.float32)] * 2,
+        + [jax.ShapeDtypeStruct((genes, BS), jnp.float32)] * (1 + raw),
         compiler_params=pltpu.CompilerParams(vmem_limit_bytes=32 * 1024 * 1024),
         cost_estimate=pl.CostEstimate(
             flops=2 * affinity.size * genes,
@@ -194,13 +192,17 @@
     places = ((second * SIDE + first) * blocks + within).reshape(-1)
     tables = ((device % (SIDE * SIDE)) * blocks + within).reshape(-1)
 
-    *streams, peak, own_peak = diffuse(
-        spread(counted, False), places, counts, tables, inverse, affinity, STREAMS
+    current, peak, own_peak = diffuse(
+        plane(*line(counted, 1), False), places, counts, tables, inverse, affinity, 1
     )
     peaks = [own_peak, peak]
+    lines = line(current, STREAMS)
     for step in range(1, STEPS):
-        pieces = [spread(stream, True) for stream in streams]
-        ends = [diffuse(piece, places, counts, tables, None, affinity, 1) for piece in pieces]
+        if step > 1:
+            lines = [line(stream, 1)[0] for stream in streams]
+        ends = [
+            diffuse(plane(part, True), places, counts, tables, None, affinity, 1) for part in lines
+        ]
         streams = [end[0] for end in ends]
         peaks.append(jnp.concatenate([end[1] for end in ends]))
     current = jnp.concatenate(streams, axis=1)

time: 198 us -> 196 us (0.990)
  waiting for transfers between devices: 38.5 us -> 47.8 us
  starting transfers between devices: 75 us -> 69 us
  Pallas kernels: 22.3 us -> 17.6 us
    ppermute x34 -> x31, waiting for transfers between devices: 13.7 us -> 23 us  [shift(): return lax.ppermute(value, ('x', 'y', 'c'), pairs)]
    ppermute x34 -> x31, starting transfers between devices: 53.2 us -> 47.2 us  [shift(): return lax.ppermute(value, ('x', 'y', 'c'), pairs)]
    pallas_call x5, Pallas kernels: 22.1 us -> 17.4 us  [diffuse(): pl.pallas_call(functools.partial(step_kernel, n, raw, ends), in_specs=[sm...]
  transfers between devices with their start and end apart: 38 -> 35, of which waited for: 11 -> 13; matrix products, arithmetic and copies ran while one was open for 3% -> 3% of each run, Pallas kernels for 7% -> 5%
where the time goes in v3:
time: 196 us
  starting transfers between devices  69 us (35%)
  waiting for transfers between devices  47.8 us (24%)
  blocking collectives  34.5 us (18%)
  Pallas kernels  17.6 us (9%)
  between operations  13.7 us (7%)
  local copies, waits for them, and re-layouts  11.6 us (6%)
    ppermute x31, starting transfers between devices, shift(): return lax.ppermute(value, ('x', 'y', 'c'), pairs)  47.2 us
    ppermute x31, waiting for transfers between devices, shift(): return lax.ppermute(value, ('x', 'y', 'c'), pairs)  23 us
    all_to_all x2, waiting for transfers between devices, to_all(): lax.all_to_all(jnp.broadcast_to(value[None], (size,) + value.shape), axis...  19.5 us
    all_to_all x1, blocking collectives, local(): result = lax.all_to_all(result, 'z', 0, 0, tiled=True)  17.5 us
    pallas_call x5, Pallas kernels, diffuse(): pl.pallas_call(functools.partial(step_kernel, n, raw, ends), in_specs=[sm...  17.4 us
    all_to_all x2, starting transfers between devices, to_all(): lax.all_to_all(jnp.broadcast_to(value[None], (size,) + value.shape), axis...  14.3 us
    all_to_all x1, blocking collectives, to_all(): lax.all_to_all(jnp.broadcast_to(value[None], (size,) + value.shape), axis...  13.6 us
    all_to_all x1, starting transfers between devices, local(): counted = lax.all_to_all(counted, XY, 2, 0, tiled=True)  7.48 us
  transfers between devices with their start and end apart: 35, of which 13 were waited for; matrix products, arithmetic and copies ran while one was open for 3% of the time, Pallas kernels for 5%

profile of v3, /device:TPU:2, one launch (start us, length us, event | category | flops | bytes accessed | tf_op | source)
XLA Modules:
  0.0 195.5 jit_solution(16400641964144508435)
XLA Ops:
  10.5 7.5 %all-to-all-start = ((bf16[2,8,16,512]{3,1,0,2:T(8,128)(2,1)}), bf16[2,8,16,512]{3,1,0,2:T(8,128)(2,1)S(1)}, u32[]{:S(2)}, u32[]{:S(2)}) async-start(bf16[2,8,16,512]{3,1,0,2:T(8,128)(2,1)} %copy.23), calls=%async_computation | async-start | bytes 524288 | tf_op jit(solution)/shard_map/all_to_all | solution.py:173
  19.5 5.2 %all-to-all-done = bf16[2,8,16,512]{3,1,0,2:T(8,128)(2,1)S(1)} async-done(((bf16[2,8,16,512]{3,1,0,2:T(8,128)(2,1)}), bf16[2,8,16,512]{3,1,0,2:T(8,128)(2,1)S(1)}, u32[]{:S(2)}, u32[]{:S(2)}) %all-to-all-start) | async-done | bytes 262176 | tf_op jit(solution)/shard_map/all_to_all | solution.py:173
  26.2 2.8 %collective-permute-start.1 = (bf16[32,32,128]{2,1,0:T(8,128)(2,1)S(1)}, bf16[32,32,128]{2,1,0:T(8,128)(2,1)S(1)}, u32[]{:S(2)}, u32[]{:S(2)}) collective-permute-start(bf16[32,32,128]{2,1,0:T(8,128)(2,1)S(1)} %bitcast.37), channel_id=1, source_target_pairs={{16,0},{5,1},{18,2},{7,3},{20,4},{1,5},{22,6},{3,7},{24,8},{13,9},... | collective-permute-start | bytes 786440 | tf_op jit(solution)/shard_map/ppermute | solution.py:31
  29.5 3.4 %psum.7 = f32[32,128]{1,0:T(8,128)S(1)} all-reduce(f32[32,128]{1,0:T(8,128)S(1)} %convert_reduce_fusion), channel_id=1, replica_groups=mesh['z'=8,'x'=4,'y'=4,'c'=2] {'c'}, use_global_device_ids=true, to_apply=%region_1.2 | all-reduce | flops 4096 | bytes 32768 | tf_op jit(solution)/shard_map/psum | solution.py:180
  33.6 8.5 %all-to-all-start.1 = ((f32[8,40,128]{2,1,0:T(8,128)}), f32[8,40,128]{2,1,0:T(8,128)S(1)}, u32[]{:S(2)}, u32[]{:S(2)}) async-start(f32[8,40,128]{2,1,0:T(8,128)} %broadcast_in_dim.11), calls=%async_computation.1 | async-start | bytes 327680 | tf_op jit(solution)/shard_map/all_to_all | solution.py:158
  46.3 8.1 %all-to-all-done.1 = f32[8,40,128]{2,1,0:T(8,128)S(1)} async-done(((f32[8,40,128]{2,1,0:T(8,128)}), f32[8,40,128]{2,1,0:T(8,128)S(1)}, u32[]{:S(2)}, u32[]{:S(2)}) %all-to-all-start.1) | async-done | bytes 163872 | tf_op jit(solution)/shard_map/all_to_all | solution.py:158
  55.3 5.9 %all-to-all-start.2 = ((f32[16,32,128]{2,1,0:T(8,128)}), f32[16,32,128]{2,1,0:T(8,128)S(1)}, u32[]{:S(2)}, u32[]{:S(2)}) async-start(f32[16,32,128]{2,1,0:T(8,128)} %broadcast_in_dim.12), calls=%async_computation.2 | async-start | bytes 524288 | tf_op jit(solution)/shard_map/all_to_all | solution.py:158
  61.6 11.4 %all-to-all-done.2 = f32[16,32,128]{2,1,0:T(8,128)S(1)} async-done(((f32[16,32,128]{2,1,0:T(8,128)}), f32[16,32,128]{2,1,0:T(8,128)S(1)}, u32[]{:S(2)}, u32[]{:S(2)}) %all-to-all-start.2) | async-done | bytes 262176 | tf_op jit(solution)/shard_map/all_to_all | solution.py:158
  73.1 3.4 %copy-done.1 = bf16[32,8,128,128]{3,2,1,0:T(8,128)(2,1)S(1)} copy-done((bf16[32,8,128,128]{3,2,1,0:T(8,128)(2,1)S(1)}, bf16[32,8,128,128]{3,2,1,0:T(8,128)(2,1)}, u32[]{:S(2)}) %copy-start.1) | copy-done | bytes 8388632
  76.4 4.9 %shard_map.47 = (bf16[32,32,128]{2,1,0:T(8,128)(2,1)S(1)}, f32[32,128]{1,0:T(8,128)S(1)}, f32[32,128]{1,0:T(8,128)S(1)}) custom-call(s32[256]{0:T(256)S(1)} %reshape.66.place_ref, s32[32]{0:T(128)S(1)} %slice_reduce_fusion.1.count_ref, s32[256]{0:T(256)S(1)} %reshape.67.table_ref, bf16[128,32,128]{2,1,0:T(8,128)(2,1)S(1)} %shard_map.46.refs_0_, ...), custom_call_target="tpu_custom_call" | custom-call | flops 268435456 | bytes 8388608 | tf_op jit(solution)/shard_map/pallas_call | solution.py:135
  85.2 2.6 %collective-permute-done.8.refs_3_ = bf16[32,32,128]{2,1,0:T(8,128)(2,1)S(1)} collective-permute-done((bf16[32,32,128]{2,1,0:T(8,128)(2,1)S(1)}, bf16[32,32,128]{2,1,0:T(8,128)(2,1)S(1)}, u32[]{:S(2)}, u32[]{:S(2)}) %collective-permute-start.8) | collective-permute-done | bytes 262176 | tf_op jit(solution)/shard_map/ppermute | solution.py:31
  87.8 3.2 %collective-permute-done.7.refs_2_ = bf16[32,32,128]{2,1,0:T(8,128)(2,1)S(1)} collective-permute-done((bf16[32,32,128]{2,1,0:T(8,128)(2,1)S(1)}, bf16[32,32,128]{2,1,0:T(8,128)(2,1)S(1)}, u32[]{:S(2)}, u32[]{:S(2)}) %collective-permute-start.7) | collective-permute-done | bytes 262176 | tf_op jit(solution)/shard_map/ppermute | solution.py:31
  91.0 2.7 %collective-permute-done.6.refs_1_ = bf16[32,32,128]{2,1,0:T(8,128)(2,1)S(1)} collective-permute-done((bf16[32,32,128]{2,1,0:T(8,128)(2,1)S(1)}, bf16[32,32,128]{2,1,0:T(8,128)(2,1)S(1)}, u32[]{:S(2)}, u32[]{:S(2)}) %collective-permute-start.6) | collective-permute-done | bytes 262176 | tf_op jit(solution)/shard_map/ppermute | solution.py:31
  94.9 2.2 %collective-permute-start.9 = (bf16[128,16,128]{2,1,0:T(8,128)(2,1)S(1)}, bf16[128,16,128]{2,1,0:T(8,128)(2,1)S(1)}, u32[]{:S(2)}, u32[]{:S(2)}) collective-permute-start(bf16[128,16,128]{2,1,0:T(8,128)(2,1)S(1)} %get-tuple-element.19.refs_0_), channel_id=1, source_target_pairs={{2,0},{9,1},{4,2},{11,3},{6,4},{13,5},{0,6},{15,7},{10,8},{17,9},{... | collective-permute-start | bytes 1572872 | tf_op jit(solution)/shard_map/ppermute | solution.py:31
  97.1 3.2 %collective-permute-start.20 = (bf16[128,16,128]{2,1,0:T(8,128)(2,1)S(1)}, bf16[128,16,128]{2,1,0:T(8,128)(2,1)S(1)}, u32[]{:S(2)}, u32[]{:S(2)}) collective-permute-start(bf16[128,16,128]{2,1,0:T(8,128)(2,1)S(1)} %get-tuple-element.22.refs_0_), channel_id=1, source_target_pairs={{2,0},{9,1},{4,2},{11,3},{6,4},{13,5},{0,6},{15,7},{10,8},{17,9},{... | collective-permute-start | bytes 1572872 | tf_op jit(solution)/shard_map/ppermute | solution.py:31
  100.4 3.9 %collective-permute-done.11.refs_4_ = bf16[128,16,128]{2,1,0:T(8,128)(2,1)S(1)} collective-permute-done((bf16[128,16,128]{2,1,0:T(8,128)(2,1)S(1)}, bf16[128,16,128]{2,1,0:T(8,128)(2,1)S(1)}, u32[]{:S(2)}, u32[]{:S(2)}) %collective-permute-start.11) | collective-permute-done | bytes 524320 | tf_op jit(solution)/shard_map/ppermute | solution.py:31
  104.6 3.3 %collective-permute-start.10 = (bf16[64,16,128]{2,1,0:T(8,128)(2,1)S(1)}, bf16[64,16,128]{2,1,0:T(8,128)(2,1)S(1)}, u32[]{:S(2)}, u32[]{:S(2)}) collective-permute-start(bf16[64,16,128]{2,1,0:T(8,128)(2,1)S(1)} %slice.74), channel_id=1, source_target_pairs={{2,0},{9,1},{4,2},{11,3},{6,4},{13,5},{0,6},{15,7},{10,8},{17,9},{... | collective-permute-start | bytes 786440 | tf_op jit(solution)/shard_map/ppermute | solution.py:31
  110.1 3.3 %collective-permute-start.21 = (bf16[64,16,128]{2,1,0:T(8,128)(2,1)S(1)}, bf16[64,16,128]{2,1,0:T(8,128)(2,1)S(1)}, u32[]{:S(2)}, u32[]{:S(2)}) collective-permute-start(bf16[64,16,128]{2,1,0:T(8,128)(2,1)S(1)} %slice.78), channel_id=1, source_target_pairs={{2,0},{9,1},{4,2},{11,3},{6,4},{13,5},{0,6},{15,7},{10,8},{17,9},{... | collective-permute-start | bytes 786440 | tf_op jit(solution)/shard_map/ppermute | solution.py:31
  113.4 3.1 %shard_map.49 = (bf16[32,16,128]{2,1,0:T(8,128)(2,1)S(1)}, f32[16,128]{1,0:T(8,128)S(1)}) custom-call(s32[256]{0:T(256)S(1)} %reshape.66.place_ref, s32[32]{0:T(128)S(1)} %slice_reduce_fusion.1.count_ref, s32[256]{0:T(256)S(1)} %reshape.67.table_ref, bf16[128,16,128]{2,1,0:T(8,128)(2,1)S(1)} %get-tuple-element.19.refs_0_, ...), custom_call_target="tpu_custom_call" | custom-call | flops 134217728 | bytes 8388608 | tf_op jit(solution)/shard_map/pallas_call | solution.py:135
  119.0 2.1 %collective-permute-start.13 = (bf16[32,16,128]{2,1,0:T(8,128)(2,1)S(1)}, bf16[32,16,128]{2,1,0:T(8,128)(2,1)S(1)}, u32[]{:S(2)}, u32[]{:S(2)}) collective-permute-start(bf16[32,16,128]{2,1,0:T(8,128)(2,1)S(1)} %get-tuple-element.20.refs_0_), channel_id=1, source_target_pairs={{8,0},{3,1},{10,2},{5,3},{12,4},{7,5},{14,6},{1,7},{16,8},{11,9},{... | collective-permute-start | bytes 393224 | tf_op jit(solution)/shard_map/ppermute | solution.py:31
  121.1 3.1 %shard_map.52 = (bf16[32,16,128]{2,1,0:T(8,128)(2,1)S(1)}, f32[16,128]{1,0:T(8,128)S(1)}) custom-call(s32[256]{0:T(256)S(1)} %reshape.66.place_ref, s32[32]{0:T(128)S(1)} %slice_reduce_fusion.1.count_ref, s32[256]{0:T(256)S(1)} %reshape.67.table_ref, bf16[128,16,128]{2,1,0:T(8,128)(2,1)S(1)} %get-tuple-element.22.refs_0_, ...), custom_call_target="tpu_custom_call" | custom-call | flops 134217728 | bytes 8388608 | tf_op jit(solution)/shard_map/pallas_call | solution.py:135
  124.3 2.8 %collective-permute-start.25 = (bf16[32,16,128]{2,1,0:T(8,128)(2,1)S(1)}, bf16[32,16,128]{2,1,0:T(8,128)(2,1)S(1)}, u32[]{:S(2)}, u32[]{:S(2)}) collective-permute-start(bf16[32,16,128]{2,1,0:T(8,128)(2,1)S(1)} %get-tuple-element.23.refs_0_), channel_id=1, source_target_pairs={{16,0},{5,1},{18,2},{7,3},{20,4},{1,5},{22,6},{3,7},{24,8},{13,9},... | collective-permute-start | bytes 393224 | tf_op jit(solution)/shard_map/ppermute | solution.py:31
  127.9 2.8 %collective-permute-start.16 = (bf16[128,16,128]{2,1,0:T(8,128)(2,1)S(1)}, bf16[128,16,128]{2,1,0:T(8,128)(2,1)S(1)}, u32[]{:S(2)}, u32[]{:S(2)}) collective-permute-start(bf16[128,16,128]{2,1,0:T(8,128)(2,1)S(1)} %shard_map.50.refs_0_), channel_id=1, source_target_pairs={{2,0},{9,1},{4,2},{11,3},{6,4},{13,5},{0,6},{15,7},{10,8},{17,9},{... | collective-permute-start | bytes 1572872 | tf_op jit(solution)/shard_map/ppermute | solution.py:31
  132.3 2.1 %collective-permute-done.24.refs_1_ = bf16[32,16,128]{2,1,0:T(8,128)(2,1)S(1)} collective-permute-done((bf16[32,16,128]{2,1,0:T(8,128)(2,1)S(1)}, bf16[32,16,128]{2,1,0:T(8,128)(2,1)S(1)}, u32[]{:S(2)}, u32[]{:S(2)}) %collective-permute-start.24) | collective-permute-done | bytes 131104 | tf_op jit(solution)/shard_map/ppermute | solution.py:31
  134.9 2.8 %collective-permute-start.27 = (bf16[128,16,128]{2,1,0:T(8,128)(2,1)S(1)}, bf16[128,16,128]{2,1,0:T(8,128)(2,1)S(1)}, u32[]{:S(2)}, u32[]{:S(2)}) collective-permute-start(bf16[128,16,128]{2,1,0:T(8,128)(2,1)S(1)} %shard_map.53.refs_0_), channel_id=1, source_target_pairs={{2,0},{9,1},{4,2},{11,3},{6,4},{13,5},{0,6},{15,7},{10,8},{17,9},{... | collective-permute-start | bytes 1572872 | tf_op jit(solution)/shard_map/ppermute | solution.py:31
  138.0 3.3 %collective-permute-start.17 = (bf16[64,16,128]{2,1,0:T(8,128)(2,1)S(1)}, bf16[64,16,128]{2,1,0:T(8,128)(2,1)S(1)}, u32[]{:S(2)}, u32[]{:S(2)}) collective-permute-start(bf16[64,16,128]{2,1,0:T(8,128)(2,1)S(1)} %slice.76), channel_id=1, source_target_pairs={{2,0},{9,1},{4,2},{11,3},{6,4},{13,5},{0,6},{15,7},{10,8},{17,9},{... | collective-permute-start | bytes 786440 | tf_op jit(solution)/shard_map/ppermute | solution.py:31
  141.3 3.6 %collective-permute-done.29.refs_4_ = bf16[128,16,128]{2,1,0:T(8,128)(2,1)S(1)} collective-permute-done((bf16[128,16,128]{2,1,0:T(8,128)(2,1)S(1)}, bf16[128,16,128]{2,1,0:T(8,128)(2,1)S(1)}, u32[]{:S(2)}, u32[]{:S(2)}) %collective-permute-start.29) | collective-permute-done | bytes 524320 | tf_op jit(solution)/shard_map/ppermute | solution.py:31
  145.2 3.3 %collective-permute-start.28 = (bf16[64,16,128]{2,1,0:T(8,128)(2,1)S(1)}, bf16[64,16,128]{2,1,0:T(8,128)(2,1)S(1)}, u32[]{:S(2)}, u32[]{:S(2)}) collective-permute-start(bf16[64,16,128]{2,1,0:T(8,128)(2,1)S(1)} %slice.80), channel_id=1, source_target_pairs={{2,0},{9,1},{4,2},{11,3},{6,4},{13,5},{0,6},{15,7},{10,8},{17,9},{... | collective-permute-start | bytes 786440 | tf_op jit(solution)/shard_map/ppermute | solution.py:31
  148.5 3.1 %shard_map.51 = (bf16[32,16,128]{2,1,0:T(8,128)(2,1)S(1)}, f32[16,128]{1,0:T(8,128)S(1)}) custom-call(s32[256]{0:T(256)S(1)} %reshape.66.place_ref, s32[32]{0:T(128)S(1)} %slice_reduce_fusion.1.count_ref, s32[256]{0:T(256)S(1)} %reshape.67.table_ref, bf16[128,16,128]{2,1,0:T(8,128)(2,1)S(1)} %shard_map.50.refs_0_, ...), custom_call_target="tpu_custom_call" | custom-call | flops 134217728 | bytes 8388608 | tf_op jit(solution)/shard_map/pallas_call | solution.py:135
  152.8 3.1 %shard_map.54 = (bf16[32,16,128]{2,1,0:T(8,128)(2,1)S(1)}, f32[16,128]{1,0:T(8,128)S(1)}) custom-call(s32[256]{0:T(256)S(1)} %reshape.66.place_ref, s32[32]{0:T(128)S(1)} %slice_reduce_fusion.1.count_ref, s32[256]{0:T(256)S(1)} %reshape.67.table_ref, bf16[128,16,128]{2,1,0:T(8,128)(2,1)S(1)} %shard_map.53.refs_0_, ...), custom_call_target="tpu_custom_call" | custom-call | flops 134217728 | bytes 8388608 | tf_op jit(solution)/shard_map/pallas_call | solution.py:135
  156.1 13.6 %all_to_all.36 = f32[16,1,128]{2,1,0:T(1,128)S(1)} all-to-all(f32[16,1,128]{2,1,0:T(1,128)S(1)} %broadcast_in_dim.27), channel_id=1, replica_groups=mesh['z'=8,'x'=4,'y'=4,'c'=2] {'x','y'}, dimensions={0} | all-to-all | bytes 16384 | tf_op jit(solution)/shard_map/all_to_all | solution.py:158
  170.0 17.5 %all_to_all.37 = bf16[32,32,128]{2,1,0:T(8,128)(2,1)S(1)} all-to-all(bf16[32,32,128]{2,1,0:T(8,128)(2,1)S(1)} %multiply_convert_fusion), channel_id=1, replica_groups=mesh['z'=8,'x'=4,'y'=4,'c'=2] {'z'}, dimensions={0} | all-to-all | bytes 524288 | tf_op jit(solution)/shard_map/all_to_all | solution.py:215
  (97 shorter events, 29.9 us)
Async XLA Ops:
  6.5 66.5 %all-gather.2.cloned.1.call-start = ((), (), s32[]{:S(2)}) async-start(), calls=%async_computation.5 | async-start | bytes 8912896 | tf_op jit(solution)/shard_map/all_gather | solution.py:167
  10.5 14.3 %all-to-all-start = ((bf16[2,8,16,512]{3,1,0,2:T(8,128)(2,1)}), bf16[2,8,16,512]{3,1,0,2:T(8,128)(2,1)S(1)}, u32[]{:S(2)}, u32[]{:S(2)}) async-start(bf16[2,8,16,512]{3,1,0,2:T(8,128)(2,1)} %copy.23), calls=%async_computation | async-start | bytes 524288 | tf_op jit(solution)/shard_map/all_to_all | solution.py:173
  25.0 17.0 %collective-permute-start.2 = (bf16[32,32,128]{2,1,0:T(8,128)(2,1)S(1)}, bf16[32,32,128]{2,1,0:T(8,128)(2,1)S(1)}, u32[]{:S(2)}, u32[]{:S(2)}) collective-permute-start(bf16[32,32,128]{2,1,0:T(8,128)(2,1)S(1)} %bitcast.36), channel_id=1, source_target_pairs={{24,0},{7,1},{26,2},{1,3},{28,4},{3,5},{30,6},{5,7},{0,8},{15,9},{... | collective-permute-start | bytes 786440 | tf_op jit(solution)/shard_map/ppermute | solution.py:31
  26.2 15.9 %collective-permute-start.1 = (bf16[32,32,128]{2,1,0:T(8,128)(2,1)S(1)}, bf16[32,32,128]{2,1,0:T(8,128)(2,1)S(1)}, u32[]{:S(2)}, u32[]{:S(2)}) collective-permute-start(bf16[32,32,128]{2,1,0:T(8,128)(2,1)S(1)} %bitcast.37), channel_id=1, source_target_pairs={{16,0},{5,1},{18,2},{7,3},{20,4},{1,5},{22,6},{3,7},{24,8},{13,9},... | collective-permute-start | bytes 786440 | tf_op jit(solution)/shard_map/ppermute | solution.py:31
  29.0 13.1 %collective-permute-start = (bf16[32,32,128]{2,1,0:T(8,128)(2,1)S(1)}, bf16[32,32,128]{2,1,0:T(8,128)(2,1)S(1)}, u32[]{:S(2)}, u32[]{:S(2)}) collective-permute-start(bf16[32,32,128]{2,1,0:T(8,128)(2,1)S(1)} %bitcast.38), channel_id=1, source_target_pairs={{8,0},{3,1},{10,2},{5,3},{12,4},{7,5},{14,6},{1,7},{16,8},{11,9},{... | collective-permute-start | bytes 786440 | tf_op jit(solution)/shard_map/ppermute | solution.py:31
  33.6 20.8 %all-to-all-start.1 = ((f32[8,40,128]{2,1,0:T(8,128)}), f32[8,40,128]{2,1,0:T(8,128)S(1)}, u32[]{:S(2)}, u32[]{:S(2)}) async-start(f32[8,40,128]{2,1,0:T(8,128)} %broadcast_in_dim.11), calls=%async_computation.1 | async-start | bytes 327680 | tf_op jit(solution)/shard_map/all_to_all | solution.py:158
  42.2 30.9 %collective-permute-start.5 = (bf16[128,32,128]{2,1,0:T(8,128)(2,1)S(1)}, bf16[128,32,128]{2,1,0:T(8,128)(2,1)S(1)}, u32[]{:S(2)}, u32[]{:S(2)}) collective-permute-start(bf16[128,32,128]{2,1,0:T(8,128)(2,1)S(1)} %shard_map.46.refs_0_), channel_id=1, source_target_pairs={{6,0},{25,1},{0,2},{27,3},{2,4},{29,5},{4,6},{31,7},{14,8},{1,9},{... | collective-permute-start | bytes 3145736 | tf_op jit(solution)/shard_map/ppermute | solution.py:31
  42.8 30.2 %collective-permute-start.4 = (bf16[128,32,128]{2,1,0:T(8,128)(2,1)S(1)}, bf16[128,32,128]{2,1,0:T(8,128)(2,1)}, u32[]{:S(2)}, u32[]{:S(2)}) collective-permute-start(bf16[128,32,128]{2,1,0:T(8,128)(2,1)S(1)} %shard_map.46.refs_0_), channel_id=1, source_target_pairs={{4,0},{17,1},{6,2},{19,3},{0,4},{21,5},{2,6},{23,7},{12,8},{25,9},... | collective-permute-start | bytes 3145736 | tf_op jit(solution)/shard_map/ppermute | solution.py:31
  44.6 28.4 %collective-permute-start.3 = (bf16[128,32,128]{2,1,0:T(8,128)(2,1)S(1)}, bf16[128,32,128]{2,1,0:T(8,128)(2,1)}, u32[]{:S(2)}, u32[]{:S(2)}) collective-permute-start(bf16[128,32,128]{2,1,0:T(8,128)(2,1)S(1)} %shard_map.46.refs_0_), channel_id=1, source_target_pairs={{2,0},{9,1},{4,2},{11,3},{6,4},{13,5},{0,6},{15,7},{10,8},{17,9},{... | collective-permute-start | bytes 3145736 | tf_op jit(solution)/shard_map/ppermute | solution.py:31
  55.3 17.7 %all-to-all-start.2 = ((f32[16,32,128]{2,1,0:T(8,128)}), f32[16,32,128]{2,1,0:T(8,128)S(1)}, u32[]{:S(2)}, u32[]{:S(2)}) async-start(f32[16,32,128]{2,1,0:T(8,128)} %broadcast_in_dim.12), calls=%async_computation.2 | async-start | bytes 524288 | tf_op jit(solution)/shard_map/all_to_all | solution.py:158
  83.1 8.0 %collective-permute-start.7 = (bf16[32,32,128]{2,1,0:T(8,128)(2,1)S(1)}, bf16[32,32,128]{2,1,0:T(8,128)(2,1)S(1)}, u32[]{:S(2)}, u32[]{:S(2)}) collective-permute-start(bf16[32,32,128]{2,1,0:T(8,128)(2,1)S(1)} %get-tuple-element.18.refs_0_), channel_id=1, source_target_pairs={{16,0},{5,1},{18,2},{7,3},{20,4},{1,5},{22,6},{3,7},{24,8},{13,9},... | collective-permute-start | bytes 786440 | tf_op jit(solution)/shard_map/ppermute | solution.py:31
  85.0 8.8 %collective-permute-start.6 = (bf16[32,32,128]{2,1,0:T(8,128)(2,1)S(1)}, bf16[32,32,128]{2,1,0:T(8,128)(2,1)S(1)}, u32[]{:S(2)}, u32[]{:S(2)}) collective-permute-start(bf16[32,32,128]{2,1,0:T(8,128)(2,1)S(1)} %get-tuple-element.18.refs_0_), channel_id=1, source_target_pairs={{8,0},{3,1},{10,2},{5,3},{12,4},{7,5},{14,6},{1,7},{16,8},{11,9},{... | collective-permute-start | bytes 786440 | tf_op jit(solution)/shard_map/ppermute | solution.py:31
  93.8 10.5 %collective-permute-start.11 = (bf16[128,16,128]{2,1,0:T(8,128)(2,1)S(1)}, bf16[128,16,128]{2,1,0:T(8,128)(2,1)S(1)}, u32[]{:S(2)}, u32[]{:S(2)}) collective-permute-start(bf16[128,16,128]{2,1,0:T(8,128)(2,1)S(1)} %get-tuple-element.19.refs_0_), channel_id=1, source_target_pairs={{6,0},{25,1},{0,2},{27,3},{2,4},{29,5},{4,6},{31,7},{14,8},{1,9},{... | collective-permute-start | bytes 1572872 | tf_op jit(solution)/shard_map/ppermute | solution.py:31
  94.9 9.7 %collective-permute-start.9 = (bf16[128,16,128]{2,1,0:T(8,128)(2,1)S(1)}, bf16[128,16,128]{2,1,0:T(8,128)(2,1)S(1)}, u32[]{:S(2)}, u32[]{:S(2)}) collective-permute-start(bf16[128,16,128]{2,1,0:T(8,128)(2,1)S(1)} %get-tuple-element.19.refs_0_), channel_id=1, source_target_pairs={{2,0},{9,1},{4,2},{11,3},{6,4},{13,5},{0,6},{15,7},{10,8},{17,9},{... | collective-permute-start | bytes 1572872 | tf_op jit(solution)/shard_map/ppermute | solution.py:31
  97.1 12.8 %collective-permute-start.22 = (bf16[128,16,128]{2,1,0:T(8,128)(2,1)S(1)}, bf16[128,16,128]{2,1,0:T(8,128)(2,1)S(1)}, u32[]{:S(2)}, u32[]{:S(2)}) collective-permute-start(bf16[128,16,128]{2,1,0:T(8,128)(2,1)S(1)} %get-tuple-element.22.refs_0_), channel_id=1, source_target_pairs={{6,0},{25,1},{0,2},{27,3},{2,4},{29,5},{4,6},{31,7},{14,8},{1,9},{... | collective-permute-start | bytes 1572872 | tf_op jit(solution)/shard_map/ppermute | solution.py:31
  97.1 12.9 %collective-permute-start.20 = (bf16[128,16,128]{2,1,0:T(8,128)(2,1)S(1)}, bf16[128,16,128]{2,1,0:T(8,128)(2,1)S(1)}, u32[]{:S(2)}, u32[]{:S(2)}) collective-permute-start(bf16[128,16,128]{2,1,0:T(8,128)(2,1)S(1)} %get-tuple-element.22.refs_0_), channel_id=1, source_target_pairs={{2,0},{9,1},{4,2},{11,3},{6,4},{13,5},{0,6},{15,7},{10,8},{17,9},{... | collective-permute-start | bytes 1572872 | tf_op jit(solution)/shard_map/ppermute | solution.py:31
  104.3 9.0 %collective-permute-start.12 = (bf16[64,16,128]{2,1,0:T(8,128)(2,1)S(1)}, bf16[64,16,128]{2,1,0:T(8,128)(2,1)S(1)}, u32[]{:S(2)}, u32[]{:S(2)}) collective-permute-start(bf16[64,16,128]{2,1,0:T(8,128)(2,1)S(1)} %slice.75), channel_id=1, source_target_pairs={{6,0},{25,1},{0,2},{27,3},{2,4},{29,5},{4,6},{31,7},{14,8},{1,9},{... | collective-permute-start | bytes 786440 | tf_op jit(solution)/shard_map/ppermute | solution.py:31
  104.6 8.7 %collective-permute-start.10 = (bf16[64,16,128]{2,1,0:T(8,128)(2,1)S(1)}, bf16[64,16,128]{2,1,0:T(8,128)(2,1)S(1)}, u32[]{:S(2)}, u32[]{:S(2)}) collective-permute-start(bf16[64,16,128]{2,1,0:T(8,128)(2,1)S(1)} %slice.74), channel_id=1, source_target_pairs={{2,0},{9,1},{4,2},{11,3},{6,4},{13,5},{0,6},{15,7},{10,8},{17,9},{... | collective-permute-start | bytes 786440 | tf_op jit(solution)/shard_map/ppermute | solution.py:31
  109.9 11.2 %collective-permute-start.23 = (bf16[64,16,128]{2,1,0:T(8,128)(2,1)S(1)}, bf16[64,16,128]{2,1,0:T(8,128)(2,1)S(1)}, u32[]{:S(2)}, u32[]{:S(2)}) collective-permute-start(bf16[64,16,128]{2,1,0:T(8,128)(2,1)S(1)} %slice.79), channel_id=1, source_target_pairs={{6,0},{25,1},{0,2},{27,3},{2,4},{29,5},{4,6},{31,7},{14,8},{1,9},{... | collective-permute-start | bytes 786440 | tf_op jit(solution)/shard_map/ppermute | solution.py:31
  110.1 11.0 %collective-permute-start.21 = (bf16[64,16,128]{2,1,0:T(8,128)(2,1)S(1)}, bf16[64,16,128]{2,1,0:T(8,128)(2,1)S(1)}, u32[]{:S(2)}, u32[]{:S(2)}) collective-permute-start(bf16[64,16,128]{2,1,0:T(8,128)(2,1)S(1)} %slice.78), channel_id=1, source_target_pairs={{2,0},{9,1},{4,2},{11,3},{6,4},{13,5},{0,6},{15,7},{10,8},{17,9},{... | collective-permute-start | bytes 786440 | tf_op jit(solution)/shard_map/ppermute | solution.py:31
  116.5 10.7 %collective-permute-start.15 = (bf16[32,16,128]{2,1,0:T(8,128)(2,1)S(1)}, bf16[32,16,128]{2,1,0:T(8,128)(2,1)S(1)}, u32[]{:S(2)}, u32[]{:S(2)}) collective-permute-start(bf16[32,16,128]{2,1,0:T(8,128)(2,1)S(1)} %get-tuple-element.20.refs_0_), channel_id=1, source_target_pairs={{24,0},{7,1},{26,2},{1,3},{28,4},{3,5},{30,6},{5,7},{0,8},{15,9},{... | collective-permute-start | bytes 393224 | tf_op jit(solution)/shard_map/ppermute | solution.py:31
  117.2 10.2 %collective-permute-start.14 = (bf16[32,16,128]{2,1,0:T(8,128)(2,1)S(1)}, bf16[32,16,128]{2,1,0:T(8,128)(2,1)S(1)}, u32[]{:S(2)}, u32[]{:S(2)}) collective-permute-start(bf16[32,16,128]{2,1,0:T(8,128)(2,1)S(1)} %get-tuple-element.20.refs_0_), channel_id=1, source_target_pairs={{16,0},{5,1},{18,2},{7,3},{20,4},{1,5},{22,6},{3,7},{24,8},{13,9},... | collective-permute-start | bytes 393224 | tf_op jit(solution)/shard_map/ppermute | solution.py:31
  119.0 8.3 %collective-permute-start.13 = (bf16[32,16,128]{2,1,0:T(8,128)(2,1)S(1)}, bf16[32,16,128]{2,1,0:T(8,128)(2,1)S(1)}, u32[]{:S(2)}, u32[]{:S(2)}) collective-permute-start(bf16[32,16,128]{2,1,0:T(8,128)(2,1)S(1)} %get-tuple-element.20.refs_0_), channel_id=1, source_target_pairs={{8,0},{3,1},{10,2},{5,3},{12,4},{7,5},{14,6},{1,7},{16,8},{11,9},{... | collective-permute-start | bytes 393224 | tf_op jit(solution)/shard_map/ppermute | solution.py:31
  124.3 7.9 %collective-permute-start.25 = (bf16[32,16,128]{2,1,0:T(8,128)(2,1)S(1)}, bf16[32,16,128]{2,1,0:T(8,128)(2,1)S(1)}, u32[]{:S(2)}, u32[]{:S(2)}) collective-permute-start(bf16[32,16,128]{2,1,0:T(8,128)(2,1)S(1)} %get-tuple-element.23.refs_0_), channel_id=1, source_target_pairs={{16,0},{5,1},{18,2},{7,3},{20,4},{1,5},{22,6},{3,7},{24,8},{13,9},... | collective-permute-start | bytes 393224 | tf_op jit(solution)/shard_map/ppermute | solution.py:31
  127.4 10.5 %collective-permute-start.18 = (bf16[128,16,128]{2,1,0:T(8,128)(2,1)S(1)}, bf16[128,16,128]{2,1,0:T(8,128)(2,1)S(1)}, u32[]{:S(2)}, u32[]{:S(2)}) collective-permute-start(bf16[128,16,128]{2,1,0:T(8,128)(2,1)S(1)} %shard_map.50.refs_0_), channel_id=1, source_target_pairs={{6,0},{25,1},{0,2},{27,3},{2,4},{29,5},{4,6},{31,7},{14,8},{1,9},{... | collective-permute-start | bytes 1572872 | tf_op jit(solution)/shard_map/ppermute | solution.py:31
  127.9 10.1 %collective-permute-start.16 = (bf16[128,16,128]{2,1,0:T(8,128)(2,1)S(1)}, bf16[128,16,128]{2,1,0:T(8,128)(2,1)S(1)}, u32[]{:S(2)}, u32[]{:S(2)}) collective-permute-start(bf16[128,16,128]{2,1,0:T(8,128)(2,1)S(1)} %shard_map.50.refs_0_), channel_id=1, source_target_pairs={{2,0},{9,1},{4,2},{11,3},{6,4},{13,5},{0,6},{15,7},{10,8},{17,9},{... | collective-permute-start | bytes 1572872 | tf_op jit(solution)/shard_map/ppermute | solution.py:31
  134.4 10.5 %collective-permute-start.29 = (bf16[128,16,128]{2,1,0:T(8,128)(2,1)S(1)}, bf16[128,16,128]{2,1,0:T(8,128)(2,1)S(1)}, u32[]{:S(2)}, u32[]{:S(2)}) collective-permute-start(bf16[128,16,128]{2,1,0:T(8,128)(2,1)S(1)} %shard_map.53.refs_0_), channel_id=1, source_target_pairs={{6,0},{25,1},{0,2},{27,3},{2,4},{29,5},{4,6},{31,7},{14,8},{1,9},{... | collective-permute-start | bytes 1572872 | tf_op jit(solution)/shard_map/ppermute | solution.py:31
  134.9 10.3 %collective-permute-start.27 = (bf16[128,16,128]{2,1,0:T(8,128)(2,1)S(1)}, bf16[128,16,128]{2,1,0:T(8,128)(2,1)S(1)}, u32[]{:S(2)}, u32[]{:S(2)}) collective-permute-start(bf16[128,16,128]{2,1,0:T(8,128)(2,1)S(1)} %shard_map.53.refs_0_), channel_id=1, source_target_pairs={{2,0},{9,1},{4,2},{11,3},{6,4},{13,5},{0,6},{15,7},{10,8},{17,9},{... | collective-permute-start | bytes 1572872 | tf_op jit(solution)/shard_map/ppermute | solution.py:31
  137.9 10.6 %collective-permute-start.19 = (bf16[64,16,128]{2,1,0:T(8,128)(2,1)S(1)}, bf16[64,16,128]{2,1,0:T(8,128)(2,1)S(1)}, u32[]{:S(2)}, u32[]{:S(2)}) collective-permute-start(bf16[64,16,128]{2,1,0:T(8,128)(2,1)S(1)} %slice.77), channel_id=1, source_target_pairs={{6,0},{25,1},{0,2},{27,3},{2,4},{29,5},{4,6},{31,7},{14,8},{1,9},{... | collective-permute-start | bytes 786440 | tf_op jit(solution)/shard_map/ppermute | solution.py:31
  138.0 10.5 %collective-permute-start.17 = (bf16[64,16,128]{2,1,0:T(8,128)(2,1)S(1)}, bf16[64,16,128]{2,1,0:T(8,128)(2,1)S(1)}, u32[]{:S(2)}, u32[]{:S(2)}) collective-permute-start(bf16[64,16,128]{2,1,0:T(8,128)(2,1)S(1)} %slice.76), channel_id=1, source_target_pairs={{2,0},{9,1},{4,2},{11,3},{6,4},{13,5},{0,6},{15,7},{10,8},{17,9},{... | collective-permute-start | bytes 786440 | tf_op jit(solution)/shard_map/ppermute | solution.py:31
  144.9 7.9 %collective-permute-start.30 = (bf16[64,16,128]{2,1,0:T(8,128)(2,1)S(1)}, bf16[64,16,128]{2,1,0:T(8,128)(2,1)S(1)}, u32[]{:S(2)}, u32[]{:S(2)}) collective-permute-start(bf16[64,16,128]{2,1,0:T(8,128)(2,1)S(1)} %slice.81), channel_id=1, source_target_pairs={{6,0},{25,1},{0,2},{27,3},{2,4},{29,5},{4,6},{31,7},{14,8},{1,9},{... | collective-permute-start | bytes 786440 | tf_op jit(solution)/shard_map/ppermute | solution.py:31
  145.2 7.5 %collective-permute-start.28 = (bf16[64,16,128]{2,1,0:T(8,128)(2,1)S(1)}, bf16[64,16,128]{2,1,0:T(8,128)(2,1)S(1)}, u32[]{:S(2)}, u32[]{:S(2)}) collective-permute-start(bf16[64,16,128]{2,1,0:T(8,128)(2,1)S(1)} %slice.80), channel_id=1, source_target_pairs={{2,0},{9,1},{4,2},{11,3},{6,4},{13,5},{0,6},{15,7},{10,8},{17,9},{... | collective-permute-start | bytes 786440 | tf_op jit(solution)/shard_map/ppermute | solution.py:31
  (6 other events, 61.7 us)
Sparse Core Ops, SparseCore 0:
  9.2 62.3 all-gather.1

commit v4 on v3

--- a/solution.py
+++ b/solution.py
@@ -13,7 +13,7 @@
 GROUP = 8
 BS = 128
 STREAMS = 2
-UNROLL = 4
+UNROLL = 16
 epsilon = 1e-06
 XY = ("x", "y")
 
@@ -66,10 +66,13 @@
     sources, refs = refs[:pieces], refs[pieces:]
     if raw:
         inverse_ref, refs = refs[0], refs[1:]
+    else:
+        share_ref, refs = refs[0], refs[1:]
     aff_ref, out_refs, refs = refs[0], refs[1 : 1 + ends], refs[1 + ends :]
     peak_ref, refs = refs[0], refs[1:]
     if raw:
         own_peak_ref, refs = refs[0], refs[1:]
+        share_ref, refs = refs[0], refs[1:]
     held, sems = refs
     blocks, slots = aff_ref.shape[:2]
     genes = held.shape[1]
@@ -97,14 +100,17 @@
             tile = fetch(row * slots + s)
             if s == 0:
                 own = tile.astype(jnp.float32)
-            tile = jnp.concatenate([tile, jnp.ones((16, BS), tile.dtype)], axis=0)
+            if raw:
+                tile = jnp.concatenate([tile, jnp.ones((16, BS), tile.dtype)], axis=0)
             if s > REMOTE:
                 tile = jnp.where(s < count, tile, jnp.zeros_like(tile))
             tiles.append(tile)
         left = jnp.concatenate(tiles, axis=1)
         right = aff_ref[row].reshape(slots * BS, BS)
         total = jnp.dot(left, right, preferred_element_type=jnp.float32)
-        mixed = 0.5 * own + total[:genes] * (0.5 / total[genes : genes + 1])
+        if raw:
+            share_ref[pl.ds(row, 1)] = 0.5 / total[genes : genes + 1]
+        mixed = 0.5 * own + total[:genes] * share_ref[pl.ds(row, 1)]
         for out_ref in out_refs:
             share = out_ref.shape[1]
             out_ref[row] = mixed[:share].astype(out_ref.dtype)
@@ -124,7 +130,7 @@
         own_peak_ref[...] = carry[1]
 
 
-def diffuse(pieces, places, counts, tables, inverse, affinity, ends):
+def diffuse(pieces, places, counts, tables, inverse, share, affinity, ends):
     blocks = affinity.shape[0]
     genes = pieces[0].shape[1]
     total = sum(piece.shape[0] for piece in pieces)
@@ -136,22 +142,23 @@
         functools.partial(step_kernel, n, raw, ends),
         in_specs=[smem] * 3
         + [pl.BlockSpec(memory_space=pl.ANY)] * n
-        + [vmem] * raw
+        + [vmem]
         + [vmem],
-        out_specs=[vmem] * (ends + 1 + raw),
+        out_specs=[vmem] * (ends + 1 + 2 * raw),
         scratch_shapes=[
             pltpu.VMEM((total, genes, BS), pieces[0].dtype),
             pltpu.SemaphoreType.DMA((n,)),
         ],
         out_shape=[jax.ShapeDtypeStruct((blocks, genes // ends, BS), jnp.bfloat16)] * ends
-        + [jax.ShapeDtypeStruct((genes, BS), jnp.float32)] * (1 + raw),
+        + [jax.ShapeDtypeStruct((genes, BS), jnp.float32)] * (1 + raw)
+        + [jax.ShapeDtypeStruct((blocks, BS), jnp.float32)] * raw,
         compiler_params=pltpu.CompilerParams(vmem_limit_bytes=32 * 1024 * 1024),
         cost_estimate=pl.CostEstimate(
             flops=2 * affinity.size * genes,
             bytes_accessed=2 * affinity.size,
             transcendentals=0,
         ),
-    )(places, counts, tables, *pieces, *([inverse] if raw else []), affinity)
+    )(places, counts, tables, *pieces, inverse if raw else share, affinity)
 
 
 def to_all(value, axis, size):
@@ -192,8 +199,8 @@
     places = ((second * SIDE + first) * blocks + within).reshape(-1)
     tables = ((device % (SIDE * SIDE)) * blocks + within).reshape(-1)
 
-    current, peak, own_peak = diffuse(
-        plane(*line(counted, 1), False), places, counts, tables, inverse, affinity, 1
+    current, peak, own_peak, share = diffuse(
+        plane(*line(counted, 1), False), places, counts, tables, inverse, None, affinity, 1
     )
     peaks = [own_peak, peak]
     lines = line(current, STREAMS)
@@ -201,7 +208,7 @@
         if step > 1:
             lines = [line(stream, 1)[0] for stream in streams]
         ends = [
-            diffuse(plane(part, True), places, counts, tables, None, affinity, 1) for part in lines
+            diffuse(plane(part, True), places, counts, tables, None, share, affinity, 1) for part in lines
         ]
         streams = [end[0] for end in ends]
         peaks.append(jnp.concatenate([end[1] for end in ends]))

time: 196 us -> 193 us (0.985)
  Pallas kernels: 17.6 us -> 13.1 us
    pallas_call x5, Pallas kernels: 17.4 us -> 12.9 us  [diffuse(): pl.pallas_call(functools.partial(step_kernel, n, raw, ends), in_specs=[sm...]
  transfers between devices with their start and end apart: 35 -> 35, of which waited for: 13 -> 14; matrix products, arithmetic and copies ran while one was open for 3% -> 3% of each run, Pallas kernels for 5% -> 3%
where the time goes in v4:
time: 193 us; the launch traced here: 192 us
  starting transfers between devices  70.4 us (36%)
  waiting for transfers between devices  47.3 us (25%)
  blocking collectives  34.8 us (18%)
  between operations  13.7 us (7%)
  Pallas kernels  13.1 us (7%)
  local copies, waits for them, and re-layouts  11.6 us (6%)
    ppermute x31, starting transfers between devices, shift(): return lax.ppermute(value, ('x', 'y', 'c'), pairs)  48.6 us
    ppermute x31, waiting for transfers between devices, shift(): return lax.ppermute(value, ('x', 'y', 'c'), pairs)  22.5 us
    all_to_all x2, waiting for transfers between devices, to_all(): lax.all_to_all(jnp.broadcast_to(value[None], (size,) + value.shape), axis...  19.5 us
    all_to_all x1, blocking collectives, local(): result = lax.all_to_all(result, 'z', 0, 0, tiled=True)  17.6 us
    all_to_all x2, starting transfers between devices, to_all(): lax.all_to_all(jnp.broadcast_to(value[None], (size,) + value.shape), axis...  14.3 us
    all_to_all x1, blocking collectives, to_all(): lax.all_to_all(jnp.broadcast_to(value[None], (size,) + value.shape), axis...  13.8 us
    pallas_call x5, Pallas kernels, diffuse(): pl.pallas_call(functools.partial(step_kernel, n, raw, ends), in_specs=[sm...  12.9 us
    all_to_all x1, starting transfers between devices, local(): counted = lax.all_to_all(counted, XY, 2, 0, tiled=True)  7.48 us
  transfers between devices with their start and end apart: 35, of which 14 were waited for; matrix products, arithmetic and copies ran while one was open for 3% of the time, Pallas kernels for 3%

profile of v4, /device:TPU:2, one launch (start us, length us, event | category | flops | bytes accessed | tf_op | source)
XLA Modules:
  0.0 192.4 jit_solution(365517653810492260)
XLA Ops:
  10.5 7.5 %all-to-all-start = ((bf16[2,8,16,512]{3,1,0,2:T(8,128)(2,1)}), bf16[2,8,16,512]{3,1,0,2:T(8,128)(2,1)S(1)}, u32[]{:S(2)}, u32[]{:S(2)}) async-start(bf16[2,8,16,512]{3,1,0,2:T(8,128)(2,1)} %copy.23), calls=%async_computation | async-start | bytes 524288 | tf_op jit(solution)/shard_map/all_to_all | solution.py:180
  19.5 5.2 %all-to-all-done = bf16[2,8,16,512]{3,1,0,2:T(8,128)(2,1)S(1)} async-done(((bf16[2,8,16,512]{3,1,0,2:T(8,128)(2,1)}), bf16[2,8,16,512]{3,1,0,2:T(8,128)(2,1)S(1)}, u32[]{:S(2)}, u32[]{:S(2)}) %all-to-all-start) | async-done | bytes 262176 | tf_op jit(solution)/shard_map/all_to_all | solution.py:180
  26.2 2.8 %collective-permute-start.1 = (bf16[32,32,128]{2,1,0:T(8,128)(2,1)S(1)}, bf16[32,32,128]{2,1,0:T(8,128)(2,1)S(1)}, u32[]{:S(2)}, u32[]{:S(2)}) collective-permute-start(bf16[32,32,128]{2,1,0:T(8,128)(2,1)S(1)} %bitcast.37), channel_id=1, source_target_pairs={{16,0},{5,1},{18,2},{7,3},{20,4},{1,5},{22,6},{3,7},{24,8},{13,9},... | collective-permute-start | bytes 786440 | tf_op jit(solution)/shard_map/ppermute | solution.py:31
  29.5 3.4 %psum.7 = f32[32,128]{1,0:T(8,128)S(1)} all-reduce(f32[32,128]{1,0:T(8,128)S(1)} %convert_reduce_fusion), channel_id=1, replica_groups=mesh['z'=8,'x'=4,'y'=4,'c'=2] {'c'}, use_global_device_ids=true, to_apply=%region_1.2 | all-reduce | flops 4096 | bytes 32768 | tf_op jit(solution)/shard_map/psum | solution.py:187
  33.6 8.5 %all-to-all-start.1 = ((f32[8,40,128]{2,1,0:T(8,128)}), f32[8,40,128]{2,1,0:T(8,128)S(1)}, u32[]{:S(2)}, u32[]{:S(2)}) async-start(f32[8,40,128]{2,1,0:T(8,128)} %broadcast_in_dim.11), calls=%async_computation.1 | async-start | bytes 327680 | tf_op jit(solution)/shard_map/all_to_all | solution.py:165
  46.3 8.1 %all-to-all-done.1 = f32[8,40,128]{2,1,0:T(8,128)S(1)} async-done(((f32[8,40,128]{2,1,0:T(8,128)}), f32[8,40,128]{2,1,0:T(8,128)S(1)}, u32[]{:S(2)}, u32[]{:S(2)}) %all-to-all-start.1) | async-done | bytes 163872 | tf_op jit(solution)/shard_map/all_to_all | solution.py:165
  55.3 5.9 %all-to-all-start.2 = ((f32[16,32,128]{2,1,0:T(8,128)}), f32[16,32,128]{2,1,0:T(8,128)S(1)}, u32[]{:S(2)}, u32[]{:S(2)}) async-start(f32[16,32,128]{2,1,0:T(8,128)} %broadcast_in_dim.12), calls=%async_computation.2 | async-start | bytes 524288 | tf_op jit(solution)/shard_map/all_to_all | solution.py:165
  61.6 11.4 %all-to-all-done.2 = f32[16,32,128]{2,1,0:T(8,128)S(1)} async-done(((f32[16,32,128]{2,1,0:T(8,128)}), f32[16,32,128]{2,1,0:T(8,128)S(1)}, u32[]{:S(2)}, u32[]{:S(2)}) %all-to-all-start.2) | async-done | bytes 262176 | tf_op jit(solution)/shard_map/all_to_all | solution.py:165
  73.1 3.4 %copy-done.1 = bf16[32,8,128,128]{3,2,1,0:T(8,128)(2,1)S(1)} copy-done((bf16[32,8,128,128]{3,2,1,0:T(8,128)(2,1)S(1)}, bf16[32,8,128,128]{3,2,1,0:T(8,128)(2,1)}, u32[]{:S(2)}) %copy-start.1) | copy-done | bytes 8388632
  76.4 4.1 %shard_map.47 = (bf16[32,32,128]{2,1,0:T(8,128)(2,1)S(1)}, f32[32,128]{1,0:T(8,128)S(1)}, f32[32,128]{1,0:T(8,128)S(1)}, f32[32,128]{1,0:T(8,128)S(1)}) custom-call(s32[256]{0:T(256)S(1)} %reshape.66.place_ref, s32[32]{0:T(128)S(1)} %slice_reduce_fusion.1.count_ref, s32[256]{0:T(256)S(1)} %reshape.67.table_ref, bf16[128,32,128]{2,1,0:T(8,128)(2,1)S(1)} %shard_map.46.refs_0_, ...), custom_call_target="tpu_custom_call" | custom-call | flops 268435456 | bytes 8388608 | tf_op jit(solution)/shard_map/pallas_call | solution.py:141
  84.4 2.6 %collective-permute-done.8.refs_3_ = bf16[32,32,128]{2,1,0:T(8,128)(2,1)S(1)} collective-permute-done((bf16[32,32,128]{2,1,0:T(8,128)(2,1)S(1)}, bf16[32,32,128]{2,1,0:T(8,128)(2,1)S(1)}, u32[]{:S(2)}, u32[]{:S(2)}) %collective-permute-start.8) | collective-permute-done | bytes 262176 | tf_op jit(solution)/shard_map/ppermute | solution.py:31
  87.0 3.2 %collective-permute-done.7.refs_2_ = bf16[32,32,128]{2,1,0:T(8,128)(2,1)S(1)} collective-permute-done((bf16[32,32,128]{2,1,0:T(8,128)(2,1)S(1)}, bf16[32,32,128]{2,1,0:T(8,128)(2,1)S(1)}, u32[]{:S(2)}, u32[]{:S(2)}) %collective-permute-start.7) | collective-permute-done | bytes 262176 | tf_op jit(solution)/shard_map/ppermute | solution.py:31
  90.2 2.7 %collective-permute-done.6.refs_1_ = bf16[32,32,128]{2,1,0:T(8,128)(2,1)S(1)} collective-permute-done((bf16[32,32,128]{2,1,0:T(8,128)(2,1)S(1)}, bf16[32,32,128]{2,1,0:T(8,128)(2,1)S(1)}, u32[]{:S(2)}, u32[]{:S(2)}) %collective-permute-start.6) | collective-permute-done | bytes 262176 | tf_op jit(solution)/shard_map/ppermute | solution.py:31
  94.1 2.2 %collective-permute-start.9 = (bf16[128,16,128]{2,1,0:T(8,128)(2,1)S(1)}, bf16[128,16,128]{2,1,0:T(8,128)(2,1)S(1)}, u32[]{:S(2)}, u32[]{:S(2)}) collective-permute-start(bf16[128,16,128]{2,1,0:T(8,128)(2,1)S(1)} %get-tuple-element.20.refs_0_), channel_id=1, source_target_pairs={{2,0},{9,1},{4,2},{11,3},{6,4},{13,5},{0,6},{15,7},{10,8},{17,9},{... | collective-permute-start | bytes 1572872 | tf_op jit(solution)/shard_map/ppermute | solution.py:31
  96.3 3.2 %collective-permute-start.20 = (bf16[128,16,128]{2,1,0:T(8,128)(2,1)S(1)}, bf16[128,16,128]{2,1,0:T(8,128)(2,1)S(1)}, u32[]{:S(2)}, u32[]{:S(2)}) collective-permute-start(bf16[128,16,128]{2,1,0:T(8,128)(2,1)S(1)} %get-tuple-element.24.refs_0_), channel_id=1, source_target_pairs={{2,0},{9,1},{4,2},{11,3},{6,4},{13,5},{0,6},{15,7},{10,8},{17,9},{... | collective-permute-start | bytes 1572872 | tf_op jit(solution)/shard_map/ppermute | solution.py:31
  99.6 3.9 %collective-permute-done.11.refs_4_ = bf16[128,16,128]{2,1,0:T(8,128)(2,1)S(1)} collective-permute-done((bf16[128,16,128]{2,1,0:T(8,128)(2,1)S(1)}, bf16[128,16,128]{2,1,0:T(8,128)(2,1)S(1)}, u32[]{:S(2)}, u32[]{:S(2)}) %collective-permute-start.11) | collective-permute-done | bytes 524320 | tf_op jit(solution)/shard_map/ppermute | solution.py:31
  103.6 3.3 %collective-permute-start.10 = (bf16[64,16,128]{2,1,0:T(8,128)(2,1)S(1)}, bf16[64,16,128]{2,1,0:T(8,128)(2,1)S(1)}, u32[]{:S(2)}, u32[]{:S(2)}) collective-permute-start(bf16[64,16,128]{2,1,0:T(8,128)(2,1)S(1)} %slice.74), channel_id=1, source_target_pairs={{2,0},{9,1},{4,2},{11,3},{6,4},{13,5},{0,6},{15,7},{10,8},{17,9},{... | collective-permute-start | bytes 786440 | tf_op jit(solution)/shard_map/ppermute | solution.py:31
  106.9 2.2 %collective-permute-done.22.refs_4_ = bf16[128,16,128]{2,1,0:T(8,128)(2,1)S(1)} collective-permute-done((bf16[128,16,128]{2,1,0:T(8,128)(2,1)S(1)}, bf16[128,16,128]{2,1,0:T(8,128)(2,1)S(1)}, u32[]{:S(2)}, u32[]{:S(2)}) %collective-permute-start.22) | collective-permute-done | bytes 524320 | tf_op jit(solution)/shard_map/ppermute | solution.py:31
  109.3 3.3 %collective-permute-start.21 = (bf16[64,16,128]{2,1,0:T(8,128)(2,1)S(1)}, bf16[64,16,128]{2,1,0:T(8,128)(2,1)S(1)}, u32[]{:S(2)}, u32[]{:S(2)}) collective-permute-start(bf16[64,16,128]{2,1,0:T(8,128)(2,1)S(1)} %slice.78), channel_id=1, source_target_pairs={{2,0},{9,1},{4,2},{11,3},{6,4},{13,5},{0,6},{15,7},{10,8},{17,9},{... | collective-permute-start | bytes 786440 | tf_op jit(solution)/shard_map/ppermute | solution.py:31
  112.6 2.2 %shard_map.49 = (bf16[32,16,128]{2,1,0:T(8,128)(2,1)S(1)}, f32[16,128]{1,0:T(8,128)S(1)}) custom-call(s32[256]{0:T(256)S(1)} %reshape.66.place_ref, s32[32]{0:T(128)S(1)} %slice_reduce_fusion.1.count_ref, s32[256]{0:T(256)S(1)} %reshape.67.table_ref, bf16[128,16,128]{2,1,0:T(8,128)(2,1)S(1)} %get-tuple-element.20.refs_0_, ...), custom_call_target="tpu_custom_call" | custom-call | flops 134217728 | bytes 8388608 | tf_op jit(solution)/shard_map/pallas_call | solution.py:141
  117.3 2.1 %collective-permute-start.13 = (bf16[32,16,128]{2,1,0:T(8,128)(2,1)S(1)}, bf16[32,16,128]{2,1,0:T(8,128)(2,1)S(1)}, u32[]{:S(2)}, u32[]{:S(2)}) collective-permute-start(bf16[32,16,128]{2,1,0:T(8,128)(2,1)S(1)} %get-tuple-element.22.refs_0_), channel_id=1, source_target_pairs={{8,0},{3,1},{10,2},{5,3},{12,4},{7,5},{14,6},{1,7},{16,8},{11,9},{... | collective-permute-start | bytes 393224 | tf_op jit(solution)/shard_map/ppermute | solution.py:31
  119.6 2.2 %shard_map.52 = (bf16[32,16,128]{2,1,0:T(8,128)(2,1)S(1)}, f32[16,128]{1,0:T(8,128)S(1)}) custom-call(s32[256]{0:T(256)S(1)} %reshape.66.place_ref, s32[32]{0:T(128)S(1)} %slice_reduce_fusion.1.count_ref, s32[256]{0:T(256)S(1)} %reshape.67.table_ref, bf16[128,16,128]{2,1,0:T(8,128)(2,1)S(1)} %get-tuple-element.24.refs_0_, ...), custom_call_target="tpu_custom_call" | custom-call | flops 134217728 | bytes 8388608 | tf_op jit(solution)/shard_map/pallas_call | solution.py:141
  122.0 2.5 %collective-permute-start.25 = (bf16[32,16,128]{2,1,0:T(8,128)(2,1)S(1)}, bf16[32,16,128]{2,1,0:T(8,128)(2,1)S(1)}, u32[]{:S(2)}, u32[]{:S(2)}) collective-permute-start(bf16[32,16,128]{2,1,0:T(8,128)(2,1)S(1)} %get-tuple-element.25.refs_0_), channel_id=1, source_target_pairs={{16,0},{5,1},{18,2},{7,3},{20,4},{1,5},{22,6},{3,7},{24,8},{13,9},... | collective-permute-start | bytes 393224 | tf_op jit(solution)/shard_map/ppermute | solution.py:31
  125.9 3.8 %collective-permute-start.16 = (bf16[128,16,128]{2,1,0:T(8,128)(2,1)S(1)}, bf16[128,16,128]{2,1,0:T(8,128)(2,1)S(1)}, u32[]{:S(2)}, u32[]{:S(2)}) collective-permute-start(bf16[128,16,128]{2,1,0:T(8,128)(2,1)S(1)} %shard_map.50.refs_0_), channel_id=1, source_target_pairs={{2,0},{9,1},{4,2},{11,3},{6,4},{13,5},{0,6},{15,7},{10,8},{17,9},{... | collective-permute-start | bytes 1572872 | tf_op jit(solution)/shard_map/ppermute | solution.py:31
  132.2 3.2 %collective-permute-start.27 = (bf16[128,16,128]{2,1,0:T(8,128)(2,1)S(1)}, bf16[128,16,128]{2,1,0:T(8,128)(2,1)S(1)}, u32[]{:S(2)}, u32[]{:S(2)}) collective-permute-start(bf16[128,16,128]{2,1,0:T(8,128)(2,1)S(1)} %shard_map.53.refs_0_), channel_id=1, source_target_pairs={{2,0},{9,1},{4,2},{11,3},{6,4},{13,5},{0,6},{15,7},{10,8},{17,9},{... | collective-permute-start | bytes 1572872 | tf_op jit(solution)/shard_map/ppermute | solution.py:31
  137.1 3.3 %collective-permute-start.17 = (bf16[64,16,128]{2,1,0:T(8,128)(2,1)S(1)}, bf16[64,16,128]{2,1,0:T(8,128)(2,1)S(1)}, u32[]{:S(2)}, u32[]{:S(2)}) collective-permute-start(bf16[64,16,128]{2,1,0:T(8,128)(2,1)S(1)} %slice.76), channel_id=1, source_target_pairs={{2,0},{9,1},{4,2},{11,3},{6,4},{13,5},{0,6},{15,7},{10,8},{17,9},{... | collective-permute-start | bytes 786440 | tf_op jit(solution)/shard_map/ppermute | solution.py:31
  140.4 2.1 %collective-permute-done.29.refs_4_ = bf16[128,16,128]{2,1,0:T(8,128)(2,1)S(1)} collective-permute-done((bf16[128,16,128]{2,1,0:T(8,128)(2,1)S(1)}, bf16[128,16,128]{2,1,0:T(8,128)(2,1)S(1)}, u32[]{:S(2)}, u32[]{:S(2)}) %collective-permute-start.29) | collective-permute-done | bytes 524320 | tf_op jit(solution)/shard_map/ppermute | solution.py:31
  142.7 3.3 %collective-permute-start.28 = (bf16[64,16,128]{2,1,0:T(8,128)(2,1)S(1)}, bf16[64,16,128]{2,1,0:T(8,128)(2,1)S(1)}, u32[]{:S(2)}, u32[]{:S(2)}) collective-permute-start(bf16[64,16,128]{2,1,0:T(8,128)(2,1)S(1)} %slice.80), channel_id=1, source_target_pairs={{2,0},{9,1},{4,2},{11,3},{6,4},{13,5},{0,6},{15,7},{10,8},{17,9},{... | collective-permute-start | bytes 786440 | tf_op jit(solution)/shard_map/ppermute | solution.py:31
  146.0 2.2 %shard_map.51 = (bf16[32,16,128]{2,1,0:T(8,128)(2,1)S(1)}, f32[16,128]{1,0:T(8,128)S(1)}) custom-call(s32[256]{0:T(256)S(1)} %reshape.66.place_ref, s32[32]{0:T(128)S(1)} %slice_reduce_fusion.1.count_ref, s32[256]{0:T(256)S(1)} %reshape.67.table_ref, bf16[128,16,128]{2,1,0:T(8,128)(2,1)S(1)} %shard_map.50.refs_0_, ...), custom_call_target="tpu_custom_call" | custom-call | flops 134217728 | bytes 8388608 | tf_op jit(solution)/shard_map/pallas_call | solution.py:141
  150.2 2.2 %shard_map.54 = (bf16[32,16,128]{2,1,0:T(8,128)(2,1)S(1)}, f32[16,128]{1,0:T(8,128)S(1)}) custom-call(s32[256]{0:T(256)S(1)} %reshape.66.place_ref, s32[32]{0:T(128)S(1)} %slice_reduce_fusion.1.count_ref, s32[256]{0:T(256)S(1)} %reshape.67.table_ref, bf16[128,16,128]{2,1,0:T(8,128)(2,1)S(1)} %shard_map.53.refs_0_, ...), custom_call_target="tpu_custom_call" | custom-call | flops 134217728 | bytes 8388608 | tf_op jit(solution)/shard_map/pallas_call | solution.py:141
  152.6 13.8 %all_to_all.36 = f32[16,1,128]{2,1,0:T(1,128)S(1)} all-to-all(f32[16,1,128]{2,1,0:T(1,128)S(1)} %broadcast_in_dim.27), channel_id=1, replica_groups=mesh['z'=8,'x'=4,'y'=4,'c'=2] {'x','y'}, dimensions={0} | all-to-all | bytes 16384 | tf_op jit(solution)/shard_map/all_to_all | solution.py:165
  166.7 17.6 %all_to_all.37 = bf16[32,32,128]{2,1,0:T(8,128)(2,1)S(1)} all-to-all(bf16[32,32,128]{2,1,0:T(8,128)(2,1)S(1)} %multiply_convert_fusion), channel_id=1, replica_groups=mesh['z'=8,'x'=4,'y'=4,'c'=2] {'z'}, dimensions={0} | all-to-all | bytes 524288 | tf_op jit(solution)/shard_map/all_to_all | solution.py:222
  (97 shorter events, 31.3 us)
Async XLA Ops:
  6.5 66.5 %all-gather.2.cloned.1.call-start = ((), (), s32[]{:S(2)}) async-start(), calls=%async_computation.5 | async-start | bytes 8912896 | tf_op jit(solution)/shard_map/all_gather | solution.py:174
  10.5 14.3 %all-to-all-start = ((bf16[2,8,16,512]{3,1,0,2:T(8,128)(2,1)}), bf16[2,8,16,512]{3,1,0,2:T(8,128)(2,1)S(1)}, u32[]{:S(2)}, u32[]{:S(2)}) async-start(bf16[2,8,16,512]{3,1,0,2:T(8,128)(2,1)} %copy.23), calls=%async_computation | async-start | bytes 524288 | tf_op jit(solution)/shard_map/all_to_all | solution.py:180
  25.0 17.0 %collective-permute-start.2 = (bf16[32,32,128]{2,1,0:T(8,128)(2,1)S(1)}, bf16[32,32,128]{2,1,0:T(8,128)(2,1)S(1)}, u32[]{:S(2)}, u32[]{:S(2)}) collective-permute-start(bf16[32,32,128]{2,1,0:T(8,128)(2,1)S(1)} %bitcast.36), channel_id=1, source_target_pairs={{24,0},{7,1},{26,2},{1,3},{28,4},{3,5},{30,6},{5,7},{0,8},{15,9},{... | collective-permute-start | bytes 786440 | tf_op jit(solution)/shard_map/ppermute | solution.py:31
  26.2 15.9 %collective-permute-start.1 = (bf16[32,32,128]{2,1,0:T(8,128)(2,1)S(1)}, bf16[32,32,128]{2,1,0:T(8,128)(2,1)S(1)}, u32[]{:S(2)}, u32[]{:S(2)}) collective-permute-start(bf16[32,32,128]{2,1,0:T(8,128)(2,1)S(1)} %bitcast.37), channel_id=1, source_target_pairs={{16,0},{5,1},{18,2},{7,3},{20,4},{1,5},{22,6},{3,7},{24,8},{13,9},... | collective-permute-start | bytes 786440 | tf_op jit(solution)/shard_map/ppermute | solution.py:31
  29.0 13.1 %collective-permute-start = (bf16[32,32,128]{2,1,0:T(8,128)(2,1)S(1)}, bf16[32,32,128]{2,1,0:T(8,128)(2,1)S(1)}, u32[]{:S(2)}, u32[]{:S(2)}) collective-permute-start(bf16[32,32,128]{2,1,0:T(8,128)(2,1)S(1)} %bitcast.38), channel_id=1, source_target_pairs={{8,0},{3,1},{10,2},{5,3},{12,4},{7,5},{14,6},{1,7},{16,8},{11,9},{... | collective-permute-start | bytes 786440 | tf_op jit(solution)/shard_map/ppermute | solution.py:31
  33.6 20.8 %all-to-all-start.1 = ((f32[8,40,128]{2,1,0:T(8,128)}), f32[8,40,128]{2,1,0:T(8,128)S(1)}, u32[]{:S(2)}, u32[]{:S(2)}) async-start(f32[8,40,128]{2,1,0:T(8,128)} %broadcast_in_dim.11), calls=%async_computation.1 | async-start | bytes 327680 | tf_op jit(solution)/shard_map/all_to_all | solution.py:165
  42.2 30.9 %collective-permute-start.5 = (bf16[128,32,128]{2,1,0:T(8,128)(2,1)S(1)}, bf16[128,32,128]{2,1,0:T(8,128)(2,1)S(1)}, u32[]{:S(2)}, u32[]{:S(2)}) collective-permute-start(bf16[128,32,128]{2,1,0:T(8,128)(2,1)S(1)} %shard_map.46.refs_0_), channel_id=1, source_target_pairs={{6,0},{25,1},{0,2},{27,3},{2,4},{29,5},{4,6},{31,7},{14,8},{1,9},{... | collective-permute-start | bytes 3145736 | tf_op jit(solution)/shard_map/ppermute | solution.py:31
  42.8 30.2 %collective-permute-start.4 = (bf16[128,32,128]{2,1,0:T(8,128)(2,1)S(1)}, bf16[128,32,128]{2,1,0:T(8,128)(2,1)}, u32[]{:S(2)}, u32[]{:S(2)}) collective-permute-start(bf16[128,32,128]{2,1,0:T(8,128)(2,1)S(1)} %shard_map.46.refs_0_), channel_id=1, source_target_pairs={{4,0},{17,1},{6,2},{19,3},{0,4},{21,5},{2,6},{23,7},{12,8},{25,9},... | collective-permute-start | bytes 3145736 | tf_op jit(solution)/shard_map/ppermute | solution.py:31
  44.6 28.4 %collective-permute-start.3 = (bf16[128,32,128]{2,1,0:T(8,128)(2,1)S(1)}, bf16[128,32,128]{2,1,0:T(8,128)(2,1)}, u32[]{:S(2)}, u32[]{:S(2)}) collective-permute-start(bf16[128,32,128]{2,1,0:T(8,128)(2,1)S(1)} %shard_map.46.refs_0_), channel_id=1, source_target_pairs={{2,0},{9,1},{4,2},{11,3},{6,4},{13,5},{0,6},{15,7},{10,8},{17,9},{... | collective-permute-start | bytes 3145736 | tf_op jit(solution)/shard_map/ppermute | solution.py:31
  55.3 17.7 %all-to-all-start.2 = ((f32[16,32,128]{2,1,0:T(8,128)}), f32[16,32,128]{2,1,0:T(8,128)S(1)}, u32[]{:S(2)}, u32[]{:S(2)}) async-start(f32[16,32,128]{2,1,0:T(8,128)} %broadcast_in_dim.12), calls=%async_computation.2 | async-start | bytes 524288 | tf_op jit(solution)/shard_map/all_to_all | solution.py:165
  82.3 8.0 %collective-permute-start.7 = (bf16[32,32,128]{2,1,0:T(8,128)(2,1)S(1)}, bf16[32,32,128]{2,1,0:T(8,128)(2,1)S(1)}, u32[]{:S(2)}, u32[]{:S(2)}) collective-permute-start(bf16[32,32,128]{2,1,0:T(8,128)(2,1)S(1)} %get-tuple-element.19.refs_0_), channel_id=1, source_target_pairs={{16,0},{5,1},{18,2},{7,3},{20,4},{1,5},{22,6},{3,7},{24,8},{13,9},... | collective-permute-start | bytes 786440 | tf_op jit(solution)/shard_map/ppermute | solution.py:31
  84.2 8.8 %collective-permute-start.6 = (bf16[32,32,128]{2,1,0:T(8,128)(2,1)S(1)}, bf16[32,32,128]{2,1,0:T(8,128)(2,1)S(1)}, u32[]{:S(2)}, u32[]{:S(2)}) collective-permute-start(bf16[32,32,128]{2,1,0:T(8,128)(2,1)S(1)} %get-tuple-element.19.refs_0_), channel_id=1, source_target_pairs={{8,0},{3,1},{10,2},{5,3},{12,4},{7,5},{14,6},{1,7},{16,8},{11,9},{... | collective-permute-start | bytes 786440 | tf_op jit(solution)/shard_map/ppermute | solution.py:31
  93.0 10.5 %collective-permute-start.11 = (bf16[128,16,128]{2,1,0:T(8,128)(2,1)S(1)}, bf16[128,16,128]{2,1,0:T(8,128)(2,1)S(1)}, u32[]{:S(2)}, u32[]{:S(2)}) collective-permute-start(bf16[128,16,128]{2,1,0:T(8,128)(2,1)S(1)} %get-tuple-element.20.refs_0_), channel_id=1, source_target_pairs={{6,0},{25,1},{0,2},{27,3},{2,4},{29,5},{4,6},{31,7},{14,8},{1,9},{... | collective-permute-start | bytes 1572872 | tf_op jit(solution)/shard_map/ppermute | solution.py:31
  94.1 9.5 %collective-permute-start.9 = (bf16[128,16,128]{2,1,0:T(8,128)(2,1)S(1)}, bf16[128,16,128]{2,1,0:T(8,128)(2,1)S(1)}, u32[]{:S(2)}, u32[]{:S(2)}) collective-permute-start(bf16[128,16,128]{2,1,0:T(8,128)(2,1)S(1)} %get-tuple-element.20.refs_0_), channel_id=1, source_target_pairs={{2,0},{9,1},{4,2},{11,3},{6,4},{13,5},{0,6},{15,7},{10,8},{17,9},{... | collective-permute-start | bytes 1572872 | tf_op jit(solution)/shard_map/ppermute | solution.py:31
  96.3 12.8 %collective-permute-start.22 = (bf16[128,16,128]{2,1,0:T(8,128)(2,1)S(1)}, bf16[128,16,128]{2,1,0:T(8,128)(2,1)S(1)}, u32[]{:S(2)}, u32[]{:S(2)}) collective-permute-start(bf16[128,16,128]{2,1,0:T(8,128)(2,1)S(1)} %get-tuple-element.24.refs_0_), channel_id=1, source_target_pairs={{6,0},{25,1},{0,2},{27,3},{2,4},{29,5},{4,6},{31,7},{14,8},{1,9},{... | collective-permute-start | bytes 1572872 | tf_op jit(solution)/shard_map/ppermute | solution.py:31
  96.3 12.9 %collective-permute-start.20 = (bf16[128,16,128]{2,1,0:T(8,128)(2,1)S(1)}, bf16[128,16,128]{2,1,0:T(8,128)(2,1)S(1)}, u32[]{:S(2)}, u32[]{:S(2)}) collective-permute-start(bf16[128,16,128]{2,1,0:T(8,128)(2,1)S(1)} %get-tuple-element.24.refs_0_), channel_id=1, source_target_pairs={{2,0},{9,1},{4,2},{11,3},{6,4},{13,5},{0,6},{15,7},{10,8},{17,9},{... | collective-permute-start | bytes 1572872 | tf_op jit(solution)/shard_map/ppermute | solution.py:31
  103.5 9.0 %collective-permute-start.12 = (bf16[64,16,128]{2,1,0:T(8,128)(2,1)S(1)}, bf16[64,16,128]{2,1,0:T(8,128)(2,1)S(1)}, u32[]{:S(2)}, u32[]{:S(2)}) collective-permute-start(bf16[64,16,128]{2,1,0:T(8,128)(2,1)S(1)} %slice.75), channel_id=1, source_target_pairs={{6,0},{25,1},{0,2},{27,3},{2,4},{29,5},{4,6},{31,7},{14,8},{1,9},{... | collective-permute-start | bytes 786440 | tf_op jit(solution)/shard_map/ppermute | solution.py:31
  103.6 8.9 %collective-permute-start.10 = (bf16[64,16,128]{2,1,0:T(8,128)(2,1)S(1)}, bf16[64,16,128]{2,1,0:T(8,128)(2,1)S(1)}, u32[]{:S(2)}, u32[]{:S(2)}) collective-permute-start(bf16[64,16,128]{2,1,0:T(8,128)(2,1)S(1)} %slice.74), channel_id=1, source_target_pairs={{2,0},{9,1},{4,2},{11,3},{6,4},{13,5},{0,6},{15,7},{10,8},{17,9},{... | collective-permute-start | bytes 786440 | tf_op jit(solution)/shard_map/ppermute | solution.py:31
  109.1 10.5 %collective-permute-start.23 = (bf16[64,16,128]{2,1,0:T(8,128)(2,1)S(1)}, bf16[64,16,128]{2,1,0:T(8,128)(2,1)S(1)}, u32[]{:S(2)}, u32[]{:S(2)}) collective-permute-start(bf16[64,16,128]{2,1,0:T(8,128)(2,1)S(1)} %slice.79), channel_id=1, source_target_pairs={{6,0},{25,1},{0,2},{27,3},{2,4},{29,5},{4,6},{31,7},{14,8},{1,9},{... | collective-permute-start | bytes 786440 | tf_op jit(solution)/shard_map/ppermute | solution.py:31
  109.3 10.3 %collective-permute-start.21 = (bf16[64,16,128]{2,1,0:T(8,128)(2,1)S(1)}, bf16[64,16,128]{2,1,0:T(8,128)(2,1)S(1)}, u32[]{:S(2)}, u32[]{:S(2)}) collective-permute-start(bf16[64,16,128]{2,1,0:T(8,128)(2,1)S(1)} %slice.78), channel_id=1, source_target_pairs={{2,0},{9,1},{4,2},{11,3},{6,4},{13,5},{0,6},{15,7},{10,8},{17,9},{... | collective-permute-start | bytes 786440 | tf_op jit(solution)/shard_map/ppermute | solution.py:31
  114.8 9.7 %collective-permute-start.15 = (bf16[32,16,128]{2,1,0:T(8,128)(2,1)S(1)}, bf16[32,16,128]{2,1,0:T(8,128)(2,1)S(1)}, u32[]{:S(2)}, u32[]{:S(2)}) collective-permute-start(bf16[32,16,128]{2,1,0:T(8,128)(2,1)S(1)} %get-tuple-element.22.refs_0_), channel_id=1, source_target_pairs={{24,0},{7,1},{26,2},{1,3},{28,4},{3,5},{30,6},{5,7},{0,8},{15,9},{... | collective-permute-start | bytes 393224 | tf_op jit(solution)/shard_map/ppermute | solution.py:31
  115.4 10.3 %collective-permute-start.14 = (bf16[32,16,128]{2,1,0:T(8,128)(2,1)S(1)}, bf16[32,16,128]{2,1,0:T(8,128)(2,1)S(1)}, u32[]{:S(2)}, u32[]{:S(2)}) collective-permute-start(bf16[32,16,128]{2,1,0:T(8,128)(2,1)S(1)} %get-tuple-element.22.refs_0_), channel_id=1, source_target_pairs={{16,0},{5,1},{18,2},{7,3},{20,4},{1,5},{22,6},{3,7},{24,8},{13,9},... | collective-permute-start | bytes 393224 | tf_op jit(solution)/shard_map/ppermute | solution.py:31
  117.3 8.5 %collective-permute-start.13 = (bf16[32,16,128]{2,1,0:T(8,128)(2,1)S(1)}, bf16[32,16,128]{2,1,0:T(8,128)(2,1)S(1)}, u32[]{:S(2)}, u32[]{:S(2)}) collective-permute-start(bf16[32,16,128]{2,1,0:T(8,128)(2,1)S(1)} %get-tuple-element.22.refs_0_), channel_id=1, source_target_pairs={{8,0},{3,1},{10,2},{5,3},{12,4},{7,5},{14,6},{1,7},{16,8},{11,9},{... | collective-permute-start | bytes 393224 | tf_op jit(solution)/shard_map/ppermute | solution.py:31
  121.8 7.9 %collective-permute-start.26 = (bf16[32,16,128]{2,1,0:T(8,128)(2,1)S(1)}, bf16[32,16,128]{2,1,0:T(8,128)(2,1)S(1)}, u32[]{:S(2)}, u32[]{:S(2)}) collective-permute-start(bf16[32,16,128]{2,1,0:T(8,128)(2,1)S(1)} %get-tuple-element.25.refs_0_), channel_id=1, source_target_pairs={{24,0},{7,1},{26,2},{1,3},{28,4},{3,5},{30,6},{5,7},{0,8},{15,9},{... | collective-permute-start | bytes 393224 | tf_op jit(solution)/shard_map/ppermute | solution.py:31
  122.0 7.9 %collective-permute-start.25 = (bf16[32,16,128]{2,1,0:T(8,128)(2,1)S(1)}, bf16[32,16,128]{2,1,0:T(8,128)(2,1)S(1)}, u32[]{:S(2)}, u32[]{:S(2)}) collective-permute-start(bf16[32,16,128]{2,1,0:T(8,128)(2,1)S(1)} %get-tuple-element.25.refs_0_), channel_id=1, source_target_pairs={{16,0},{5,1},{18,2},{7,3},{20,4},{1,5},{22,6},{3,7},{24,8},{13,9},... | collective-permute-start | bytes 393224 | tf_op jit(solution)/shard_map/ppermute | solution.py:31
  125.8 10.9 %collective-permute-start.18 = (bf16[128,16,128]{2,1,0:T(8,128)(2,1)S(1)}, bf16[128,16,128]{2,1,0:T(8,128)(2,1)S(1)}, u32[]{:S(2)}, u32[]{:S(2)}) collective-permute-start(bf16[128,16,128]{2,1,0:T(8,128)(2,1)S(1)} %shard_map.50.refs_0_), channel_id=1, source_target_pairs={{6,0},{25,1},{0,2},{27,3},{2,4},{29,5},{4,6},{31,7},{14,8},{1,9},{... | collective-permute-start | bytes 1572872 | tf_op jit(solution)/shard_map/ppermute | solution.py:31
  125.9 11.2 %collective-permute-start.16 = (bf16[128,16,128]{2,1,0:T(8,128)(2,1)S(1)}, bf16[128,16,128]{2,1,0:T(8,128)(2,1)S(1)}, u32[]{:S(2)}, u32[]{:S(2)}) collective-permute-start(bf16[128,16,128]{2,1,0:T(8,128)(2,1)S(1)} %shard_map.50.refs_0_), channel_id=1, source_target_pairs={{2,0},{9,1},{4,2},{11,3},{6,4},{13,5},{0,6},{15,7},{10,8},{17,9},{... | collective-permute-start | bytes 1572872 | tf_op jit(solution)/shard_map/ppermute | solution.py:31
  131.9 10.7 %collective-permute-start.29 = (bf16[128,16,128]{2,1,0:T(8,128)(2,1)S(1)}, bf16[128,16,128]{2,1,0:T(8,128)(2,1)S(1)}, u32[]{:S(2)}, u32[]{:S(2)}) collective-permute-start(bf16[128,16,128]{2,1,0:T(8,128)(2,1)S(1)} %shard_map.53.refs_0_), channel_id=1, source_target_pairs={{6,0},{25,1},{0,2},{27,3},{2,4},{29,5},{4,6},{31,7},{14,8},{1,9},{... | collective-permute-start | bytes 1572872 | tf_op jit(solution)/shard_map/ppermute | solution.py:31
  132.2 10.4 %collective-permute-start.27 = (bf16[128,16,128]{2,1,0:T(8,128)(2,1)S(1)}, bf16[128,16,128]{2,1,0:T(8,128)(2,1)S(1)}, u32[]{:S(2)}, u32[]{:S(2)}) collective-permute-start(bf16[128,16,128]{2,1,0:T(8,128)(2,1)S(1)} %shard_map.53.refs_0_), channel_id=1, source_target_pairs={{2,0},{9,1},{4,2},{11,3},{6,4},{13,5},{0,6},{15,7},{10,8},{17,9},{... | collective-permute-start | bytes 1572872 | tf_op jit(solution)/shard_map/ppermute | solution.py:31
  136.8 9.2 %collective-permute-start.19 = (bf16[64,16,128]{2,1,0:T(8,128)(2,1)S(1)}, bf16[64,16,128]{2,1,0:T(8,128)(2,1)S(1)}, u32[]{:S(2)}, u32[]{:S(2)}) collective-permute-start(bf16[64,16,128]{2,1,0:T(8,128)(2,1)S(1)} %slice.77), channel_id=1, source_target_pairs={{6,0},{25,1},{0,2},{27,3},{2,4},{29,5},{4,6},{31,7},{14,8},{1,9},{... | collective-permute-start | bytes 786440 | tf_op jit(solution)/shard_map/ppermute | solution.py:31
  137.1 8.9 %collective-permute-start.17 = (bf16[64,16,128]{2,1,0:T(8,128)(2,1)S(1)}, bf16[64,16,128]{2,1,0:T(8,128)(2,1)S(1)}, u32[]{:S(2)}, u32[]{:S(2)}) collective-permute-start(bf16[64,16,128]{2,1,0:T(8,128)(2,1)S(1)} %slice.76), channel_id=1, source_target_pairs={{2,0},{9,1},{4,2},{11,3},{6,4},{13,5},{0,6},{15,7},{10,8},{17,9},{... | collective-permute-start | bytes 786440 | tf_op jit(solution)/shard_map/ppermute | solution.py:31
  142.6 7.7 %collective-permute-start.30 = (bf16[64,16,128]{2,1,0:T(8,128)(2,1)S(1)}, bf16[64,16,128]{2,1,0:T(8,128)(2,1)S(1)}, u32[]{:S(2)}, u32[]{:S(2)}) collective-permute-start(bf16[64,16,128]{2,1,0:T(8,128)(2,1)S(1)} %slice.81), channel_id=1, source_target_pairs={{6,0},{25,1},{0,2},{27,3},{2,4},{29,5},{4,6},{31,7},{14,8},{1,9},{... | collective-permute-start | bytes 786440 | tf_op jit(solution)/shard_map/ppermute | solution.py:31
  (6 other events, 62.1 us)
Sparse Core Ops, SparseCore 0:
  9.2 62.3 all-gather.1

commit v5 on v4

--- a/solution.py
+++ b/solution.py
@@ -184,7 +184,8 @@
     table = jnp.concatenate([neighbours, counts[:, None]], axis=1).reshape(1, -1)
     used = table.shape[1]
     table = jnp.pad(table.astype(jnp.float32), ((0, 7), (0, BS - used)))
-    sums = lax.psum(jnp.sum(counted.astype(jnp.float32), axis=1), "c")
+    sums = jnp.sum(counted.astype(jnp.float32), axis=1)
+    sums = sums + lax.ppermute(sums, "c", [(0, 1), (1, 0)])
     sums = to_all(jnp.concatenate([sums, table]), "z", GROUP)
     inverse = (2 * GROUP * genes) / jnp.sum(sums[:, :blocks], axis=0)
     inverse = to_all(inverse, XY, SIDE * SIDE).reshape(-1, BS)

time: 193 us -> 190 us (0.984)
  blocking collectives: 34.8 us -> 30.9 us
    psum x1 -> x0, blocking collectives: 3.36 us -> none  [local(): sums = lax.psum(jnp.sum(counted.astype(jnp.float32), axis=1), 'c')]
  transfers between devices with their start and end apart: 35 -> 36, of which waited for: 14 -> 14; matrix products, arithmetic and copies ran while one was open for 3% -> 3% of each run, Pallas kernels for 3% -> 4%
where the time goes in v5:
time: 190 us
  starting transfers between devices  70.1 us (37%)
  waiting for transfers between devices  48.7 us (26%)
  blocking collectives  30.9 us (16%)
  between operations  13.7 us (7%)
  Pallas kernels  13.1 us (7%)
  local copies, waits for them, and re-layouts  11.7 us (6%)
    ppermute x31, starting transfers between devices, shift(): return lax.ppermute(value, ('x', 'y', 'c'), pairs)  48.2 us
    ppermute x31, waiting for transfers between devices, shift(): return lax.ppermute(value, ('x', 'y', 'c'), pairs)  22.1 us
    all_to_all x2, waiting for transfers between devices, to_all(): lax.all_to_all(jnp.broadcast_to(value[None], (size,) + value.shape), axis...  19.6 us
    all_to_all x1, blocking collectives, local(): result = lax.all_to_all(result, 'z', 0, 0, tiled=True)  17.3 us
    all_to_all x2, starting transfers between devices, to_all(): lax.all_to_all(jnp.broadcast_to(value[None], (size,) + value.shape), axis...  14.3 us
    all_to_all x1, blocking collectives, to_all(): lax.all_to_all(jnp.broadcast_to(value[None], (size,) + value.shape), axis...  13.7 us
    pallas_call x5, Pallas kernels, diffuse(): pl.pallas_call(functools.partial(step_kernel, n, raw, ends), in_specs=[sm...  12.9 us
    all_to_all x1, starting transfers between devices, local(): counted = lax.all_to_all(counted, XY, 2, 0, tiled=True)  7.48 us
  transfers between devices with their start and end apart: 36, of which 14 were waited for; matrix products, arithmetic and copies ran while one was open for 3% of the time, Pallas kernels for 4%

profile of v5, /device:TPU:2, one launch (start us, length us, event | category | flops | bytes accessed | tf_op | source)
XLA Modules:
  0.0 189.6 jit_solution(15552156681534337130)
XLA Ops:
  10.5 7.5 %all-to-all-start = ((bf16[2,8,16,512]{3,1,0,2:T(8,128)(2,1)}), bf16[2,8,16,512]{3,1,0,2:T(8,128)(2,1)S(1)}, u32[]{:S(2)}, u32[]{:S(2)}) async-start(bf16[2,8,16,512]{3,1,0,2:T(8,128)(2,1)} %copy.23), calls=%async_computation | async-start | bytes 524288 | tf_op jit(solution)/shard_map/all_to_all | solution.py:180
  18.7 6.1 %all-to-all-done = bf16[2,8,16,512]{3,1,0,2:T(8,128)(2,1)S(1)} async-done(((bf16[2,8,16,512]{3,1,0,2:T(8,128)(2,1)}), bf16[2,8,16,512]{3,1,0,2:T(8,128)(2,1)S(1)}, u32[]{:S(2)}, u32[]{:S(2)}) %all-to-all-start) | async-done | bytes 262176 | tf_op jit(solution)/shard_map/all_to_all | solution.py:180
  27.2 2.8 %collective-permute-start.2 = (bf16[32,32,128]{2,1,0:T(8,128)(2,1)S(1)}, bf16[32,32,128]{2,1,0:T(8,128)(2,1)S(1)}, u32[]{:S(2)}, u32[]{:S(2)}) collective-permute-start(bf16[32,32,128]{2,1,0:T(8,128)(2,1)S(1)} %bitcast.37), channel_id=1, source_target_pairs={{16,0},{5,1},{18,2},{7,3},{20,4},{1,5},{22,6},{3,7},{24,8},{13,9},... | collective-permute-start | bytes 786440 | tf_op jit(solution)/shard_map/ppermute | solution.py:31
  31.2 8.5 %all-to-all-start.1 = ((f32[8,40,128]{2,1,0:T(8,128)}), f32[8,40,128]{2,1,0:T(8,128)S(1)}, u32[]{:S(2)}, u32[]{:S(2)}) async-start(f32[8,40,128]{2,1,0:T(8,128)} %broadcast_in_dim.11), calls=%async_computation.1 | async-start | bytes 327680 | tf_op jit(solution)/shard_map/all_to_all | solution.py:165
  43.9 7.7 %all-to-all-done.1 = f32[8,40,128]{2,1,0:T(8,128)S(1)} async-done(((f32[8,40,128]{2,1,0:T(8,128)}), f32[8,40,128]{2,1,0:T(8,128)S(1)}, u32[]{:S(2)}, u32[]{:S(2)}) %all-to-all-start.1) | async-done | bytes 163872 | tf_op jit(solution)/shard_map/all_to_all | solution.py:165
  52.5 5.8 %all-to-all-start.2 = ((f32[16,32,128]{2,1,0:T(8,128)}), f32[16,32,128]{2,1,0:T(8,128)S(1)}, u32[]{:S(2)}, u32[]{:S(2)}) async-start(f32[16,32,128]{2,1,0:T(8,128)} %broadcast_in_dim.12), calls=%async_computation.2 | async-start | bytes 524288 | tf_op jit(solution)/shard_map/all_to_all | solution.py:165
  58.8 11.8 %all-to-all-done.2 = f32[16,32,128]{2,1,0:T(8,128)S(1)} async-done(((f32[16,32,128]{2,1,0:T(8,128)}), f32[16,32,128]{2,1,0:T(8,128)S(1)}, u32[]{:S(2)}, u32[]{:S(2)}) %all-to-all-start.2) | async-done | bytes 262176 | tf_op jit(solution)/shard_map/all_to_all | solution.py:165
  71.6 3.4 %copy-done.1 = bf16[32,8,128,128]{3,2,1,0:T(8,128)(2,1)S(1)} copy-done((bf16[32,8,128,128]{3,2,1,0:T(8,128)(2,1)S(1)}, bf16[32,8,128,128]{3,2,1,0:T(8,128)(2,1)}, u32[]{:S(2)}) %copy-start.1) | copy-done | bytes 8388632
  75.0 4.1 %shard_map.47 = (bf16[32,32,128]{2,1,0:T(8,128)(2,1)S(1)}, f32[32,128]{1,0:T(8,128)S(1)}, f32[32,128]{1,0:T(8,128)S(1)}, f32[32,128]{1,0:T(8,128)S(1)}) custom-call(s32[256]{0:T(256)S(1)} %reshape.66.place_ref, s32[32]{0:T(128)S(1)} %slice_reduce_fusion.1.count_ref, s32[256]{0:T(256)S(1)} %reshape.67.table_ref, bf16[128,32,128]{2,1,0:T(8,128)(2,1)S(1)} %shard_map.46.refs_0_, ...), custom_call_target="tpu_custom_call" | custom-call | flops 268435456 | bytes 8388608 | tf_op jit(solution)/shard_map/pallas_call | solution.py:141
  81.8 2.1 %collective-permute-start.7 = (bf16[32,32,128]{2,1,0:T(8,128)(2,1)S(1)}, bf16[32,32,128]{2,1,0:T(8,128)(2,1)S(1)}, u32[]{:S(2)}, u32[]{:S(2)}) collective-permute-start(bf16[32,32,128]{2,1,0:T(8,128)(2,1)S(1)} %get-tuple-element.19.refs_0_), channel_id=1, source_target_pairs={{8,0},{3,1},{10,2},{5,3},{12,4},{7,5},{14,6},{1,7},{16,8},{11,9},{... | collective-permute-start | bytes 786440 | tf_op jit(solution)/shard_map/ppermute | solution.py:31
  85.6 3.1 %collective-permute-done.8.refs_2_ = bf16[32,32,128]{2,1,0:T(8,128)(2,1)S(1)} collective-permute-done((bf16[32,32,128]{2,1,0:T(8,128)(2,1)S(1)}, bf16[32,32,128]{2,1,0:T(8,128)(2,1)S(1)}, u32[]{:S(2)}, u32[]{:S(2)}) %collective-permute-start.8) | collective-permute-done | bytes 262176 | tf_op jit(solution)/shard_map/ppermute | solution.py:31
  88.6 2.4 %collective-permute-done.7.refs_1_ = bf16[32,32,128]{2,1,0:T(8,128)(2,1)S(1)} collective-permute-done((bf16[32,32,128]{2,1,0:T(8,128)(2,1)S(1)}, bf16[32,32,128]{2,1,0:T(8,128)(2,1)S(1)}, u32[]{:S(2)}, u32[]{:S(2)}) %collective-permute-start.7) | collective-permute-done | bytes 262176 | tf_op jit(solution)/shard_map/ppermute | solution.py:31
  94.7 3.0 %collective-permute-start.21 = (bf16[128,16,128]{2,1,0:T(8,128)(2,1)S(1)}, bf16[128,16,128]{2,1,0:T(8,128)(2,1)S(1)}, u32[]{:S(2)}, u32[]{:S(2)}) collective-permute-start(bf16[128,16,128]{2,1,0:T(8,128)(2,1)S(1)} %get-tuple-element.24.refs_0_), channel_id=1, source_target_pairs={{2,0},{9,1},{4,2},{11,3},{6,4},{13,5},{0,6},{15,7},{10,8},{17,9},{... | collective-permute-start | bytes 1572872 | tf_op jit(solution)/shard_map/ppermute | solution.py:31
  97.6 3.9 %collective-permute-done.12.refs_4_ = bf16[128,16,128]{2,1,0:T(8,128)(2,1)S(1)} collective-permute-done((bf16[128,16,128]{2,1,0:T(8,128)(2,1)S(1)}, bf16[128,16,128]{2,1,0:T(8,128)(2,1)S(1)}, u32[]{:S(2)}, u32[]{:S(2)}) %collective-permute-start.12) | collective-permute-done | bytes 524320 | tf_op jit(solution)/shard_map/ppermute | solution.py:31
  101.9 3.0 %collective-permute-start.11 = (bf16[64,16,128]{2,1,0:T(8,128)(2,1)S(1)}, bf16[64,16,128]{2,1,0:T(8,128)(2,1)S(1)}, u32[]{:S(2)}, u32[]{:S(2)}) collective-permute-start(bf16[64,16,128]{2,1,0:T(8,128)(2,1)S(1)} %slice.74), channel_id=1, source_target_pairs={{2,0},{9,1},{4,2},{11,3},{6,4},{13,5},{0,6},{15,7},{10,8},{17,9},{... | collective-permute-start | bytes 786440 | tf_op jit(solution)/shard_map/ppermute | solution.py:31
  105.0 2.2 %collective-permute-done.23.refs_4_ = bf16[128,16,128]{2,1,0:T(8,128)(2,1)S(1)} collective-permute-done((bf16[128,16,128]{2,1,0:T(8,128)(2,1)S(1)}, bf16[128,16,128]{2,1,0:T(8,128)(2,1)S(1)}, u32[]{:S(2)}, u32[]{:S(2)}) %collective-permute-start.23) | collective-permute-done | bytes 524320 | tf_op jit(solution)/shard_map/ppermute | solution.py:31
  107.6 3.0 %collective-permute-start.22 = (bf16[64,16,128]{2,1,0:T(8,128)(2,1)S(1)}, bf16[64,16,128]{2,1,0:T(8,128)(2,1)S(1)}, u32[]{:S(2)}, u32[]{:S(2)}) collective-permute-start(bf16[64,16,128]{2,1,0:T(8,128)(2,1)S(1)} %slice.78), channel_id=1, source_target_pairs={{2,0},{9,1},{4,2},{11,3},{6,4},{13,5},{0,6},{15,7},{10,8},{17,9},{... | collective-permute-start | bytes 786440 | tf_op jit(solution)/shard_map/ppermute | solution.py:31
  110.6 2.2 %shard_map.49 = (bf16[32,16,128]{2,1,0:T(8,128)(2,1)S(1)}, f32[16,128]{1,0:T(8,128)S(1)}) custom-call(s32[256]{0:T(256)S(1)} %reshape.66.place_ref, s32[32]{0:T(128)S(1)} %slice_reduce_fusion.1.count_ref, s32[256]{0:T(256)S(1)} %reshape.67.table_ref, bf16[128,16,128]{2,1,0:T(8,128)(2,1)S(1)} %get-tuple-element.20.refs_0_, ...), custom_call_target="tpu_custom_call" | custom-call | flops 134217728 | bytes 8388608 | tf_op jit(solution)/shard_map/pallas_call | solution.py:141
  115.0 2.0 %collective-permute-start.14 = (bf16[32,16,128]{2,1,0:T(8,128)(2,1)S(1)}, bf16[32,16,128]{2,1,0:T(8,128)(2,1)S(1)}, u32[]{:S(2)}, u32[]{:S(2)}) collective-permute-start(bf16[32,16,128]{2,1,0:T(8,128)(2,1)S(1)} %get-tuple-element.22.refs_0_), channel_id=1, source_target_pairs={{8,0},{3,1},{10,2},{5,3},{12,4},{7,5},{14,6},{1,7},{16,8},{11,9},{... | collective-permute-start | bytes 393224 | tf_op jit(solution)/shard_map/ppermute | solution.py:31
  117.0 2.2 %shard_map.52 = (bf16[32,16,128]{2,1,0:T(8,128)(2,1)S(1)}, f32[16,128]{1,0:T(8,128)S(1)}) custom-call(s32[256]{0:T(256)S(1)} %reshape.66.place_ref, s32[32]{0:T(128)S(1)} %slice_reduce_fusion.1.count_ref, s32[256]{0:T(256)S(1)} %reshape.67.table_ref, bf16[128,16,128]{2,1,0:T(8,128)(2,1)S(1)} %get-tuple-element.24.refs_0_, ...), custom_call_target="tpu_custom_call" | custom-call | flops 134217728 | bytes 8388608 | tf_op jit(solution)/shard_map/pallas_call | solution.py:141
  119.4 3.5 %collective-permute-start.26 = (bf16[32,16,128]{2,1,0:T(8,128)(2,1)S(1)}, bf16[32,16,128]{2,1,0:T(8,128)(2,1)S(1)}, u32[]{:S(2)}, u32[]{:S(2)}) collective-permute-start(bf16[32,16,128]{2,1,0:T(8,128)(2,1)S(1)} %get-tuple-element.25.refs_0_), channel_id=1, source_target_pairs={{16,0},{5,1},{18,2},{7,3},{20,4},{1,5},{22,6},{3,7},{24,8},{13,9},... | collective-permute-start | bytes 393224 | tf_op jit(solution)/shard_map/ppermute | solution.py:31
  124.2 2.1 %collective-permute-start.17 = (bf16[128,16,128]{2,1,0:T(8,128)(2,1)S(1)}, bf16[128,16,128]{2,1,0:T(8,128)(2,1)S(1)}, u32[]{:S(2)}, u32[]{:S(2)}) collective-permute-start(bf16[128,16,128]{2,1,0:T(8,128)(2,1)S(1)} %shard_map.50.refs_0_), channel_id=1, source_target_pairs={{2,0},{9,1},{4,2},{11,3},{6,4},{13,5},{0,6},{15,7},{10,8},{17,9},{... | collective-permute-start | bytes 1572872 | tf_op jit(solution)/shard_map/ppermute | solution.py:31
  127.2 2.5 %collective-permute-done.25.refs_1_ = bf16[32,16,128]{2,1,0:T(8,128)(2,1)S(1)} collective-permute-done((bf16[32,16,128]{2,1,0:T(8,128)(2,1)S(1)}, bf16[32,16,128]{2,1,0:T(8,128)(2,1)S(1)}, u32[]{:S(2)}, u32[]{:S(2)}) %collective-permute-start.25) | collective-permute-done | bytes 131104 | tf_op jit(solution)/shard_map/ppermute | solution.py:31
  130.9 2.3 %collective-permute-start.28 = (bf16[128,16,128]{2,1,0:T(8,128)(2,1)S(1)}, bf16[128,16,128]{2,1,0:T(8,128)(2,1)S(1)}, u32[]{:S(2)}, u32[]{:S(2)}) collective-permute-start(bf16[128,16,128]{2,1,0:T(8,128)(2,1)S(1)} %shard_map.53.refs_0_), channel_id=1, source_target_pairs={{2,0},{9,1},{4,2},{11,3},{6,4},{13,5},{0,6},{15,7},{10,8},{17,9},{... | collective-permute-start | bytes 1572872 | tf_op jit(solution)/shard_map/ppermute | solution.py:31
  133.8 3.3 %collective-permute-start.18 = (bf16[64,16,128]{2,1,0:T(8,128)(2,1)S(1)}, bf16[64,16,128]{2,1,0:T(8,128)(2,1)S(1)}, u32[]{:S(2)}, u32[]{:S(2)}) collective-permute-start(bf16[64,16,128]{2,1,0:T(8,128)(2,1)S(1)} %slice.76), channel_id=1, source_target_pairs={{2,0},{9,1},{4,2},{11,3},{6,4},{13,5},{0,6},{15,7},{10,8},{17,9},{... | collective-permute-start | bytes 786440 | tf_op jit(solution)/shard_map/ppermute | solution.py:31
  137.1 3.2 %collective-permute-done.30.refs_4_ = bf16[128,16,128]{2,1,0:T(8,128)(2,1)S(1)} collective-permute-done((bf16[128,16,128]{2,1,0:T(8,128)(2,1)S(1)}, bf16[128,16,128]{2,1,0:T(8,128)(2,1)S(1)}, u32[]{:S(2)}, u32[]{:S(2)}) %collective-permute-start.30) | collective-permute-done | bytes 524320 | tf_op jit(solution)/shard_map/ppermute | solution.py:31
  140.4 3.3 %collective-permute-start.29 = (bf16[64,16,128]{2,1,0:T(8,128)(2,1)S(1)}, bf16[64,16,128]{2,1,0:T(8,128)(2,1)S(1)}, u32[]{:S(2)}, u32[]{:S(2)}) collective-permute-start(bf16[64,16,128]{2,1,0:T(8,128)(2,1)S(1)} %slice.80), channel_id=1, source_target_pairs={{2,0},{9,1},{4,2},{11,3},{6,4},{13,5},{0,6},{15,7},{10,8},{17,9},{... | collective-permute-start | bytes 786440 | tf_op jit(solution)/shard_map/ppermute | solution.py:31
  143.7 2.2 %shard_map.51 = (bf16[32,16,128]{2,1,0:T(8,128)(2,1)S(1)}, f32[16,128]{1,0:T(8,128)S(1)}) custom-call(s32[256]{0:T(256)S(1)} %reshape.66.place_ref, s32[32]{0:T(128)S(1)} %slice_reduce_fusion.1.count_ref, s32[256]{0:T(256)S(1)} %reshape.67.table_ref, bf16[128,16,128]{2,1,0:T(8,128)(2,1)S(1)} %shard_map.50.refs_0_, ...), custom_call_target="tpu_custom_call" | custom-call | flops 134217728 | bytes 8388608 | tf_op jit(solution)/shard_map/pallas_call | solution.py:141
  145.9 2.0 %collective-permute-done.31.refs_3_ = bf16[64,16,128]{2,1,0:T(8,128)(2,1)S(1)} collective-permute-done((bf16[64,16,128]{2,1,0:T(8,128)(2,1)S(1)}, bf16[64,16,128]{2,1,0:T(8,128)(2,1)S(1)}, u32[]{:S(2)}, u32[]{:S(2)}) %collective-permute-start.31) | collective-permute-done | bytes 262176 | tf_op jit(solution)/shard_map/ppermute | solution.py:31
  148.0 2.2 %shard_map.54 = (bf16[32,16,128]{2,1,0:T(8,128)(2,1)S(1)}, f32[16,128]{1,0:T(8,128)S(1)}) custom-call(s32[256]{0:T(256)S(1)} %reshape.66.place_ref, s32[32]{0:T(128)S(1)} %slice_reduce_fusion.1.count_ref, s32[256]{0:T(256)S(1)} %reshape.67.table_ref, bf16[128,16,128]{2,1,0:T(8,128)(2,1)S(1)} %shard_map.53.refs_0_, ...), custom_call_target="tpu_custom_call" | custom-call | flops 134217728 | bytes 8388608 | tf_op jit(solution)/shard_map/pallas_call | solution.py:141
  150.3 13.7 %all_to_all.36 = f32[16,1,128]{2,1,0:T(1,128)S(1)} all-to-all(f32[16,1,128]{2,1,0:T(1,128)S(1)} %broadcast_in_dim.27), channel_id=1, replica_groups=mesh['z'=8,'x'=4,'y'=4,'c'=2] {'x','y'}, dimensions={0} | all-to-all | bytes 16384 | tf_op jit(solution)/shard_map/all_to_all | solution.py:165
  164.3 17.3 %all_to_all.37 = bf16[32,32,128]{2,1,0:T(8,128)(2,1)S(1)} all-to-all(bf16[32,32,128]{2,1,0:T(8,128)(2,1)S(1)} %multiply_convert_fusion), channel_id=1, replica_groups=mesh['z'=8,'x'=4,'y'=4,'c'=2] {'z'}, dimensions={0} | all-to-all | bytes 524288 | tf_op jit(solution)/shard_map/all_to_all | solution.py:223
  (99 shorter events, 31.8 us)
Async XLA Ops:
  6.5 65.1 %all-gather.2.cloned.1.call-start = ((), (), s32[]{:S(2)}) async-start(), calls=%async_computation.5 | async-start | bytes 8912896 | tf_op jit(solution)/shard_map/all_gather | solution.py:174
  10.5 14.3 %all-to-all-start = ((bf16[2,8,16,512]{3,1,0,2:T(8,128)(2,1)}), bf16[2,8,16,512]{3,1,0,2:T(8,128)(2,1)S(1)}, u32[]{:S(2)}, u32[]{:S(2)}) async-start(bf16[2,8,16,512]{3,1,0,2:T(8,128)(2,1)} %copy.23), calls=%async_computation | async-start | bytes 524288 | tf_op jit(solution)/shard_map/all_to_all | solution.py:180
  26.1 13.6 %collective-permute-start.3 = (bf16[32,32,128]{2,1,0:T(8,128)(2,1)S(1)}, bf16[32,32,128]{2,1,0:T(8,128)(2,1)S(1)}, u32[]{:S(2)}, u32[]{:S(2)}) collective-permute-start(bf16[32,32,128]{2,1,0:T(8,128)(2,1)S(1)} %bitcast.36), channel_id=1, source_target_pairs={{24,0},{7,1},{26,2},{1,3},{28,4},{3,5},{30,6},{5,7},{0,8},{15,9},{... | collective-permute-start | bytes 786440 | tf_op jit(solution)/shard_map/ppermute | solution.py:31
  27.2 12.5 %collective-permute-start.2 = (bf16[32,32,128]{2,1,0:T(8,128)(2,1)S(1)}, bf16[32,32,128]{2,1,0:T(8,128)(2,1)S(1)}, u32[]{:S(2)}, u32[]{:S(2)}) collective-permute-start(bf16[32,32,128]{2,1,0:T(8,128)(2,1)S(1)} %bitcast.37), channel_id=1, source_target_pairs={{16,0},{5,1},{18,2},{7,3},{20,4},{1,5},{22,6},{3,7},{24,8},{13,9},... | collective-permute-start | bytes 786440 | tf_op jit(solution)/shard_map/ppermute | solution.py:31
  30.0 9.6 %collective-permute-start.1 = (bf16[32,32,128]{2,1,0:T(8,128)(2,1)S(1)}, bf16[32,32,128]{2,1,0:T(8,128)(2,1)S(1)}, u32[]{:S(2)}, u32[]{:S(2)}) collective-permute-start(bf16[32,32,128]{2,1,0:T(8,128)(2,1)S(1)} %bitcast.38), channel_id=1, source_target_pairs={{8,0},{3,1},{10,2},{5,3},{12,4},{7,5},{14,6},{1,7},{16,8},{11,9},{... | collective-permute-start | bytes 786440 | tf_op jit(solution)/shard_map/ppermute | solution.py:31
  31.2 20.4 %all-to-all-start.1 = ((f32[8,40,128]{2,1,0:T(8,128)}), f32[8,40,128]{2,1,0:T(8,128)S(1)}, u32[]{:S(2)}, u32[]{:S(2)}) async-start(f32[8,40,128]{2,1,0:T(8,128)} %broadcast_in_dim.11), calls=%async_computation.1 | async-start | bytes 327680 | tf_op jit(solution)/shard_map/all_to_all | solution.py:165
  39.8 30.9 %collective-permute-start.6 = (bf16[128,32,128]{2,1,0:T(8,128)(2,1)S(1)}, bf16[128,32,128]{2,1,0:T(8,128)(2,1)S(1)}, u32[]{:S(2)}, u32[]{:S(2)}) collective-permute-start(bf16[128,32,128]{2,1,0:T(8,128)(2,1)S(1)} %shard_map.46.refs_0_), channel_id=1, source_target_pairs={{6,0},{25,1},{0,2},{27,3},{2,4},{29,5},{4,6},{31,7},{14,8},{1,9},{... | collective-permute-start | bytes 3145736 | tf_op jit(solution)/shard_map/ppermute | solution.py:31
  40.4 30.2 %collective-permute-start.5 = (bf16[128,32,128]{2,1,0:T(8,128)(2,1)S(1)}, bf16[128,32,128]{2,1,0:T(8,128)(2,1)}, u32[]{:S(2)}, u32[]{:S(2)}) collective-permute-start(bf16[128,32,128]{2,1,0:T(8,128)(2,1)S(1)} %shard_map.46.refs_0_), channel_id=1, source_target_pairs={{4,0},{17,1},{6,2},{19,3},{0,4},{21,5},{2,6},{23,7},{12,8},{25,9},... | collective-permute-start | bytes 3145736 | tf_op jit(solution)/shard_map/ppermute | solution.py:31
  42.2 28.4 %collective-permute-start.4 = (bf16[128,32,128]{2,1,0:T(8,128)(2,1)S(1)}, bf16[128,32,128]{2,1,0:T(8,128)(2,1)}, u32[]{:S(2)}, u32[]{:S(2)}) collective-permute-start(bf16[128,32,128]{2,1,0:T(8,128)(2,1)S(1)} %shard_map.46.refs_0_), channel_id=1, source_target_pairs={{2,0},{9,1},{4,2},{11,3},{6,4},{13,5},{0,6},{15,7},{10,8},{17,9},{... | collective-permute-start | bytes 3145736 | tf_op jit(solution)/shard_map/ppermute | solution.py:31
  52.5 18.1 %all-to-all-start.2 = ((f32[16,32,128]{2,1,0:T(8,128)}), f32[16,32,128]{2,1,0:T(8,128)S(1)}, u32[]{:S(2)}, u32[]{:S(2)}) async-start(f32[16,32,128]{2,1,0:T(8,128)} %broadcast_in_dim.12), calls=%async_computation.2 | async-start | bytes 524288 | tf_op jit(solution)/shard_map/all_to_all | solution.py:165
  80.7 8.0 %collective-permute-start.8 = (bf16[32,32,128]{2,1,0:T(8,128)(2,1)S(1)}, bf16[32,32,128]{2,1,0:T(8,128)(2,1)S(1)}, u32[]{:S(2)}, u32[]{:S(2)}) collective-permute-start(bf16[32,32,128]{2,1,0:T(8,128)(2,1)S(1)} %get-tuple-element.19.refs_0_), channel_id=1, source_target_pairs={{16,0},{5,1},{18,2},{7,3},{20,4},{1,5},{22,6},{3,7},{24,8},{13,9},... | collective-permute-start | bytes 786440 | tf_op jit(solution)/shard_map/ppermute | solution.py:31
  81.8 9.2 %collective-permute-start.7 = (bf16[32,32,128]{2,1,0:T(8,128)(2,1)S(1)}, bf16[32,32,128]{2,1,0:T(8,128)(2,1)S(1)}, u32[]{:S(2)}, u32[]{:S(2)}) collective-permute-start(bf16[32,32,128]{2,1,0:T(8,128)(2,1)S(1)} %get-tuple-element.19.refs_0_), channel_id=1, source_target_pairs={{8,0},{3,1},{10,2},{5,3},{12,4},{7,5},{14,6},{1,7},{16,8},{11,9},{... | collective-permute-start | bytes 786440 | tf_op jit(solution)/shard_map/ppermute | solution.py:31
  91.1 10.5 %collective-permute-start.12 = (bf16[128,16,128]{2,1,0:T(8,128)(2,1)S(1)}, bf16[128,16,128]{2,1,0:T(8,128)(2,1)S(1)}, u32[]{:S(2)}, u32[]{:S(2)}) collective-permute-start(bf16[128,16,128]{2,1,0:T(8,128)(2,1)S(1)} %get-tuple-element.20.refs_0_), channel_id=1, source_target_pairs={{6,0},{25,1},{0,2},{27,3},{2,4},{29,5},{4,6},{31,7},{14,8},{1,9},{... | collective-permute-start | bytes 1572872 | tf_op jit(solution)/shard_map/ppermute | solution.py:31
  92.6 9.3 %collective-permute-start.10 = (bf16[128,16,128]{2,1,0:T(8,128)(2,1)S(1)}, bf16[128,16,128]{2,1,0:T(8,128)(2,1)S(1)}, u32[]{:S(2)}, u32[]{:S(2)}) collective-permute-start(bf16[128,16,128]{2,1,0:T(8,128)(2,1)S(1)} %get-tuple-element.20.refs_0_), channel_id=1, source_target_pairs={{2,0},{9,1},{4,2},{11,3},{6,4},{13,5},{0,6},{15,7},{10,8},{17,9},{... | collective-permute-start | bytes 1572872 | tf_op jit(solution)/shard_map/ppermute | solution.py:31
  94.4 12.8 %collective-permute-start.23 = (bf16[128,16,128]{2,1,0:T(8,128)(2,1)S(1)}, bf16[128,16,128]{2,1,0:T(8,128)(2,1)S(1)}, u32[]{:S(2)}, u32[]{:S(2)}) collective-permute-start(bf16[128,16,128]{2,1,0:T(8,128)(2,1)S(1)} %get-tuple-element.24.refs_0_), channel_id=1, source_target_pairs={{6,0},{25,1},{0,2},{27,3},{2,4},{29,5},{4,6},{31,7},{14,8},{1,9},{... | collective-permute-start | bytes 1572872 | tf_op jit(solution)/shard_map/ppermute | solution.py:31
  94.7 12.9 %collective-permute-start.21 = (bf16[128,16,128]{2,1,0:T(8,128)(2,1)S(1)}, bf16[128,16,128]{2,1,0:T(8,128)(2,1)S(1)}, u32[]{:S(2)}, u32[]{:S(2)}) collective-permute-start(bf16[128,16,128]{2,1,0:T(8,128)(2,1)S(1)} %get-tuple-element.24.refs_0_), channel_id=1, source_target_pairs={{2,0},{9,1},{4,2},{11,3},{6,4},{13,5},{0,6},{15,7},{10,8},{17,9},{... | collective-permute-start | bytes 1572872 | tf_op jit(solution)/shard_map/ppermute | solution.py:31
  101.6 9.0 %collective-permute-start.13 = (bf16[64,16,128]{2,1,0:T(8,128)(2,1)S(1)}, bf16[64,16,128]{2,1,0:T(8,128)(2,1)S(1)}, u32[]{:S(2)}, u32[]{:S(2)}) collective-permute-start(bf16[64,16,128]{2,1,0:T(8,128)(2,1)S(1)} %slice.75), channel_id=1, source_target_pairs={{6,0},{25,1},{0,2},{27,3},{2,4},{29,5},{4,6},{31,7},{14,8},{1,9},{... | collective-permute-start | bytes 786440 | tf_op jit(solution)/shard_map/ppermute | solution.py:31
  101.9 8.7 %collective-permute-start.11 = (bf16[64,16,128]{2,1,0:T(8,128)(2,1)S(1)}, bf16[64,16,128]{2,1,0:T(8,128)(2,1)S(1)}, u32[]{:S(2)}, u32[]{:S(2)}) collective-permute-start(bf16[64,16,128]{2,1,0:T(8,128)(2,1)S(1)} %slice.74), channel_id=1, source_target_pairs={{2,0},{9,1},{4,2},{11,3},{6,4},{13,5},{0,6},{15,7},{10,8},{17,9},{... | collective-permute-start | bytes 786440 | tf_op jit(solution)/shard_map/ppermute | solution.py:31
  107.2 9.8 %collective-permute-start.24 = (bf16[64,16,128]{2,1,0:T(8,128)(2,1)S(1)}, bf16[64,16,128]{2,1,0:T(8,128)(2,1)S(1)}, u32[]{:S(2)}, u32[]{:S(2)}) collective-permute-start(bf16[64,16,128]{2,1,0:T(8,128)(2,1)S(1)} %slice.79), channel_id=1, source_target_pairs={{6,0},{25,1},{0,2},{27,3},{2,4},{29,5},{4,6},{31,7},{14,8},{1,9},{... | collective-permute-start | bytes 786440 | tf_op jit(solution)/shard_map/ppermute | solution.py:31
  107.6 9.5 %collective-permute-start.22 = (bf16[64,16,128]{2,1,0:T(8,128)(2,1)S(1)}, bf16[64,16,128]{2,1,0:T(8,128)(2,1)S(1)}, u32[]{:S(2)}, u32[]{:S(2)}) collective-permute-start(bf16[64,16,128]{2,1,0:T(8,128)(2,1)S(1)} %slice.78), channel_id=1, source_target_pairs={{2,0},{9,1},{4,2},{11,3},{6,4},{13,5},{0,6},{15,7},{10,8},{17,9},{... | collective-permute-start | bytes 786440 | tf_op jit(solution)/shard_map/ppermute | solution.py:31
  112.8 10.1 %collective-permute-start.16 = (bf16[32,16,128]{2,1,0:T(8,128)(2,1)S(1)}, bf16[32,16,128]{2,1,0:T(8,128)(2,1)S(1)}, u32[]{:S(2)}, u32[]{:S(2)}) collective-permute-start(bf16[32,16,128]{2,1,0:T(8,128)(2,1)S(1)} %get-tuple-element.22.refs_0_), channel_id=1, source_target_pairs={{24,0},{7,1},{26,2},{1,3},{28,4},{3,5},{30,6},{5,7},{0,8},{15,9},{... | collective-permute-start | bytes 393224 | tf_op jit(solution)/shard_map/ppermute | solution.py:31
  113.8 9.1 %collective-permute-start.15 = (bf16[32,16,128]{2,1,0:T(8,128)(2,1)S(1)}, bf16[32,16,128]{2,1,0:T(8,128)(2,1)S(1)}, u32[]{:S(2)}, u32[]{:S(2)}) collective-permute-start(bf16[32,16,128]{2,1,0:T(8,128)(2,1)S(1)} %get-tuple-element.22.refs_0_), channel_id=1, source_target_pairs={{16,0},{5,1},{18,2},{7,3},{20,4},{1,5},{22,6},{3,7},{24,8},{13,9},... | collective-permute-start | bytes 393224 | tf_op jit(solution)/shard_map/ppermute | solution.py:31
  115.0 7.9 %collective-permute-start.14 = (bf16[32,16,128]{2,1,0:T(8,128)(2,1)S(1)}, bf16[32,16,128]{2,1,0:T(8,128)(2,1)S(1)}, u32[]{:S(2)}, u32[]{:S(2)}) collective-permute-start(bf16[32,16,128]{2,1,0:T(8,128)(2,1)S(1)} %get-tuple-element.22.refs_0_), channel_id=1, source_target_pairs={{8,0},{3,1},{10,2},{5,3},{12,4},{7,5},{14,6},{1,7},{16,8},{11,9},{... | collective-permute-start | bytes 393224 | tf_op jit(solution)/shard_map/ppermute | solution.py:31
  119.4 7.8 %collective-permute-start.26 = (bf16[32,16,128]{2,1,0:T(8,128)(2,1)S(1)}, bf16[32,16,128]{2,1,0:T(8,128)(2,1)S(1)}, u32[]{:S(2)}, u32[]{:S(2)}) collective-permute-start(bf16[32,16,128]{2,1,0:T(8,128)(2,1)S(1)} %get-tuple-element.25.refs_0_), channel_id=1, source_target_pairs={{16,0},{5,1},{18,2},{7,3},{20,4},{1,5},{22,6},{3,7},{24,8},{13,9},... | collective-permute-start | bytes 393224 | tf_op jit(solution)/shard_map/ppermute | solution.py:31
  123.0 10.5 %collective-permute-start.19 = (bf16[128,16,128]{2,1,0:T(8,128)(2,1)S(1)}, bf16[128,16,128]{2,1,0:T(8,128)(2,1)S(1)}, u32[]{:S(2)}, u32[]{:S(2)}) collective-permute-start(bf16[128,16,128]{2,1,0:T(8,128)(2,1)S(1)} %shard_map.50.refs_0_), channel_id=1, source_target_pairs={{6,0},{25,1},{0,2},{27,3},{2,4},{29,5},{4,6},{31,7},{14,8},{1,9},{... | collective-permute-start | bytes 1572872 | tf_op jit(solution)/shard_map/ppermute | solution.py:31
  124.2 9.6 %collective-permute-start.17 = (bf16[128,16,128]{2,1,0:T(8,128)(2,1)S(1)}, bf16[128,16,128]{2,1,0:T(8,128)(2,1)S(1)}, u32[]{:S(2)}, u32[]{:S(2)}) collective-permute-start(bf16[128,16,128]{2,1,0:T(8,128)(2,1)S(1)} %shard_map.50.refs_0_), channel_id=1, source_target_pairs={{2,0},{9,1},{4,2},{11,3},{6,4},{13,5},{0,6},{15,7},{10,8},{17,9},{... | collective-permute-start | bytes 1572872 | tf_op jit(solution)/shard_map/ppermute | solution.py:31
  129.8 10.5 %collective-permute-start.30 = (bf16[128,16,128]{2,1,0:T(8,128)(2,1)S(1)}, bf16[128,16,128]{2,1,0:T(8,128)(2,1)S(1)}, u32[]{:S(2)}, u32[]{:S(2)}) collective-permute-start(bf16[128,16,128]{2,1,0:T(8,128)(2,1)S(1)} %shard_map.53.refs_0_), channel_id=1, source_target_pairs={{6,0},{25,1},{0,2},{27,3},{2,4},{29,5},{4,6},{31,7},{14,8},{1,9},{... | collective-permute-start | bytes 1572872 | tf_op jit(solution)/shard_map/ppermute | solution.py:31
  130.9 9.4 %collective-permute-start.28 = (bf16[128,16,128]{2,1,0:T(8,128)(2,1)S(1)}, bf16[128,16,128]{2,1,0:T(8,128)(2,1)S(1)}, u32[]{:S(2)}, u32[]{:S(2)}) collective-permute-start(bf16[128,16,128]{2,1,0:T(8,128)(2,1)S(1)} %shard_map.53.refs_0_), channel_id=1, source_target_pairs={{2,0},{9,1},{4,2},{11,3},{6,4},{13,5},{0,6},{15,7},{10,8},{17,9},{... | collective-permute-start | bytes 1572872 | tf_op jit(solution)/shard_map/ppermute | solution.py:31
  133.4 10.3 %collective-permute-start.20 = (bf16[64,16,128]{2,1,0:T(8,128)(2,1)S(1)}, bf16[64,16,128]{2,1,0:T(8,128)(2,1)S(1)}, u32[]{:S(2)}, u32[]{:S(2)}) collective-permute-start(bf16[64,16,128]{2,1,0:T(8,128)(2,1)S(1)} %slice.77), channel_id=1, source_target_pairs={{6,0},{25,1},{0,2},{27,3},{2,4},{29,5},{4,6},{31,7},{14,8},{1,9},{... | collective-permute-start | bytes 786440 | tf_op jit(solution)/shard_map/ppermute | solution.py:31
  133.8 9.9 %collective-permute-start.18 = (bf16[64,16,128]{2,1,0:T(8,128)(2,1)S(1)}, bf16[64,16,128]{2,1,0:T(8,128)(2,1)S(1)}, u32[]{:S(2)}, u32[]{:S(2)}) collective-permute-start(bf16[64,16,128]{2,1,0:T(8,128)(2,1)S(1)} %slice.76), channel_id=1, source_target_pairs={{2,0},{9,1},{4,2},{11,3},{6,4},{13,5},{0,6},{15,7},{10,8},{17,9},{... | collective-permute-start | bytes 786440 | tf_op jit(solution)/shard_map/ppermute | solution.py:31
  140.3 7.7 %collective-permute-start.31 = (bf16[64,16,128]{2,1,0:T(8,128)(2,1)S(1)}, bf16[64,16,128]{2,1,0:T(8,128)(2,1)S(1)}, u32[]{:S(2)}, u32[]{:S(2)}) collective-permute-start(bf16[64,16,128]{2,1,0:T(8,128)(2,1)S(1)} %slice.81), channel_id=1, source_target_pairs={{6,0},{25,1},{0,2},{27,3},{2,4},{29,5},{4,6},{31,7},{14,8},{1,9},{... | collective-permute-start | bytes 786440 | tf_op jit(solution)/shard_map/ppermute | solution.py:31
  140.4 7.5 %collective-permute-start.29 = (bf16[64,16,128]{2,1,0:T(8,128)(2,1)S(1)}, bf16[64,16,128]{2,1,0:T(8,128)(2,1)S(1)}, u32[]{:S(2)}, u32[]{:S(2)}) collective-permute-start(bf16[64,16,128]{2,1,0:T(8,128)(2,1)S(1)} %slice.80), channel_id=1, source_target_pairs={{2,0},{9,1},{4,2},{11,3},{6,4},{13,5},{0,6},{15,7},{10,8},{17,9},{... | collective-permute-start | bytes 786440 | tf_op jit(solution)/shard_map/ppermute | solution.py:31
  (7 other events, 66.0 us)
Sparse Core Ops, SparseCore 0:
  9.2 62.3 all-gather.1

commit v6 on v5

--- a/solution.py
+++ b/solution.py
@@ -13,7 +13,7 @@
 GROUP = 8
 BS = 128
 STREAMS = 2
-UNROLL = 16
+UNROLL = 32
 epsilon = 1e-06
 XY = ("x", "y")
 

time: 190 us -> 190 us (level)
  transfers between devices with their start and end apart: 36 -> 36, of which waited for: 14 -> 14; matrix products, arithmetic and copies ran while one was open for 3% -> 3% of each run, Pallas kernels for 4% -> 3%
where the time goes in v6:
time: 190 us
  starting transfers between devices  69.8 us (37%)
  waiting for transfers between devices  49.1 us (26%)
  blocking collectives  31 us (16%)
  between operations  13.7 us (7%)
  Pallas kernels  12.9 us (7%)
  local copies, waits for them, and re-layouts  11.7 us (6%)
    ppermute x31, starting transfers between devices, shift(): return lax.ppermute(value, ('x', 'y', 'c'), pairs)  48 us
    ppermute x31, waiting for transfers between devices, shift(): return lax.ppermute(value, ('x', 'y', 'c'), pairs)  22.5 us
    all_to_all x2, waiting for transfers between devices, to_all(): lax.all_to_all(jnp.broadcast_to(value[None], (size,) + value.shape), axis...  19.6 us
    all_to_all x1, blocking collectives, local(): result = lax.all_to_all(result, 'z', 0, 0, tiled=True)  17.3 us
    all_to_all x2, starting transfers between devices, to_all(): lax.all_to_all(jnp.broadcast_to(value[None], (size,) + value.shape), axis...  14.3 us
    all_to_all x1, blocking collectives, to_all(): lax.all_to_all(jnp.broadcast_to(value[None], (size,) + value.shape), axis...  13.7 us
    pallas_call x5, Pallas kernels, diffuse(): pl.pallas_call(functools.partial(step_kernel, n, raw, ends), in_specs=[sm...  12.6 us
    all_to_all x1, starting transfers between devices, local(): counted = lax.all_to_all(counted, XY, 2, 0, tiled=True)  7.48 us
  transfers between devices with their start and end apart: 36, of which 14 were waited for; matrix products, arithmetic and copies ran while one was open for 3% of the time, Pallas kernels for 3%

profile of v6, /device:TPU:2, one launch (start us, length us, event | category | flops | bytes accessed | tf_op | source)
XLA Modules:
  0.0 189.5 jit_solution(6767394995139302308)
XLA Ops:
  10.5 7.5 %all-to-all-start = ((bf16[2,8,16,512]{3,1,0,2:T(8,128)(2,1)}), bf16[2,8,16,512]{3,1,0,2:T(8,128)(2,1)S(1)}, u32[]{:S(2)}, u32[]{:S(2)}) async-start(bf16[2,8,16,512]{3,1,0,2:T(8,128)(2,1)} %copy.23), calls=%async_computation | async-start | bytes 524288 | tf_op jit(solution)/shard_map/all_to_all | solution.py:180
  18.7 6.1 %all-to-all-done = bf16[2,8,16,512]{3,1,0,2:T(8,128)(2,1)S(1)} async-done(((bf16[2,8,16,512]{3,1,0,2:T(8,128)(2,1)}), bf16[2,8,16,512]{3,1,0,2:T(8,128)(2,1)S(1)}, u32[]{:S(2)}, u32[]{:S(2)}) %all-to-all-start) | async-done | bytes 262176 | tf_op jit(solution)/shard_map/all_to_all | solution.py:180
  27.2 2.8 %collective-permute-start.2 = (bf16[32,32,128]{2,1,0:T(8,128)(2,1)S(1)}, bf16[32,32,128]{2,1,0:T(8,128)(2,1)S(1)}, u32[]{:S(2)}, u32[]{:S(2)}) collective-permute-start(bf16[32,32,128]{2,1,0:T(8,128)(2,1)S(1)} %bitcast.37), channel_id=1, source_target_pairs={{16,0},{5,1},{18,2},{7,3},{20,4},{1,5},{22,6},{3,7},{24,8},{13,9},... | collective-permute-start | bytes 786440 | tf_op jit(solution)/shard_map/ppermute | solution.py:31
  31.2 8.5 %all-to-all-start.1 = ((f32[8,40,128]{2,1,0:T(8,128)}), f32[8,40,128]{2,1,0:T(8,128)S(1)}, u32[]{:S(2)}, u32[]{:S(2)}) async-start(f32[8,40,128]{2,1,0:T(8,128)} %broadcast_in_dim.11), calls=%async_computation.1 | async-start | bytes 327680 | tf_op jit(solution)/shard_map/all_to_all | solution.py:165
  43.9 7.7 %all-to-all-done.1 = f32[8,40,128]{2,1,0:T(8,128)S(1)} async-done(((f32[8,40,128]{2,1,0:T(8,128)}), f32[8,40,128]{2,1,0:T(8,128)S(1)}, u32[]{:S(2)}, u32[]{:S(2)}) %all-to-all-start.1) | async-done | bytes 163872 | tf_op jit(solution)/shard_map/all_to_all | solution.py:165
  52.5 5.8 %all-to-all-start.2 = ((f32[16,32,128]{2,1,0:T(8,128)}), f32[16,32,128]{2,1,0:T(8,128)S(1)}, u32[]{:S(2)}, u32[]{:S(2)}) async-start(f32[16,32,128]{2,1,0:T(8,128)} %broadcast_in_dim.12), calls=%async_computation.2 | async-start | bytes 524288 | tf_op jit(solution)/shard_map/all_to_all | solution.py:165
  58.8 11.8 %all-to-all-done.2 = f32[16,32,128]{2,1,0:T(8,128)S(1)} async-done(((f32[16,32,128]{2,1,0:T(8,128)}), f32[16,32,128]{2,1,0:T(8,128)S(1)}, u32[]{:S(2)}, u32[]{:S(2)}) %all-to-all-start.2) | async-done | bytes 262176 | tf_op jit(solution)/shard_map/all_to_all | solution.py:165
  71.6 3.4 %copy-done.1 = bf16[32,8,128,128]{3,2,1,0:T(8,128)(2,1)S(1)} copy-done((bf16[32,8,128,128]{3,2,1,0:T(8,128)(2,1)S(1)}, bf16[32,8,128,128]{3,2,1,0:T(8,128)(2,1)}, u32[]{:S(2)}) %copy-start.1) | copy-done | bytes 8388632
  75.0 4.1 %shard_map.47 = (bf16[32,32,128]{2,1,0:T(8,128)(2,1)S(1)}, f32[32,128]{1,0:T(8,128)S(1)}, f32[32,128]{1,0:T(8,128)S(1)}, f32[32,128]{1,0:T(8,128)S(1)}) custom-call(s32[256]{0:T(256)S(1)} %reshape.66.place_ref, s32[32]{0:T(128)S(1)} %slice_reduce_fusion.1.count_ref, s32[256]{0:T(256)S(1)} %reshape.67.table_ref, bf16[128,32,128]{2,1,0:T(8,128)(2,1)S(1)} %shard_map.46.refs_0_, ...), custom_call_target="tpu_custom_call" | custom-call | flops 268435456 | bytes 8388608 | tf_op jit(solution)/shard_map/pallas_call | solution.py:141
  81.8 2.1 %collective-permute-start.7 = (bf16[32,32,128]{2,1,0:T(8,128)(2,1)S(1)}, bf16[32,32,128]{2,1,0:T(8,128)(2,1)S(1)}, u32[]{:S(2)}, u32[]{:S(2)}) collective-permute-start(bf16[32,32,128]{2,1,0:T(8,128)(2,1)S(1)} %get-tuple-element.19.refs_0_), channel_id=1, source_target_pairs={{8,0},{3,1},{10,2},{5,3},{12,4},{7,5},{14,6},{1,7},{16,8},{11,9},{... | collective-permute-start | bytes 786440 | tf_op jit(solution)/shard_map/ppermute | solution.py:31
  85.5 3.1 %collective-permute-done.8.refs_2_ = bf16[32,32,128]{2,1,0:T(8,128)(2,1)S(1)} collective-permute-done((bf16[32,32,128]{2,1,0:T(8,128)(2,1)S(1)}, bf16[32,32,128]{2,1,0:T(8,128)(2,1)S(1)}, u32[]{:S(2)}, u32[]{:S(2)}) %collective-permute-start.8) | collective-permute-done | bytes 262176 | tf_op jit(solution)/shard_map/ppermute | solution.py:31
  88.6 2.4 %collective-permute-done.7.refs_1_ = bf16[32,32,128]{2,1,0:T(8,128)(2,1)S(1)} collective-permute-done((bf16[32,32,128]{2,1,0:T(8,128)(2,1)S(1)}, bf16[32,32,128]{2,1,0:T(8,128)(2,1)S(1)}, u32[]{:S(2)}, u32[]{:S(2)}) %collective-permute-start.7) | collective-permute-done | bytes 262176 | tf_op jit(solution)/shard_map/ppermute | solution.py:31
  94.6 3.0 %collective-permute-start.21 = (bf16[128,16,128]{2,1,0:T(8,128)(2,1)S(1)}, bf16[128,16,128]{2,1,0:T(8,128)(2,1)S(1)}, u32[]{:S(2)}, u32[]{:S(2)}) collective-permute-start(bf16[128,16,128]{2,1,0:T(8,128)(2,1)S(1)} %get-tuple-element.24.refs_0_), channel_id=1, source_target_pairs={{2,0},{9,1},{4,2},{11,3},{6,4},{13,5},{0,6},{15,7},{10,8},{17,9},{... | collective-permute-start | bytes 1572872 | tf_op jit(solution)/shard_map/ppermute | solution.py:31
  97.6 3.9 %collective-permute-done.12.refs_4_ = bf16[128,16,128]{2,1,0:T(8,128)(2,1)S(1)} collective-permute-done((bf16[128,16,128]{2,1,0:T(8,128)(2,1)S(1)}, bf16[128,16,128]{2,1,0:T(8,128)(2,1)S(1)}, u32[]{:S(2)}, u32[]{:S(2)}) %collective-permute-start.12) | collective-permute-done | bytes 524320 | tf_op jit(solution)/shard_map/ppermute | solution.py:31
  101.9 3.0 %collective-permute-start.11 = (bf16[64,16,128]{2,1,0:T(8,128)(2,1)S(1)}, bf16[64,16,128]{2,1,0:T(8,128)(2,1)S(1)}, u32[]{:S(2)}, u32[]{:S(2)}) collective-permute-start(bf16[64,16,128]{2,1,0:T(8,128)(2,1)S(1)} %slice.74), channel_id=1, source_target_pairs={{2,0},{9,1},{4,2},{11,3},{6,4},{13,5},{0,6},{15,7},{10,8},{17,9},{... | collective-permute-start | bytes 786440 | tf_op jit(solution)/shard_map/ppermute | solution.py:31
  104.9 2.2 %collective-permute-done.23.refs_4_ = bf16[128,16,128]{2,1,0:T(8,128)(2,1)S(1)} collective-permute-done((bf16[128,16,128]{2,1,0:T(8,128)(2,1)S(1)}, bf16[128,16,128]{2,1,0:T(8,128)(2,1)S(1)}, u32[]{:S(2)}, u32[]{:S(2)}) %collective-permute-start.23) | collective-permute-done | bytes 524320 | tf_op jit(solution)/shard_map/ppermute | solution.py:31
  107.5 3.0 %collective-permute-start.22 = (bf16[64,16,128]{2,1,0:T(8,128)(2,1)S(1)}, bf16[64,16,128]{2,1,0:T(8,128)(2,1)S(1)}, u32[]{:S(2)}, u32[]{:S(2)}) collective-permute-start(bf16[64,16,128]{2,1,0:T(8,128)(2,1)S(1)} %slice.78), channel_id=1, source_target_pairs={{2,0},{9,1},{4,2},{11,3},{6,4},{13,5},{0,6},{15,7},{10,8},{17,9},{... | collective-permute-start | bytes 786440 | tf_op jit(solution)/shard_map/ppermute | solution.py:31
  110.6 2.1 %shard_map.49 = (bf16[32,16,128]{2,1,0:T(8,128)(2,1)S(1)}, f32[16,128]{1,0:T(8,128)S(1)}) custom-call(s32[256]{0:T(256)S(1)} %reshape.66.place_ref, s32[32]{0:T(128)S(1)} %slice_reduce_fusion.1.count_ref, s32[256]{0:T(256)S(1)} %reshape.67.table_ref, bf16[128,16,128]{2,1,0:T(8,128)(2,1)S(1)} %get-tuple-element.20.refs_0_, ...), custom_call_target="tpu_custom_call" | custom-call | flops 134217728 | bytes 8388608 | tf_op jit(solution)/shard_map/pallas_call | solution.py:141
  114.9 2.0 %collective-permute-start.14 = (bf16[32,16,128]{2,1,0:T(8,128)(2,1)S(1)}, bf16[32,16,128]{2,1,0:T(8,128)(2,1)S(1)}, u32[]{:S(2)}, u32[]{:S(2)}) collective-permute-start(bf16[32,16,128]{2,1,0:T(8,128)(2,1)S(1)} %get-tuple-element.22.refs_0_), channel_id=1, source_target_pairs={{8,0},{3,1},{10,2},{5,3},{12,4},{7,5},{14,6},{1,7},{16,8},{11,9},{... | collective-permute-start | bytes 393224 | tf_op jit(solution)/shard_map/ppermute | solution.py:31
  116.9 2.1 %shard_map.52 = (bf16[32,16,128]{2,1,0:T(8,128)(2,1)S(1)}, f32[16,128]{1,0:T(8,128)S(1)}) custom-call(s32[256]{0:T(256)S(1)} %reshape.66.place_ref, s32[32]{0:T(128)S(1)} %slice_reduce_fusion.1.count_ref, s32[256]{0:T(256)S(1)} %reshape.67.table_ref, bf16[128,16,128]{2,1,0:T(8,128)(2,1)S(1)} %get-tuple-element.24.refs_0_, ...), custom_call_target="tpu_custom_call" | custom-call | flops 134217728 | bytes 8388608 | tf_op jit(solution)/shard_map/pallas_call | solution.py:141
  119.4 3.4 %collective-permute-start.26 = (bf16[32,16,128]{2,1,0:T(8,128)(2,1)S(1)}, bf16[32,16,128]{2,1,0:T(8,128)(2,1)S(1)}, u32[]{:S(2)}, u32[]{:S(2)}) collective-permute-start(bf16[32,16,128]{2,1,0:T(8,128)(2,1)S(1)} %get-tuple-element.25.refs_0_), channel_id=1, source_target_pairs={{16,0},{5,1},{18,2},{7,3},{20,4},{1,5},{22,6},{3,7},{24,8},{13,9},... | collective-permute-start | bytes 393224 | tf_op jit(solution)/shard_map/ppermute | solution.py:31
  124.0 2.1 %collective-permute-start.17 = (bf16[128,16,128]{2,1,0:T(8,128)(2,1)S(1)}, bf16[128,16,128]{2,1,0:T(8,128)(2,1)S(1)}, u32[]{:S(2)}, u32[]{:S(2)}) collective-permute-start(bf16[128,16,128]{2,1,0:T(8,128)(2,1)S(1)} %shard_map.50.refs_0_), channel_id=1, source_target_pairs={{2,0},{9,1},{4,2},{11,3},{6,4},{13,5},{0,6},{15,7},{10,8},{17,9},{... | collective-permute-start | bytes 1572872 | tf_op jit(solution)/shard_map/ppermute | solution.py:31
  127.2 2.4 %collective-permute-done.25.refs_1_ = bf16[32,16,128]{2,1,0:T(8,128)(2,1)S(1)} collective-permute-done((bf16[32,16,128]{2,1,0:T(8,128)(2,1)S(1)}, bf16[32,16,128]{2,1,0:T(8,128)(2,1)S(1)}, u32[]{:S(2)}, u32[]{:S(2)}) %collective-permute-start.25) | collective-permute-done | bytes 131104 | tf_op jit(solution)/shard_map/ppermute | solution.py:31
  130.8 2.3 %collective-permute-start.28 = (bf16[128,16,128]{2,1,0:T(8,128)(2,1)S(1)}, bf16[128,16,128]{2,1,0:T(8,128)(2,1)S(1)}, u32[]{:S(2)}, u32[]{:S(2)}) collective-permute-start(bf16[128,16,128]{2,1,0:T(8,128)(2,1)S(1)} %shard_map.53.refs_0_), channel_id=1, source_target_pairs={{2,0},{9,1},{4,2},{11,3},{6,4},{13,5},{0,6},{15,7},{10,8},{17,9},{... | collective-permute-start | bytes 1572872 | tf_op jit(solution)/shard_map/ppermute | solution.py:31
  133.4 3.3 %collective-permute-start.18 = (bf16[64,16,128]{2,1,0:T(8,128)(2,1)S(1)}, bf16[64,16,128]{2,1,0:T(8,128)(2,1)S(1)}, u32[]{:S(2)}, u32[]{:S(2)}) collective-permute-start(bf16[64,16,128]{2,1,0:T(8,128)(2,1)S(1)} %slice.76), channel_id=1, source_target_pairs={{2,0},{9,1},{4,2},{11,3},{6,4},{13,5},{0,6},{15,7},{10,8},{17,9},{... | collective-permute-start | bytes 786440 | tf_op jit(solution)/shard_map/ppermute | solution.py:31
  136.7 3.5 %collective-permute-done.30.refs_4_ = bf16[128,16,128]{2,1,0:T(8,128)(2,1)S(1)} collective-permute-done((bf16[128,16,128]{2,1,0:T(8,128)(2,1)S(1)}, bf16[128,16,128]{2,1,0:T(8,128)(2,1)S(1)}, u32[]{:S(2)}, u32[]{:S(2)}) %collective-permute-start.30) | collective-permute-done | bytes 524320 | tf_op jit(solution)/shard_map/ppermute | solution.py:31
  140.3 3.3 %collective-permute-start.29 = (bf16[64,16,128]{2,1,0:T(8,128)(2,1)S(1)}, bf16[64,16,128]{2,1,0:T(8,128)(2,1)S(1)}, u32[]{:S(2)}, u32[]{:S(2)}) collective-permute-start(bf16[64,16,128]{2,1,0:T(8,128)(2,1)S(1)} %slice.80), channel_id=1, source_target_pairs={{2,0},{9,1},{4,2},{11,3},{6,4},{13,5},{0,6},{15,7},{10,8},{17,9},{... | collective-permute-start | bytes 786440 | tf_op jit(solution)/shard_map/ppermute | solution.py:31
  143.6 2.1 %shard_map.51 = (bf16[32,16,128]{2,1,0:T(8,128)(2,1)S(1)}, f32[16,128]{1,0:T(8,128)S(1)}) custom-call(s32[256]{0:T(256)S(1)} %reshape.66.place_ref, s32[32]{0:T(128)S(1)} %slice_reduce_fusion.1.count_ref, s32[256]{0:T(256)S(1)} %reshape.67.table_ref, bf16[128,16,128]{2,1,0:T(8,128)(2,1)S(1)} %shard_map.50.refs_0_, ...), custom_call_target="tpu_custom_call" | custom-call | flops 134217728 | bytes 8388608 | tf_op jit(solution)/shard_map/pallas_call | solution.py:141
  145.8 2.1 %collective-permute-done.31.refs_3_ = bf16[64,16,128]{2,1,0:T(8,128)(2,1)S(1)} collective-permute-done((bf16[64,16,128]{2,1,0:T(8,128)(2,1)S(1)}, bf16[64,16,128]{2,1,0:T(8,128)(2,1)S(1)}, u32[]{:S(2)}, u32[]{:S(2)}) %collective-permute-start.31) | collective-permute-done | bytes 262176 | tf_op jit(solution)/shard_map/ppermute | solution.py:31
  147.9 2.1 %shard_map.54 = (bf16[32,16,128]{2,1,0:T(8,128)(2,1)S(1)}, f32[16,128]{1,0:T(8,128)S(1)}) custom-call(s32[256]{0:T(256)S(1)} %reshape.66.place_ref, s32[32]{0:T(128)S(1)} %slice_reduce_fusion.1.count_ref, s32[256]{0:T(256)S(1)} %reshape.67.table_ref, bf16[128,16,128]{2,1,0:T(8,128)(2,1)S(1)} %shard_map.53.refs_0_, ...), custom_call_target="tpu_custom_call" | custom-call | flops 134217728 | bytes 8388608 | tf_op jit(solution)/shard_map/pallas_call | solution.py:141
  150.2 13.7 %all_to_all.36 = f32[16,1,128]{2,1,0:T(1,128)S(1)} all-to-all(f32[16,1,128]{2,1,0:T(1,128)S(1)} %broadcast_in_dim.27), channel_id=1, replica_groups=mesh['z'=8,'x'=4,'y'=4,'c'=2] {'x','y'}, dimensions={0} | all-to-all | bytes 16384 | tf_op jit(solution)/shard_map/all_to_all | solution.py:165
  164.2 17.3 %all_to_all.37 = bf16[32,32,128]{2,1,0:T(8,128)(2,1)S(1)} all-to-all(bf16[32,32,128]{2,1,0:T(8,128)(2,1)S(1)} %multiply_convert_fusion), channel_id=1, replica_groups=mesh['z'=8,'x'=4,'y'=4,'c'=2] {'z'}, dimensions={0} | all-to-all | bytes 524288 | tf_op jit(solution)/shard_map/all_to_all | solution.py:223
  (99 shorter events, 31.6 us)
Async XLA Ops:
  6.5 65.1 %all-gather.2.cloned.1.call-start = ((), (), s32[]{:S(2)}) async-start(), calls=%async_computation.5 | async-start | bytes 8912896 | tf_op jit(solution)/shard_map/all_gather | solution.py:174
  10.5 14.3 %all-to-all-start = ((bf16[2,8,16,512]{3,1,0,2:T(8,128)(2,1)}), bf16[2,8,16,512]{3,1,0,2:T(8,128)(2,1)S(1)}, u32[]{:S(2)}, u32[]{:S(2)}) async-start(bf16[2,8,16,512]{3,1,0,2:T(8,128)(2,1)} %copy.23), calls=%async_computation | async-start | bytes 524288 | tf_op jit(solution)/shard_map/all_to_all | solution.py:180
  26.1 13.6 %collective-permute-start.3 = (bf16[32,32,128]{2,1,0:T(8,128)(2,1)S(1)}, bf16[32,32,128]{2,1,0:T(8,128)(2,1)S(1)}, u32[]{:S(2)}, u32[]{:S(2)}) collective-permute-start(bf16[32,32,128]{2,1,0:T(8,128)(2,1)S(1)} %bitcast.36), channel_id=1, source_target_pairs={{24,0},{7,1},{26,2},{1,3},{28,4},{3,5},{30,6},{5,7},{0,8},{15,9},{... | collective-permute-start | bytes 786440 | tf_op jit(solution)/shard_map/ppermute | solution.py:31
  27.2 12.5 %collective-permute-start.2 = (bf16[32,32,128]{2,1,0:T(8,128)(2,1)S(1)}, bf16[32,32,128]{2,1,0:T(8,128)(2,1)S(1)}, u32[]{:S(2)}, u32[]{:S(2)}) collective-permute-start(bf16[32,32,128]{2,1,0:T(8,128)(2,1)S(1)} %bitcast.37), channel_id=1, source_target_pairs={{16,0},{5,1},{18,2},{7,3},{20,4},{1,5},{22,6},{3,7},{24,8},{13,9},... | collective-permute-start | bytes 786440 | tf_op jit(solution)/shard_map/ppermute | solution.py:31
  30.0 9.6 %collective-permute-start.1 = (bf16[32,32,128]{2,1,0:T(8,128)(2,1)S(1)}, bf16[32,32,128]{2,1,0:T(8,128)(2,1)S(1)}, u32[]{:S(2)}, u32[]{:S(2)}) collective-permute-start(bf16[32,32,128]{2,1,0:T(8,128)(2,1)S(1)} %bitcast.38), channel_id=1, source_target_pairs={{8,0},{3,1},{10,2},{5,3},{12,4},{7,5},{14,6},{1,7},{16,8},{11,9},{... | collective-permute-start | bytes 786440 | tf_op jit(solution)/shard_map/ppermute | solution.py:31
  31.2 20.4 %all-to-all-start.1 = ((f32[8,40,128]{2,1,0:T(8,128)}), f32[8,40,128]{2,1,0:T(8,128)S(1)}, u32[]{:S(2)}, u32[]{:S(2)}) async-start(f32[8,40,128]{2,1,0:T(8,128)} %broadcast_in_dim.11), calls=%async_computation.1 | async-start | bytes 327680 | tf_op jit(solution)/shard_map/all_to_all | solution.py:165
  39.8 30.9 %collective-permute-start.6 = (bf16[128,32,128]{2,1,0:T(8,128)(2,1)S(1)}, bf16[128,32,128]{2,1,0:T(8,128)(2,1)S(1)}, u32[]{:S(2)}, u32[]{:S(2)}) collective-permute-start(bf16[128,32,128]{2,1,0:T(8,128)(2,1)S(1)} %shard_map.46.refs_0_), channel_id=1, source_target_pairs={{6,0},{25,1},{0,2},{27,3},{2,4},{29,5},{4,6},{31,7},{14,8},{1,9},{... | collective-permute-start | bytes 3145736 | tf_op jit(solution)/shard_map/ppermute | solution.py:31
  40.4 30.2 %collective-permute-start.5 = (bf16[128,32,128]{2,1,0:T(8,128)(2,1)S(1)}, bf16[128,32,128]{2,1,0:T(8,128)(2,1)}, u32[]{:S(2)}, u32[]{:S(2)}) collective-permute-start(bf16[128,32,128]{2,1,0:T(8,128)(2,1)S(1)} %shard_map.46.refs_0_), channel_id=1, source_target_pairs={{4,0},{17,1},{6,2},{19,3},{0,4},{21,5},{2,6},{23,7},{12,8},{25,9},... | collective-permute-start | bytes 3145736 | tf_op jit(solution)/shard_map/ppermute | solution.py:31
  42.2 28.4 %collective-permute-start.4 = (bf16[128,32,128]{2,1,0:T(8,128)(2,1)S(1)}, bf16[128,32,128]{2,1,0:T(8,128)(2,1)}, u32[]{:S(2)}, u32[]{:S(2)}) collective-permute-start(bf16[128,32,128]{2,1,0:T(8,128)(2,1)S(1)} %shard_map.46.refs_0_), channel_id=1, source_target_pairs={{2,0},{9,1},{4,2},{11,3},{6,4},{13,5},{0,6},{15,7},{10,8},{17,9},{... | collective-permute-start | bytes 3145736 | tf_op jit(solution)/shard_map/ppermute | solution.py:31
  52.5 18.1 %all-to-all-start.2 = ((f32[16,32,128]{2,1,0:T(8,128)}), f32[16,32,128]{2,1,0:T(8,128)S(1)}, u32[]{:S(2)}, u32[]{:S(2)}) async-start(f32[16,32,128]{2,1,0:T(8,128)} %broadcast_in_dim.12), calls=%async_computation.2 | async-start | bytes 524288 | tf_op jit(solution)/shard_map/all_to_all | solution.py:165
  80.6 8.0 %collective-permute-start.8 = (bf16[32,32,128]{2,1,0:T(8,128)(2,1)S(1)}, bf16[32,32,128]{2,1,0:T(8,128)(2,1)S(1)}, u32[]{:S(2)}, u32[]{:S(2)}) collective-permute-start(bf16[32,32,128]{2,1,0:T(8,128)(2,1)S(1)} %get-tuple-element.19.refs_0_), channel_id=1, source_target_pairs={{16,0},{5,1},{18,2},{7,3},{20,4},{1,5},{22,6},{3,7},{24,8},{13,9},... | collective-permute-start | bytes 786440 | tf_op jit(solution)/shard_map/ppermute | solution.py:31
  81.8 9.2 %collective-permute-start.7 = (bf16[32,32,128]{2,1,0:T(8,128)(2,1)S(1)}, bf16[32,32,128]{2,1,0:T(8,128)(2,1)S(1)}, u32[]{:S(2)}, u32[]{:S(2)}) collective-permute-start(bf16[32,32,128]{2,1,0:T(8,128)(2,1)S(1)} %get-tuple-element.19.refs_0_), channel_id=1, source_target_pairs={{8,0},{3,1},{10,2},{5,3},{12,4},{7,5},{14,6},{1,7},{16,8},{11,9},{... | collective-permute-start | bytes 786440 | tf_op jit(solution)/shard_map/ppermute | solution.py:31
  91.0 10.5 %collective-permute-start.12 = (bf16[128,16,128]{2,1,0:T(8,128)(2,1)S(1)}, bf16[128,16,128]{2,1,0:T(8,128)(2,1)S(1)}, u32[]{:S(2)}, u32[]{:S(2)}) collective-permute-start(bf16[128,16,128]{2,1,0:T(8,128)(2,1)S(1)} %get-tuple-element.20.refs_0_), channel_id=1, source_target_pairs={{6,0},{25,1},{0,2},{27,3},{2,4},{29,5},{4,6},{31,7},{14,8},{1,9},{... | collective-permute-start | bytes 1572872 | tf_op jit(solution)/shard_map/ppermute | solution.py:31
  92.6 9.3 %collective-permute-start.10 = (bf16[128,16,128]{2,1,0:T(8,128)(2,1)S(1)}, bf16[128,16,128]{2,1,0:T(8,128)(2,1)S(1)}, u32[]{:S(2)}, u32[]{:S(2)}) collective-permute-start(bf16[128,16,128]{2,1,0:T(8,128)(2,1)S(1)} %get-tuple-element.20.refs_0_), channel_id=1, source_target_pairs={{2,0},{9,1},{4,2},{11,3},{6,4},{13,5},{0,6},{15,7},{10,8},{17,9},{... | collective-permute-start | bytes 1572872 | tf_op jit(solution)/shard_map/ppermute | solution.py:31
  94.3 12.8 %collective-permute-start.23 = (bf16[128,16,128]{2,1,0:T(8,128)(2,1)S(1)}, bf16[128,16,128]{2,1,0:T(8,128)(2,1)S(1)}, u32[]{:S(2)}, u32[]{:S(2)}) collective-permute-start(bf16[128,16,128]{2,1,0:T(8,128)(2,1)S(1)} %get-tuple-element.24.refs_0_), channel_id=1, source_target_pairs={{6,0},{25,1},{0,2},{27,3},{2,4},{29,5},{4,6},{31,7},{14,8},{1,9},{... | collective-permute-start | bytes 1572872 | tf_op jit(solution)/shard_map/ppermute | solution.py:31
  94.6 12.9 %collective-permute-start.21 = (bf16[128,16,128]{2,1,0:T(8,128)(2,1)S(1)}, bf16[128,16,128]{2,1,0:T(8,128)(2,1)S(1)}, u32[]{:S(2)}, u32[]{:S(2)}) collective-permute-start(bf16[128,16,128]{2,1,0:T(8,128)(2,1)S(1)} %get-tuple-element.24.refs_0_), channel_id=1, source_target_pairs={{2,0},{9,1},{4,2},{11,3},{6,4},{13,5},{0,6},{15,7},{10,8},{17,9},{... | collective-permute-start | bytes 1572872 | tf_op jit(solution)/shard_map/ppermute | solution.py:31
  101.5 9.0 %collective-permute-start.13 = (bf16[64,16,128]{2,1,0:T(8,128)(2,1)S(1)}, bf16[64,16,128]{2,1,0:T(8,128)(2,1)S(1)}, u32[]{:S(2)}, u32[]{:S(2)}) collective-permute-start(bf16[64,16,128]{2,1,0:T(8,128)(2,1)S(1)} %slice.75), channel_id=1, source_target_pairs={{6,0},{25,1},{0,2},{27,3},{2,4},{29,5},{4,6},{31,7},{14,8},{1,9},{... | collective-permute-start | bytes 786440 | tf_op jit(solution)/shard_map/ppermute | solution.py:31
  101.9 8.7 %collective-permute-start.11 = (bf16[64,16,128]{2,1,0:T(8,128)(2,1)S(1)}, bf16[64,16,128]{2,1,0:T(8,128)(2,1)S(1)}, u32[]{:S(2)}, u32[]{:S(2)}) collective-permute-start(bf16[64,16,128]{2,1,0:T(8,128)(2,1)S(1)} %slice.74), channel_id=1, source_target_pairs={{2,0},{9,1},{4,2},{11,3},{6,4},{13,5},{0,6},{15,7},{10,8},{17,9},{... | collective-permute-start | bytes 786440 | tf_op jit(solution)/shard_map/ppermute | solution.py:31
  107.1 9.8 %collective-permute-start.24 = (bf16[64,16,128]{2,1,0:T(8,128)(2,1)S(1)}, bf16[64,16,128]{2,1,0:T(8,128)(2,1)S(1)}, u32[]{:S(2)}, u32[]{:S(2)}) collective-permute-start(bf16[64,16,128]{2,1,0:T(8,128)(2,1)S(1)} %slice.79), channel_id=1, source_target_pairs={{6,0},{25,1},{0,2},{27,3},{2,4},{29,5},{4,6},{31,7},{14,8},{1,9},{... | collective-permute-start | bytes 786440 | tf_op jit(solution)/shard_map/ppermute | solution.py:31
  107.5 9.4 %collective-permute-start.22 = (bf16[64,16,128]{2,1,0:T(8,128)(2,1)S(1)}, bf16[64,16,128]{2,1,0:T(8,128)(2,1)S(1)}, u32[]{:S(2)}, u32[]{:S(2)}) collective-permute-start(bf16[64,16,128]{2,1,0:T(8,128)(2,1)S(1)} %slice.78), channel_id=1, source_target_pairs={{2,0},{9,1},{4,2},{11,3},{6,4},{13,5},{0,6},{15,7},{10,8},{17,9},{... | collective-permute-start | bytes 786440 | tf_op jit(solution)/shard_map/ppermute | solution.py:31
  112.7 10.0 %collective-permute-start.16 = (bf16[32,16,128]{2,1,0:T(8,128)(2,1)S(1)}, bf16[32,16,128]{2,1,0:T(8,128)(2,1)S(1)}, u32[]{:S(2)}, u32[]{:S(2)}) collective-permute-start(bf16[32,16,128]{2,1,0:T(8,128)(2,1)S(1)} %get-tuple-element.22.refs_0_), channel_id=1, source_target_pairs={{24,0},{7,1},{26,2},{1,3},{28,4},{3,5},{30,6},{5,7},{0,8},{15,9},{... | collective-permute-start | bytes 393224 | tf_op jit(solution)/shard_map/ppermute | solution.py:31
  113.7 9.0 %collective-permute-start.15 = (bf16[32,16,128]{2,1,0:T(8,128)(2,1)S(1)}, bf16[32,16,128]{2,1,0:T(8,128)(2,1)S(1)}, u32[]{:S(2)}, u32[]{:S(2)}) collective-permute-start(bf16[32,16,128]{2,1,0:T(8,128)(2,1)S(1)} %get-tuple-element.22.refs_0_), channel_id=1, source_target_pairs={{16,0},{5,1},{18,2},{7,3},{20,4},{1,5},{22,6},{3,7},{24,8},{13,9},... | collective-permute-start | bytes 393224 | tf_op jit(solution)/shard_map/ppermute | solution.py:31
  114.9 7.9 %collective-permute-start.14 = (bf16[32,16,128]{2,1,0:T(8,128)(2,1)S(1)}, bf16[32,16,128]{2,1,0:T(8,128)(2,1)S(1)}, u32[]{:S(2)}, u32[]{:S(2)}) collective-permute-start(bf16[32,16,128]{2,1,0:T(8,128)(2,1)S(1)} %get-tuple-element.22.refs_0_), channel_id=1, source_target_pairs={{8,0},{3,1},{10,2},{5,3},{12,4},{7,5},{14,6},{1,7},{16,8},{11,9},{... | collective-permute-start | bytes 393224 | tf_op jit(solution)/shard_map/ppermute | solution.py:31
  119.4 7.9 %collective-permute-start.26 = (bf16[32,16,128]{2,1,0:T(8,128)(2,1)S(1)}, bf16[32,16,128]{2,1,0:T(8,128)(2,1)S(1)}, u32[]{:S(2)}, u32[]{:S(2)}) collective-permute-start(bf16[32,16,128]{2,1,0:T(8,128)(2,1)S(1)} %get-tuple-element.25.refs_0_), channel_id=1, source_target_pairs={{16,0},{5,1},{18,2},{7,3},{20,4},{1,5},{22,6},{3,7},{24,8},{13,9},... | collective-permute-start | bytes 393224 | tf_op jit(solution)/shard_map/ppermute | solution.py:31
  122.8 10.5 %collective-permute-start.19 = (bf16[128,16,128]{2,1,0:T(8,128)(2,1)S(1)}, bf16[128,16,128]{2,1,0:T(8,128)(2,1)S(1)}, u32[]{:S(2)}, u32[]{:S(2)}) collective-permute-start(bf16[128,16,128]{2,1,0:T(8,128)(2,1)S(1)} %shard_map.50.refs_0_), channel_id=1, source_target_pairs={{6,0},{25,1},{0,2},{27,3},{2,4},{29,5},{4,6},{31,7},{14,8},{1,9},{... | collective-permute-start | bytes 1572872 | tf_op jit(solution)/shard_map/ppermute | solution.py:31
  124.0 9.4 %collective-permute-start.17 = (bf16[128,16,128]{2,1,0:T(8,128)(2,1)S(1)}, bf16[128,16,128]{2,1,0:T(8,128)(2,1)S(1)}, u32[]{:S(2)}, u32[]{:S(2)}) collective-permute-start(bf16[128,16,128]{2,1,0:T(8,128)(2,1)S(1)} %shard_map.50.refs_0_), channel_id=1, source_target_pairs={{2,0},{9,1},{4,2},{11,3},{6,4},{13,5},{0,6},{15,7},{10,8},{17,9},{... | collective-permute-start | bytes 1572872 | tf_op jit(solution)/shard_map/ppermute | solution.py:31
  129.7 10.5 %collective-permute-start.30 = (bf16[128,16,128]{2,1,0:T(8,128)(2,1)S(1)}, bf16[128,16,128]{2,1,0:T(8,128)(2,1)S(1)}, u32[]{:S(2)}, u32[]{:S(2)}) collective-permute-start(bf16[128,16,128]{2,1,0:T(8,128)(2,1)S(1)} %shard_map.53.refs_0_), channel_id=1, source_target_pairs={{6,0},{25,1},{0,2},{27,3},{2,4},{29,5},{4,6},{31,7},{14,8},{1,9},{... | collective-permute-start | bytes 1572872 | tf_op jit(solution)/shard_map/ppermute | solution.py:31
  130.8 9.5 %collective-permute-start.28 = (bf16[128,16,128]{2,1,0:T(8,128)(2,1)S(1)}, bf16[128,16,128]{2,1,0:T(8,128)(2,1)S(1)}, u32[]{:S(2)}, u32[]{:S(2)}) collective-permute-start(bf16[128,16,128]{2,1,0:T(8,128)(2,1)S(1)} %shard_map.53.refs_0_), channel_id=1, source_target_pairs={{2,0},{9,1},{4,2},{11,3},{6,4},{13,5},{0,6},{15,7},{10,8},{17,9},{... | collective-permute-start | bytes 1572872 | tf_op jit(solution)/shard_map/ppermute | solution.py:31
  133.3 10.3 %collective-permute-start.20 = (bf16[64,16,128]{2,1,0:T(8,128)(2,1)S(1)}, bf16[64,16,128]{2,1,0:T(8,128)(2,1)S(1)}, u32[]{:S(2)}, u32[]{:S(2)}) collective-permute-start(bf16[64,16,128]{2,1,0:T(8,128)(2,1)S(1)} %slice.77), channel_id=1, source_target_pairs={{6,0},{25,1},{0,2},{27,3},{2,4},{29,5},{4,6},{31,7},{14,8},{1,9},{... | collective-permute-start | bytes 786440 | tf_op jit(solution)/shard_map/ppermute | solution.py:31
  133.4 10.2 %collective-permute-start.18 = (bf16[64,16,128]{2,1,0:T(8,128)(2,1)S(1)}, bf16[64,16,128]{2,1,0:T(8,128)(2,1)S(1)}, u32[]{:S(2)}, u32[]{:S(2)}) collective-permute-start(bf16[64,16,128]{2,1,0:T(8,128)(2,1)S(1)} %slice.76), channel_id=1, source_target_pairs={{2,0},{9,1},{4,2},{11,3},{6,4},{13,5},{0,6},{15,7},{10,8},{17,9},{... | collective-permute-start | bytes 786440 | tf_op jit(solution)/shard_map/ppermute | solution.py:31
  140.2 7.7 %collective-permute-start.31 = (bf16[64,16,128]{2,1,0:T(8,128)(2,1)S(1)}, bf16[64,16,128]{2,1,0:T(8,128)(2,1)S(1)}, u32[]{:S(2)}, u32[]{:S(2)}) collective-permute-start(bf16[64,16,128]{2,1,0:T(8,128)(2,1)S(1)} %slice.81), channel_id=1, source_target_pairs={{6,0},{25,1},{0,2},{27,3},{2,4},{29,5},{4,6},{31,7},{14,8},{1,9},{... | collective-permute-start | bytes 786440 | tf_op jit(solution)/shard_map/ppermute | solution.py:31
  140.3 7.5 %collective-permute-start.29 = (bf16[64,16,128]{2,1,0:T(8,128)(2,1)S(1)}, bf16[64,16,128]{2,1,0:T(8,128)(2,1)S(1)}, u32[]{:S(2)}, u32[]{:S(2)}) collective-permute-start(bf16[64,16,128]{2,1,0:T(8,128)(2,1)S(1)} %slice.80), channel_id=1, source_target_pairs={{2,0},{9,1},{4,2},{11,3},{6,4},{13,5},{0,6},{15,7},{10,8},{17,9},{... | collective-permute-start | bytes 786440 | tf_op jit(solution)/shard_map/ppermute | solution.py:31
  (7 other events, 66.0 us)
Sparse Core Ops, SparseCore 0:
  9.2 62.3 all-gather.1

commit v7 on v5

--- a/solution.py
+++ b/solution.py
@@ -170,7 +170,8 @@
 def local(stored, neighbours, counts, affinity):
     core, my_x, my_y = lax.axis_index("c"), lax.axis_index("x"), lax.axis_index("y")
     blocks_dev, slots = neighbours.shape
-    part = lax.dynamic_slice_in_dim(affinity, core * (blocks_dev // 2), blocks_dev // 2, 0)
+    half = blocks_dev // 2
+    part = jnp.where(core == 0, affinity[:half], affinity[half:])
     affinity = lax.all_gather(part, ("z", "c"), tiled=True)
 
     genes_dev = stored.shape[0]

time: 190 us -> 190 us (level)
  local copies, waits for them, and re-layouts: 11.7 us -> 9.58 us
  other arithmetic: 1.41 us -> 3.46 us
    select_n x0 -> x1, other arithmetic: none -> 2.05 us  [local(): part = jnp.where(core == 0, affinity[:half], affinity[half:])]
    unnamed x8 -> x6, local copies, waits for them, and re-layouts: 6.42 us -> 5.19 us
where the time goes in v7:
time: 190 us; the launch traced here: 189 us
  starting transfers between devices  70.1 us (37%)
  waiting for transfers between devices  48.8 us (26%)
  blocking collectives  30.9 us (16%)
  between operations  13.7 us (7%)
  Pallas kernels  12.8 us (7%)
  local copies, waits for them, and re-layouts  9.58 us (5%)
  other arithmetic  3.46 us (2%)
    ppermute x31, starting transfers between devices, shift(): return lax.ppermute(value, ('x', 'y', 'c'), pairs)  48.2 us
    ppermute x31, waiting for transfers between devices, shift(): return lax.ppermute(value, ('x', 'y', 'c'), pairs)  22.1 us
    all_to_all x2, waiting for transfers between devices, to_all(): lax.all_to_all(jnp.broadcast_to(value[None], (size,) + value.shape), axis...  19.6 us
    all_to_all x1, blocking collectives, local(): result = lax.all_to_all(result, 'z', 0, 0, tiled=True)  17.2 us
    all_to_all x2, starting transfers between devices, to_all(): lax.all_to_all(jnp.broadcast_to(value[None], (size,) + value.shape), axis...  14.3 us
    all_to_all x1, blocking collectives, to_all(): lax.all_to_all(jnp.broadcast_to(value[None], (size,) + value.shape), axis...  13.7 us
    pallas_call x5, Pallas kernels, diffuse(): pl.pallas_call(functools.partial(step_kernel, n, raw, ends), in_specs=[sm...  12.6 us
    all_to_all x1, starting transfers between devices, local(): counted = lax.all_to_all(counted, XY, 2, 0, tiled=True)  7.48 us
  transfers between devices with their start and end apart: 36, of which 14 were waited for; matrix products, arithmetic and copies ran while one was open for 3% of the time, Pallas kernels for 4%

profile of v7, /device:TPU:2, one launch (start us, length us, event | category | flops | bytes accessed | tf_op | source)
XLA Modules:
  0.0 189.2 jit_solution(2663223604312273456)
XLA Ops:
  6.5 2.0 %slice_select_fusion = bf16[2,8,128,128]{3,2,1,0:T(8,128)(2,1)} fusion(bf16[4,8,128,128]{3,2,1,0:T(8,128)(2,1)} %param.7, pred[]{:T(512)S(6)} %eq.10), kind=kLoop, calls=%fused_computation.3 | loop fusion | flops 262144 | bytes 1572865 | tf_op jit(solution)/shard_map/jit(_where)/select_n | solution.py:174
  10.5 7.5 %all-to-all-start = ((bf16[2,8,16,512]{3,1,0,2:T(8,128)(2,1)}), bf16[2,8,16,512]{3,1,0,2:T(8,128)(2,1)S(1)}, u32[]{:S(2)}, u32[]{:S(2)}) async-start(bf16[2,8,16,512]{3,1,0,2:T(8,128)(2,1)} %copy.23), calls=%async_computation | async-start | bytes 524288 | tf_op jit(solution)/shard_map/all_to_all | solution.py:181
  18.7 6.1 %all-to-all-done = bf16[2,8,16,512]{3,1,0,2:T(8,128)(2,1)S(1)} async-done(((bf16[2,8,16,512]{3,1,0,2:T(8,128)(2,1)}), bf16[2,8,16,512]{3,1,0,2:T(8,128)(2,1)S(1)}, u32[]{:S(2)}, u32[]{:S(2)}) %all-to-all-start) | async-done | bytes 262176 | tf_op jit(solution)/shard_map/all_to_all | solution.py:181
  27.2 2.8 %collective-permute-start.2 = (bf16[32,32,128]{2,1,0:T(8,128)(2,1)S(1)}, bf16[32,32,128]{2,1,0:T(8,128)(2,1)S(1)}, u32[]{:S(2)}, u32[]{:S(2)}) collective-permute-start(bf16[32,32,128]{2,1,0:T(8,128)(2,1)S(1)} %bitcast.37), channel_id=1, source_target_pairs={{16,0},{5,1},{18,2},{7,3},{20,4},{1,5},{22,6},{3,7},{24,8},{13,9},... | collective-permute-start | bytes 786440 | tf_op jit(solution)/shard_map/ppermute | solution.py:31
  31.2 8.5 %all-to-all-start.1 = ((f32[8,40,128]{2,1,0:T(8,128)}), f32[8,40,128]{2,1,0:T(8,128)S(1)}, u32[]{:S(2)}, u32[]{:S(2)}) async-start(f32[8,40,128]{2,1,0:T(8,128)} %broadcast_in_dim.11), calls=%async_computation.1 | async-start | bytes 327680 | tf_op jit(solution)/shard_map/all_to_all | solution.py:165
  43.9 7.7 %all-to-all-done.1 = f32[8,40,128]{2,1,0:T(8,128)S(1)} async-done(((f32[8,40,128]{2,1,0:T(8,128)}), f32[8,40,128]{2,1,0:T(8,128)S(1)}, u32[]{:S(2)}, u32[]{:S(2)}) %all-to-all-start.1) | async-done | bytes 163872 | tf_op jit(solution)/shard_map/all_to_all | solution.py:165
  52.5 5.8 %all-to-all-start.2 = ((f32[16,32,128]{2,1,0:T(8,128)}), f32[16,32,128]{2,1,0:T(8,128)S(1)}, u32[]{:S(2)}, u32[]{:S(2)}) async-start(f32[16,32,128]{2,1,0:T(8,128)} %broadcast_in_dim.12), calls=%async_computation.2 | async-start | bytes 524288 | tf_op jit(solution)/shard_map/all_to_all | solution.py:165
  58.7 11.9 %all-to-all-done.2 = f32[16,32,128]{2,1,0:T(8,128)S(1)} async-done(((f32[16,32,128]{2,1,0:T(8,128)}), f32[16,32,128]{2,1,0:T(8,128)S(1)}, u32[]{:S(2)}, u32[]{:S(2)}) %all-to-all-start.2) | async-done | bytes 262176 | tf_op jit(solution)/shard_map/all_to_all | solution.py:165
  71.6 3.4 %copy-done = bf16[32,8,128,128]{3,2,1,0:T(8,128)(2,1)S(1)} copy-done((bf16[32,8,128,128]{3,2,1,0:T(8,128)(2,1)S(1)}, bf16[32,8,128,128]{3,2,1,0:T(8,128)(2,1)}, u32[]{:S(2)}) %copy-start) | copy-done | bytes 8388632
  75.0 3.8 %shard_map.47 = (bf16[32,32,128]{2,1,0:T(8,128)(2,1)S(1)}, f32[32,128]{1,0:T(8,128)S(1)}, f32[32,128]{1,0:T(8,128)S(1)}, f32[32,128]{1,0:T(8,128)S(1)}) custom-call(s32[256]{0:T(256)S(1)} %reshape.66.place_ref, s32[32]{0:T(128)S(1)} %slice_reduce_fusion.1.count_ref, s32[256]{0:T(256)S(1)} %reshape.67.table_ref, bf16[128,32,128]{2,1,0:T(8,128)(2,1)S(1)} %shard_map.46.refs_0_, ...), custom_call_target="tpu_custom_call" | custom-call | flops 268435456 | bytes 8388608 | tf_op jit(solution)/shard_map/pallas_call | solution.py:141
  81.5 2.1 %collective-permute-start.7 = (bf16[32,32,128]{2,1,0:T(8,128)(2,1)S(1)}, bf16[32,32,128]{2,1,0:T(8,128)(2,1)S(1)}, u32[]{:S(2)}, u32[]{:S(2)}) collective-permute-start(bf16[32,32,128]{2,1,0:T(8,128)(2,1)S(1)} %get-tuple-element.19.refs_0_), channel_id=1, source_target_pairs={{8,0},{3,1},{10,2},{5,3},{12,4},{7,5},{14,6},{1,7},{16,8},{11,9},{... | collective-permute-start | bytes 786440 | tf_op jit(solution)/shard_map/ppermute | solution.py:31
  85.3 3.1 %collective-permute-done.8.refs_2_ = bf16[32,32,128]{2,1,0:T(8,128)(2,1)S(1)} collective-permute-done((bf16[32,32,128]{2,1,0:T(8,128)(2,1)S(1)}, bf16[32,32,128]{2,1,0:T(8,128)(2,1)S(1)}, u32[]{:S(2)}, u32[]{:S(2)}) %collective-permute-start.8) | collective-permute-done | bytes 262176 | tf_op jit(solution)/shard_map/ppermute | solution.py:31
  88.3 2.3 %collective-permute-done.7.refs_1_ = bf16[32,32,128]{2,1,0:T(8,128)(2,1)S(1)} collective-permute-done((bf16[32,32,128]{2,1,0:T(8,128)(2,1)S(1)}, bf16[32,32,128]{2,1,0:T(8,128)(2,1)S(1)}, u32[]{:S(2)}, u32[]{:S(2)}) %collective-permute-start.7) | collective-permute-done | bytes 262176 | tf_op jit(solution)/shard_map/ppermute | solution.py:31
  94.4 3.0 %collective-permute-start.21 = (bf16[128,16,128]{2,1,0:T(8,128)(2,1)S(1)}, bf16[128,16,128]{2,1,0:T(8,128)(2,1)S(1)}, u32[]{:S(2)}, u32[]{:S(2)}) collective-permute-start(bf16[128,16,128]{2,1,0:T(8,128)(2,1)S(1)} %get-tuple-element.24.refs_0_), channel_id=1, source_target_pairs={{2,0},{9,1},{4,2},{11,3},{6,4},{13,5},{0,6},{15,7},{10,8},{17,9},{... | collective-permute-start | bytes 1572872 | tf_op jit(solution)/shard_map/ppermute | solution.py:31
  97.3 3.9 %collective-permute-done.12.refs_4_ = bf16[128,16,128]{2,1,0:T(8,128)(2,1)S(1)} collective-permute-done((bf16[128,16,128]{2,1,0:T(8,128)(2,1)S(1)}, bf16[128,16,128]{2,1,0:T(8,128)(2,1)S(1)}, u32[]{:S(2)}, u32[]{:S(2)}) %collective-permute-start.12) | collective-permute-done | bytes 524320 | tf_op jit(solution)/shard_map/ppermute | solution.py:31
  101.6 3.0 %collective-permute-start.11 = (bf16[64,16,128]{2,1,0:T(8,128)(2,1)S(1)}, bf16[64,16,128]{2,1,0:T(8,128)(2,1)S(1)}, u32[]{:S(2)}, u32[]{:S(2)}) collective-permute-start(bf16[64,16,128]{2,1,0:T(8,128)(2,1)S(1)} %slice.82), channel_id=1, source_target_pairs={{2,0},{9,1},{4,2},{11,3},{6,4},{13,5},{0,6},{15,7},{10,8},{17,9},{... | collective-permute-start | bytes 786440 | tf_op jit(solution)/shard_map/ppermute | solution.py:31
  104.7 2.2 %collective-permute-done.23.refs_4_ = bf16[128,16,128]{2,1,0:T(8,128)(2,1)S(1)} collective-permute-done((bf16[128,16,128]{2,1,0:T(8,128)(2,1)S(1)}, bf16[128,16,128]{2,1,0:T(8,128)(2,1)S(1)}, u32[]{:S(2)}, u32[]{:S(2)}) %collective-permute-start.23) | collective-permute-done | bytes 524320 | tf_op jit(solution)/shard_map/ppermute | solution.py:31
  107.2 3.0 %collective-permute-start.22 = (bf16[64,16,128]{2,1,0:T(8,128)(2,1)S(1)}, bf16[64,16,128]{2,1,0:T(8,128)(2,1)S(1)}, u32[]{:S(2)}, u32[]{:S(2)}) collective-permute-start(bf16[64,16,128]{2,1,0:T(8,128)(2,1)S(1)} %slice.86), channel_id=1, source_target_pairs={{2,0},{9,1},{4,2},{11,3},{6,4},{13,5},{0,6},{15,7},{10,8},{17,9},{... | collective-permute-start | bytes 786440 | tf_op jit(solution)/shard_map/ppermute | solution.py:31
  110.3 2.2 %shard_map.49 = (bf16[32,16,128]{2,1,0:T(8,128)(2,1)S(1)}, f32[16,128]{1,0:T(8,128)S(1)}) custom-call(s32[256]{0:T(256)S(1)} %reshape.66.place_ref, s32[32]{0:T(128)S(1)} %slice_reduce_fusion.1.count_ref, s32[256]{0:T(256)S(1)} %reshape.67.table_ref, bf16[128,16,128]{2,1,0:T(8,128)(2,1)S(1)} %get-tuple-element.20.refs_0_, ...), custom_call_target="tpu_custom_call" | custom-call | flops 134217728 | bytes 8388608 | tf_op jit(solution)/shard_map/pallas_call | solution.py:141
  116.7 2.2 %shard_map.52 = (bf16[32,16,128]{2,1,0:T(8,128)(2,1)S(1)}, f32[16,128]{1,0:T(8,128)S(1)}) custom-call(s32[256]{0:T(256)S(1)} %reshape.66.place_ref, s32[32]{0:T(128)S(1)} %slice_reduce_fusion.1.count_ref, s32[256]{0:T(256)S(1)} %reshape.67.table_ref, bf16[128,16,128]{2,1,0:T(8,128)(2,1)S(1)} %get-tuple-element.24.refs_0_, ...), custom_call_target="tpu_custom_call" | custom-call | flops 134217728 | bytes 8388608 | tf_op jit(solution)/shard_map/pallas_call | solution.py:141
  119.1 3.5 %collective-permute-start.26 = (bf16[32,16,128]{2,1,0:T(8,128)(2,1)S(1)}, bf16[32,16,128]{2,1,0:T(8,128)(2,1)S(1)}, u32[]{:S(2)}, u32[]{:S(2)}) collective-permute-start(bf16[32,16,128]{2,1,0:T(8,128)(2,1)S(1)} %get-tuple-element.25.refs_0_), channel_id=1, source_target_pairs={{16,0},{5,1},{18,2},{7,3},{20,4},{1,5},{22,6},{3,7},{24,8},{13,9},... | collective-permute-start | bytes 393224 | tf_op jit(solution)/shard_map/ppermute | solution.py:31
  123.8 2.1 %collective-permute-start.17 = (bf16[128,16,128]{2,1,0:T(8,128)(2,1)S(1)}, bf16[128,16,128]{2,1,0:T(8,128)(2,1)S(1)}, u32[]{:S(2)}, u32[]{:S(2)}) collective-permute-start(bf16[128,16,128]{2,1,0:T(8,128)(2,1)S(1)} %shard_map.50.refs_0_), channel_id=1, source_target_pairs={{2,0},{9,1},{4,2},{11,3},{6,4},{13,5},{0,6},{15,7},{10,8},{17,9},{... | collective-permute-start | bytes 1572872 | tf_op jit(solution)/shard_map/ppermute | solution.py:31
  126.9 2.5 %collective-permute-done.25.refs_1_ = bf16[32,16,128]{2,1,0:T(8,128)(2,1)S(1)} collective-permute-done((bf16[32,16,128]{2,1,0:T(8,128)(2,1)S(1)}, bf16[32,16,128]{2,1,0:T(8,128)(2,1)S(1)}, u32[]{:S(2)}, u32[]{:S(2)}) %collective-permute-start.25) | collective-permute-done | bytes 131104 | tf_op jit(solution)/shard_map/ppermute | solution.py:31
  130.6 2.3 %collective-permute-start.28 = (bf16[128,16,128]{2,1,0:T(8,128)(2,1)S(1)}, bf16[128,16,128]{2,1,0:T(8,128)(2,1)S(1)}, u32[]{:S(2)}, u32[]{:S(2)}) collective-permute-start(bf16[128,16,128]{2,1,0:T(8,128)(2,1)S(1)} %shard_map.53.refs_0_), channel_id=1, source_target_pairs={{2,0},{9,1},{4,2},{11,3},{6,4},{13,5},{0,6},{15,7},{10,8},{17,9},{... | collective-permute-start | bytes 1572872 | tf_op jit(solution)/shard_map/ppermute | solution.py:31
  133.5 3.3 %collective-permute-start.18 = (bf16[64,16,128]{2,1,0:T(8,128)(2,1)S(1)}, bf16[64,16,128]{2,1,0:T(8,128)(2,1)S(1)}, u32[]{:S(2)}, u32[]{:S(2)}) collective-permute-start(bf16[64,16,128]{2,1,0:T(8,128)(2,1)S(1)} %slice.84), channel_id=1, source_target_pairs={{2,0},{9,1},{4,2},{11,3},{6,4},{13,5},{0,6},{15,7},{10,8},{17,9},{... | collective-permute-start | bytes 786440 | tf_op jit(solution)/shard_map/ppermute | solution.py:31
  136.8 3.2 %collective-permute-done.30.refs_4_ = bf16[128,16,128]{2,1,0:T(8,128)(2,1)S(1)} collective-permute-done((bf16[128,16,128]{2,1,0:T(8,128)(2,1)S(1)}, bf16[128,16,128]{2,1,0:T(8,128)(2,1)S(1)}, u32[]{:S(2)}, u32[]{:S(2)}) %collective-permute-start.30) | collective-permute-done | bytes 524320 | tf_op jit(solution)/shard_map/ppermute | solution.py:31
  140.1 3.3 %collective-permute-start.29 = (bf16[64,16,128]{2,1,0:T(8,128)(2,1)S(1)}, bf16[64,16,128]{2,1,0:T(8,128)(2,1)S(1)}, u32[]{:S(2)}, u32[]{:S(2)}) collective-permute-start(bf16[64,16,128]{2,1,0:T(8,128)(2,1)S(1)} %slice.88), channel_id=1, source_target_pairs={{2,0},{9,1},{4,2},{11,3},{6,4},{13,5},{0,6},{15,7},{10,8},{17,9},{... | collective-permute-start | bytes 786440 | tf_op jit(solution)/shard_map/ppermute | solution.py:31
  143.4 2.2 %shard_map.51 = (bf16[32,16,128]{2,1,0:T(8,128)(2,1)S(1)}, f32[16,128]{1,0:T(8,128)S(1)}) custom-call(s32[256]{0:T(256)S(1)} %reshape.66.place_ref, s32[32]{0:T(128)S(1)} %slice_reduce_fusion.1.count_ref, s32[256]{0:T(256)S(1)} %reshape.67.table_ref, bf16[128,16,128]{2,1,0:T(8,128)(2,1)S(1)} %shard_map.50.refs_0_, ...), custom_call_target="tpu_custom_call" | custom-call | flops 134217728 | bytes 8388608 | tf_op jit(solution)/shard_map/pallas_call | solution.py:141
  145.6 2.0 %collective-permute-done.31.refs_3_ = bf16[64,16,128]{2,1,0:T(8,128)(2,1)S(1)} collective-permute-done((bf16[64,16,128]{2,1,0:T(8,128)(2,1)S(1)}, bf16[64,16,128]{2,1,0:T(8,128)(2,1)S(1)}, u32[]{:S(2)}, u32[]{:S(2)}) %collective-permute-start.31) | collective-permute-done | bytes 262176 | tf_op jit(solution)/shard_map/ppermute | solution.py:31
  147.6 2.2 %shard_map.54 = (bf16[32,16,128]{2,1,0:T(8,128)(2,1)S(1)}, f32[16,128]{1,0:T(8,128)S(1)}) custom-call(s32[256]{0:T(256)S(1)} %reshape.66.place_ref, s32[32]{0:T(128)S(1)} %slice_reduce_fusion.1.count_ref, s32[256]{0:T(256)S(1)} %reshape.67.table_ref, bf16[128,16,128]{2,1,0:T(8,128)(2,1)S(1)} %shard_map.53.refs_0_, ...), custom_call_target="tpu_custom_call" | custom-call | flops 134217728 | bytes 8388608 | tf_op jit(solution)/shard_map/pallas_call | solution.py:141
  150.0 13.7 %all_to_all.36 = f32[16,1,128]{2,1,0:T(1,128)S(1)} all-to-all(f32[16,1,128]{2,1,0:T(1,128)S(1)} %broadcast_in_dim.27), channel_id=1, replica_groups=mesh['z'=8,'x'=4,'y'=4,'c'=2] {'x','y'}, dimensions={0} | all-to-all | bytes 16384 | tf_op jit(solution)/shard_map/all_to_all | solution.py:165
  164.0 17.2 %all_to_all.37 = bf16[32,32,128]{2,1,0:T(8,128)(2,1)S(1)} all-to-all(bf16[32,32,128]{2,1,0:T(8,128)(2,1)S(1)} %multiply_convert_fusion), channel_id=1, replica_groups=mesh['z'=8,'x'=4,'y'=4,'c'=2] {'z'}, dimensions={0} | all-to-all | bytes 524288 | tf_op jit(solution)/shard_map/all_to_all | solution.py:224
  (97 shorter events, 31.6 us)
Async XLA Ops:
  6.5 65.1 %all-gather.2.cloned.1.call-start = ((), (), s32[]{:S(2)}) async-start(), calls=%async_computation.5 | async-start | bytes 8912896 | tf_op jit(solution)/shard_map/all_gather | solution.py:175
  10.5 14.3 %all-to-all-start = ((bf16[2,8,16,512]{3,1,0,2:T(8,128)(2,1)}), bf16[2,8,16,512]{3,1,0,2:T(8,128)(2,1)S(1)}, u32[]{:S(2)}, u32[]{:S(2)}) async-start(bf16[2,8,16,512]{3,1,0,2:T(8,128)(2,1)} %copy.23), calls=%async_computation | async-start | bytes 524288 | tf_op jit(solution)/shard_map/all_to_all | solution.py:181
  26.1 13.6 %collective-permute-start.3 = (bf16[32,32,128]{2,1,0:T(8,128)(2,1)S(1)}, bf16[32,32,128]{2,1,0:T(8,128)(2,1)S(1)}, u32[]{:S(2)}, u32[]{:S(2)}) collective-permute-start(bf16[32,32,128]{2,1,0:T(8,128)(2,1)S(1)} %bitcast.36), channel_id=1, source_target_pairs={{24,0},{7,1},{26,2},{1,3},{28,4},{3,5},{30,6},{5,7},{0,8},{15,9},{... | collective-permute-start | bytes 786440 | tf_op jit(solution)/shard_map/ppermute | solution.py:31
  27.2 12.5 %collective-permute-start.2 = (bf16[32,32,128]{2,1,0:T(8,128)(2,1)S(1)}, bf16[32,32,128]{2,1,0:T(8,128)(2,1)S(1)}, u32[]{:S(2)}, u32[]{:S(2)}) collective-permute-start(bf16[32,32,128]{2,1,0:T(8,128)(2,1)S(1)} %bitcast.37), channel_id=1, source_target_pairs={{16,0},{5,1},{18,2},{7,3},{20,4},{1,5},{22,6},{3,7},{24,8},{13,9},... | collective-permute-start | bytes 786440 | tf_op jit(solution)/shard_map/ppermute | solution.py:31
  30.0 9.6 %collective-permute-start.1 = (bf16[32,32,128]{2,1,0:T(8,128)(2,1)S(1)}, bf16[32,32,128]{2,1,0:T(8,128)(2,1)S(1)}, u32[]{:S(2)}, u32[]{:S(2)}) collective-permute-start(bf16[32,32,128]{2,1,0:T(8,128)(2,1)S(1)} %bitcast.38), channel_id=1, source_target_pairs={{8,0},{3,1},{10,2},{5,3},{12,4},{7,5},{14,6},{1,7},{16,8},{11,9},{... | collective-permute-start | bytes 786440 | tf_op jit(solution)/shard_map/ppermute | solution.py:31
  31.2 20.4 %all-to-all-start.1 = ((f32[8,40,128]{2,1,0:T(8,128)}), f32[8,40,128]{2,1,0:T(8,128)S(1)}, u32[]{:S(2)}, u32[]{:S(2)}) async-start(f32[8,40,128]{2,1,0:T(8,128)} %broadcast_in_dim.11), calls=%async_computation.1 | async-start | bytes 327680 | tf_op jit(solution)/shard_map/all_to_all | solution.py:165
  39.7 30.9 %collective-permute-start.6 = (bf16[128,32,128]{2,1,0:T(8,128)(2,1)S(1)}, bf16[128,32,128]{2,1,0:T(8,128)(2,1)S(1)}, u32[]{:S(2)}, u32[]{:S(2)}) collective-permute-start(bf16[128,32,128]{2,1,0:T(8,128)(2,1)S(1)} %shard_map.46.refs_0_), channel_id=1, source_target_pairs={{6,0},{25,1},{0,2},{27,3},{2,4},{29,5},{4,6},{31,7},{14,8},{1,9},{... | collective-permute-start | bytes 3145736 | tf_op jit(solution)/shard_map/ppermute | solution.py:31
  40.4 30.2 %collective-permute-start.5 = (bf16[128,32,128]{2,1,0:T(8,128)(2,1)S(1)}, bf16[128,32,128]{2,1,0:T(8,128)(2,1)S(1)}, u32[]{:S(2)}, u32[]{:S(2)}) collective-permute-start(bf16[128,32,128]{2,1,0:T(8,128)(2,1)S(1)} %shard_map.46.refs_0_), channel_id=1, source_target_pairs={{4,0},{17,1},{6,2},{19,3},{0,4},{21,5},{2,6},{23,7},{12,8},{25,9},... | collective-permute-start | bytes 3145736 | tf_op jit(solution)/shard_map/ppermute | solution.py:31
  42.2 28.4 %collective-permute-start.4 = (bf16[128,32,128]{2,1,0:T(8,128)(2,1)S(1)}, bf16[128,32,128]{2,1,0:T(8,128)(2,1)}, u32[]{:S(2)}, u32[]{:S(2)}) collective-permute-start(bf16[128,32,128]{2,1,0:T(8,128)(2,1)S(1)} %shard_map.46.refs_0_), channel_id=1, source_target_pairs={{2,0},{9,1},{4,2},{11,3},{6,4},{13,5},{0,6},{15,7},{10,8},{17,9},{... | collective-permute-start | bytes 3145736 | tf_op jit(solution)/shard_map/ppermute | solution.py:31
  52.5 18.1 %all-to-all-start.2 = ((f32[16,32,128]{2,1,0:T(8,128)}), f32[16,32,128]{2,1,0:T(8,128)S(1)}, u32[]{:S(2)}, u32[]{:S(2)}) async-start(f32[16,32,128]{2,1,0:T(8,128)} %broadcast_in_dim.12), calls=%async_computation.2 | async-start | bytes 524288 | tf_op jit(solution)/shard_map/all_to_all | solution.py:165
  80.4 8.0 %collective-permute-start.8 = (bf16[32,32,128]{2,1,0:T(8,128)(2,1)S(1)}, bf16[32,32,128]{2,1,0:T(8,128)(2,1)S(1)}, u32[]{:S(2)}, u32[]{:S(2)}) collective-permute-start(bf16[32,32,128]{2,1,0:T(8,128)(2,1)S(1)} %get-tuple-element.19.refs_0_), channel_id=1, source_target_pairs={{16,0},{5,1},{18,2},{7,3},{20,4},{1,5},{22,6},{3,7},{24,8},{13,9},... | collective-permute-start | bytes 786440 | tf_op jit(solution)/shard_map/ppermute | solution.py:31
  81.5 9.2 %collective-permute-start.7 = (bf16[32,32,128]{2,1,0:T(8,128)(2,1)S(1)}, bf16[32,32,128]{2,1,0:T(8,128)(2,1)S(1)}, u32[]{:S(2)}, u32[]{:S(2)}) collective-permute-start(bf16[32,32,128]{2,1,0:T(8,128)(2,1)S(1)} %get-tuple-element.19.refs_0_), channel_id=1, source_target_pairs={{8,0},{3,1},{10,2},{5,3},{12,4},{7,5},{14,6},{1,7},{16,8},{11,9},{... | collective-permute-start | bytes 786440 | tf_op jit(solution)/shard_map/ppermute | solution.py:31
  90.8 10.5 %collective-permute-start.12 = (bf16[128,16,128]{2,1,0:T(8,128)(2,1)S(1)}, bf16[128,16,128]{2,1,0:T(8,128)(2,1)S(1)}, u32[]{:S(2)}, u32[]{:S(2)}) collective-permute-start(bf16[128,16,128]{2,1,0:T(8,128)(2,1)S(1)} %get-tuple-element.20.refs_0_), channel_id=1, source_target_pairs={{6,0},{25,1},{0,2},{27,3},{2,4},{29,5},{4,6},{31,7},{14,8},{1,9},{... | collective-permute-start | bytes 1572872 | tf_op jit(solution)/shard_map/ppermute | solution.py:31
  92.3 9.3 %collective-permute-start.10 = (bf16[128,16,128]{2,1,0:T(8,128)(2,1)S(1)}, bf16[128,16,128]{2,1,0:T(8,128)(2,1)S(1)}, u32[]{:S(2)}, u32[]{:S(2)}) collective-permute-start(bf16[128,16,128]{2,1,0:T(8,128)(2,1)S(1)} %get-tuple-element.20.refs_0_), channel_id=1, source_target_pairs={{2,0},{9,1},{4,2},{11,3},{6,4},{13,5},{0,6},{15,7},{10,8},{17,9},{... | collective-permute-start | bytes 1572872 | tf_op jit(solution)/shard_map/ppermute | solution.py:31
  94.1 12.8 %collective-permute-start.23 = (bf16[128,16,128]{2,1,0:T(8,128)(2,1)S(1)}, bf16[128,16,128]{2,1,0:T(8,128)(2,1)S(1)}, u32[]{:S(2)}, u32[]{:S(2)}) collective-permute-start(bf16[128,16,128]{2,1,0:T(8,128)(2,1)S(1)} %get-tuple-element.24.refs_0_), channel_id=1, source_target_pairs={{6,0},{25,1},{0,2},{27,3},{2,4},{29,5},{4,6},{31,7},{14,8},{1,9},{... | collective-permute-start | bytes 1572872 | tf_op jit(solution)/shard_map/ppermute | solution.py:31
  94.4 12.9 %collective-permute-start.21 = (bf16[128,16,128]{2,1,0:T(8,128)(2,1)S(1)}, bf16[128,16,128]{2,1,0:T(8,128)(2,1)S(1)}, u32[]{:S(2)}, u32[]{:S(2)}) collective-permute-start(bf16[128,16,128]{2,1,0:T(8,128)(2,1)S(1)} %get-tuple-element.24.refs_0_), channel_id=1, source_target_pairs={{2,0},{9,1},{4,2},{11,3},{6,4},{13,5},{0,6},{15,7},{10,8},{17,9},{... | collective-permute-start | bytes 1572872 | tf_op jit(solution)/shard_map/ppermute | solution.py:31
  101.3 9.0 %collective-permute-start.13 = (bf16[64,16,128]{2,1,0:T(8,128)(2,1)S(1)}, bf16[64,16,128]{2,1,0:T(8,128)(2,1)S(1)}, u32[]{:S(2)}, u32[]{:S(2)}) collective-permute-start(bf16[64,16,128]{2,1,0:T(8,128)(2,1)S(1)} %slice.83), channel_id=1, source_target_pairs={{6,0},{25,1},{0,2},{27,3},{2,4},{29,5},{4,6},{31,7},{14,8},{1,9},{... | collective-permute-start | bytes 786440 | tf_op jit(solution)/shard_map/ppermute | solution.py:31
  101.6 8.7 %collective-permute-start.11 = (bf16[64,16,128]{2,1,0:T(8,128)(2,1)S(1)}, bf16[64,16,128]{2,1,0:T(8,128)(2,1)S(1)}, u32[]{:S(2)}, u32[]{:S(2)}) collective-permute-start(bf16[64,16,128]{2,1,0:T(8,128)(2,1)S(1)} %slice.82), channel_id=1, source_target_pairs={{2,0},{9,1},{4,2},{11,3},{6,4},{13,5},{0,6},{15,7},{10,8},{17,9},{... | collective-permute-start | bytes 786440 | tf_op jit(solution)/shard_map/ppermute | solution.py:31
  106.9 9.8 %collective-permute-start.24 = (bf16[64,16,128]{2,1,0:T(8,128)(2,1)S(1)}, bf16[64,16,128]{2,1,0:T(8,128)(2,1)S(1)}, u32[]{:S(2)}, u32[]{:S(2)}) collective-permute-start(bf16[64,16,128]{2,1,0:T(8,128)(2,1)S(1)} %slice.87), channel_id=1, source_target_pairs={{6,0},{25,1},{0,2},{27,3},{2,4},{29,5},{4,6},{31,7},{14,8},{1,9},{... | collective-permute-start | bytes 786440 | tf_op jit(solution)/shard_map/ppermute | solution.py:31
  107.2 9.5 %collective-permute-start.22 = (bf16[64,16,128]{2,1,0:T(8,128)(2,1)S(1)}, bf16[64,16,128]{2,1,0:T(8,128)(2,1)S(1)}, u32[]{:S(2)}, u32[]{:S(2)}) collective-permute-start(bf16[64,16,128]{2,1,0:T(8,128)(2,1)S(1)} %slice.86), channel_id=1, source_target_pairs={{2,0},{9,1},{4,2},{11,3},{6,4},{13,5},{0,6},{15,7},{10,8},{17,9},{... | collective-permute-start | bytes 786440 | tf_op jit(solution)/shard_map/ppermute | solution.py:31
  112.5 10.1 %collective-permute-start.16 = (bf16[32,16,128]{2,1,0:T(8,128)(2,1)S(1)}, bf16[32,16,128]{2,1,0:T(8,128)(2,1)S(1)}, u32[]{:S(2)}, u32[]{:S(2)}) collective-permute-start(bf16[32,16,128]{2,1,0:T(8,128)(2,1)S(1)} %get-tuple-element.22.refs_0_), channel_id=1, source_target_pairs={{24,0},{7,1},{26,2},{1,3},{28,4},{3,5},{30,6},{5,7},{0,8},{15,9},{... | collective-permute-start | bytes 393224 | tf_op jit(solution)/shard_map/ppermute | solution.py:31
  113.5 9.1 %collective-permute-start.15 = (bf16[32,16,128]{2,1,0:T(8,128)(2,1)S(1)}, bf16[32,16,128]{2,1,0:T(8,128)(2,1)S(1)}, u32[]{:S(2)}, u32[]{:S(2)}) collective-permute-start(bf16[32,16,128]{2,1,0:T(8,128)(2,1)S(1)} %get-tuple-element.22.refs_0_), channel_id=1, source_target_pairs={{16,0},{5,1},{18,2},{7,3},{20,4},{1,5},{22,6},{3,7},{24,8},{13,9},... | collective-permute-start | bytes 393224 | tf_op jit(solution)/shard_map/ppermute | solution.py:31
  114.7 7.9 %collective-permute-start.14 = (bf16[32,16,128]{2,1,0:T(8,128)(2,1)S(1)}, bf16[32,16,128]{2,1,0:T(8,128)(2,1)S(1)}, u32[]{:S(2)}, u32[]{:S(2)}) collective-permute-start(bf16[32,16,128]{2,1,0:T(8,128)(2,1)S(1)} %get-tuple-element.22.refs_0_), channel_id=1, source_target_pairs={{8,0},{3,1},{10,2},{5,3},{12,4},{7,5},{14,6},{1,7},{16,8},{11,9},{... | collective-permute-start | bytes 393224 | tf_op jit(solution)/shard_map/ppermute | solution.py:31
  119.1 7.8 %collective-permute-start.26 = (bf16[32,16,128]{2,1,0:T(8,128)(2,1)S(1)}, bf16[32,16,128]{2,1,0:T(8,128)(2,1)S(1)}, u32[]{:S(2)}, u32[]{:S(2)}) collective-permute-start(bf16[32,16,128]{2,1,0:T(8,128)(2,1)S(1)} %get-tuple-element.25.refs_0_), channel_id=1, source_target_pairs={{16,0},{5,1},{18,2},{7,3},{20,4},{1,5},{22,6},{3,7},{24,8},{13,9},... | collective-permute-start | bytes 393224 | tf_op jit(solution)/shard_map/ppermute | solution.py:31
  122.6 10.5 %collective-permute-start.19 = (bf16[128,16,128]{2,1,0:T(8,128)(2,1)S(1)}, bf16[128,16,128]{2,1,0:T(8,128)(2,1)S(1)}, u32[]{:S(2)}, u32[]{:S(2)}) collective-permute-start(bf16[128,16,128]{2,1,0:T(8,128)(2,1)S(1)} %shard_map.50.refs_0_), channel_id=1, source_target_pairs={{6,0},{25,1},{0,2},{27,3},{2,4},{29,5},{4,6},{31,7},{14,8},{1,9},{... | collective-permute-start | bytes 1572872 | tf_op jit(solution)/shard_map/ppermute | solution.py:31
  123.8 9.6 %collective-permute-start.17 = (bf16[128,16,128]{2,1,0:T(8,128)(2,1)S(1)}, bf16[128,16,128]{2,1,0:T(8,128)(2,1)S(1)}, u32[]{:S(2)}, u32[]{:S(2)}) collective-permute-start(bf16[128,16,128]{2,1,0:T(8,128)(2,1)S(1)} %shard_map.50.refs_0_), channel_id=1, source_target_pairs={{2,0},{9,1},{4,2},{11,3},{6,4},{13,5},{0,6},{15,7},{10,8},{17,9},{... | collective-permute-start | bytes 1572872 | tf_op jit(solution)/shard_map/ppermute | solution.py:31
  129.5 10.5 %collective-permute-start.30 = (bf16[128,16,128]{2,1,0:T(8,128)(2,1)S(1)}, bf16[128,16,128]{2,1,0:T(8,128)(2,1)S(1)}, u32[]{:S(2)}, u32[]{:S(2)}) collective-permute-start(bf16[128,16,128]{2,1,0:T(8,128)(2,1)S(1)} %shard_map.53.refs_0_), channel_id=1, source_target_pairs={{6,0},{25,1},{0,2},{27,3},{2,4},{29,5},{4,6},{31,7},{14,8},{1,9},{... | collective-permute-start | bytes 1572872 | tf_op jit(solution)/shard_map/ppermute | solution.py:31
  130.6 9.5 %collective-permute-start.28 = (bf16[128,16,128]{2,1,0:T(8,128)(2,1)S(1)}, bf16[128,16,128]{2,1,0:T(8,128)(2,1)S(1)}, u32[]{:S(2)}, u32[]{:S(2)}) collective-permute-start(bf16[128,16,128]{2,1,0:T(8,128)(2,1)S(1)} %shard_map.53.refs_0_), channel_id=1, source_target_pairs={{2,0},{9,1},{4,2},{11,3},{6,4},{13,5},{0,6},{15,7},{10,8},{17,9},{... | collective-permute-start | bytes 1572872 | tf_op jit(solution)/shard_map/ppermute | solution.py:31
  133.1 10.3 %collective-permute-start.20 = (bf16[64,16,128]{2,1,0:T(8,128)(2,1)S(1)}, bf16[64,16,128]{2,1,0:T(8,128)(2,1)S(1)}, u32[]{:S(2)}, u32[]{:S(2)}) collective-permute-start(bf16[64,16,128]{2,1,0:T(8,128)(2,1)S(1)} %slice.85), channel_id=1, source_target_pairs={{6,0},{25,1},{0,2},{27,3},{2,4},{29,5},{4,6},{31,7},{14,8},{1,9},{... | collective-permute-start | bytes 786440 | tf_op jit(solution)/shard_map/ppermute | solution.py:31
  133.5 9.9 %collective-permute-start.18 = (bf16[64,16,128]{2,1,0:T(8,128)(2,1)S(1)}, bf16[64,16,128]{2,1,0:T(8,128)(2,1)S(1)}, u32[]{:S(2)}, u32[]{:S(2)}) collective-permute-start(bf16[64,16,128]{2,1,0:T(8,128)(2,1)S(1)} %slice.84), channel_id=1, source_target_pairs={{2,0},{9,1},{4,2},{11,3},{6,4},{13,5},{0,6},{15,7},{10,8},{17,9},{... | collective-permute-start | bytes 786440 | tf_op jit(solution)/shard_map/ppermute | solution.py:31
  140.0 7.7 %collective-permute-start.31 = (bf16[64,16,128]{2,1,0:T(8,128)(2,1)S(1)}, bf16[64,16,128]{2,1,0:T(8,128)(2,1)S(1)}, u32[]{:S(2)}, u32[]{:S(2)}) collective-permute-start(bf16[64,16,128]{2,1,0:T(8,128)(2,1)S(1)} %slice.89), channel_id=1, source_target_pairs={{6,0},{25,1},{0,2},{27,3},{2,4},{29,5},{4,6},{31,7},{14,8},{1,9},{... | collective-permute-start | bytes 786440 | tf_op jit(solution)/shard_map/ppermute | solution.py:31
  140.1 7.5 %collective-permute-start.29 = (bf16[64,16,128]{2,1,0:T(8,128)(2,1)S(1)}, bf16[64,16,128]{2,1,0:T(8,128)(2,1)S(1)}, u32[]{:S(2)}, u32[]{:S(2)}) collective-permute-start(bf16[64,16,128]{2,1,0:T(8,128)(2,1)S(1)} %slice.88), channel_id=1, source_target_pairs={{2,0},{9,1},{4,2},{11,3},{6,4},{13,5},{0,6},{15,7},{10,8},{17,9},{... | collective-permute-start | bytes 786440 | tf_op jit(solution)/shard_map/ppermute | solution.py:31
  (6 other events, 64.5 us)
Sparse Core Ops, SparseCore 0:
  9.2 62.3 all-gather.1
